TPU v7x, 32 devices: a whole 2x2x4 slice. The times are simulated.
32 devices in a mesh: dp: 8 (over z, y), lon: 4 (over x, core).
Axes of the slice: x: 2, y: 2, z: 4, core: 2. Of those that a mesh axis runs over, the one named last changes fastest.
Arguments:
- fields: bfloat16 [8, 16, 512, 192], P('dp', None, 'lon'), may hold values from -6 to 6
- cotangent: bfloat16 [8, 16, 512, 192], P('dp', None, 'lon'), may hold values from -6 to 6
- land_sea: int32 [16, 512], P(None, 'lon'), may hold values 0 or 1
- kernel: float32 [7, 7, 192], replicated, may hold values from -0.875 to 0.875
- ln_gain: float32 [192], replicated, may hold values from 0.5 to 1.5
- weight_in: bfloat16 [192, 768], replicated, may hold values from -0.4375 to 0.4375
- bias_in: float32 [768], replicated, may hold values from -3 to 3
- weight_out: bfloat16 [768, 192], replicated, may hold values from -0.21875 to 0.21875
Outputs:
- output: bfloat16 [8, 16, 512, 192], P('dp', None, 'lon')
- grad_fields: bfloat16 [8, 16, 512, 192], P('dp', None, 'lon')
- grad_in: float32 [192, 768], P('dp')
- grad_out: float32 [768, 192], P('dp')
- grad_kernel: float32 [7, 7, 192], replicated
- grad_gain: float32 [192], replicated
- grad_bias: float32 [768], replicated
All inputs are finite; a program needn't handle non-finite values. No bound on the sum of `land_sea` on one device may be relied on, other than what follows from the above.
Results may differ from a plain program's by a relative error of at most 0.025.
Values may be sent and summed in bfloat16 or wider, within the bound.
No kernel may reach another device: no remote copies, remote signals or barrier semaphores. Data moves between devices by JAX's collectives and lax.ppermute only.
A program may use at most 64 MiB of HBM per device.

v0:
```python
import math

import jax
import jax.numpy as jnp
from jax import lax
from jax.sharding import PartitionSpec as P


def extended(x, sides, width):
    for axis, dim in sides:
        peers, length = (lax.axis_size(axis), x.shape[dim])
        up = [(i, (i + 1) % peers) for i in range(peers)]
        down = [(j, i) for i, j in up]
        last = lax.slice_in_dim(x, length - width, length, axis=dim)
        first = lax.slice_in_dim(x, 0, width, axis=dim)
        before = lax.ppermute(last, axis, up)
        after = lax.ppermute(first, axis, down)
        x = jnp.concatenate([before, x, after], axis=dim)
    return x


def gelu_exact(value):
    return value * (1.0 + lax.erf(value / math.sqrt(2.0))) / 2.0


def gelu_slope(value):
    return (1.0 + lax.erf(value / math.sqrt(2.0))) / 2.0 + value * jnp.exp(
        -value * value / 2.0
    ) / math.sqrt(2.0 * math.pi)


def pad_rows(block):
    return jnp.pad(block, ((0, 0), (3, 3), (0, 0), (0, 0)))


def depthwise(padded, kernel, lat_rows, lon_cols):
    total = jnp.zeros((padded.shape[0], lat_rows, lon_cols, padded.shape[3]), jnp.float32)
    for row_off in range(7):
        for col_off in range(7):
            total = (
                total
                + padded[:, row_off : row_off + lat_rows, col_off : col_off + lon_cols].astype(
                    jnp.float32
                )
                * kernel[row_off, col_off]
            )
    return total


def transposed(padded, kernel, lat_rows, lon_cols):
    total = jnp.zeros((padded.shape[0], lat_rows, lon_cols, padded.shape[3]), jnp.float32)
    for row_off in range(7):
        for col_off in range(7):
            total = (
                total
                + padded[
                    :, 6 - row_off : 6 - row_off + lat_rows, 6 - col_off : 6 - col_off + lon_cols
                ].astype(jnp.float32)
                * kernel[row_off, col_off]
            )
    return total


def kernel_terms(padded, d_conv, lat_rows, lon_cols):
    d_float = d_conv.astype(jnp.float32)
    rows_out = []
    for row_off in range(7):
        cols_out = []
        for col_off in range(7):
            window = padded[:, row_off : row_off + lat_rows, col_off : col_off + lon_cols].astype(
                jnp.float32
            )
            cols_out.append(jnp.sum(window * d_float, axis=(0, 1, 2)))
        rows_out.append(jnp.stack(cols_out, axis=0))
    return jnp.stack(rows_out, axis=0)


def per_device(fields, cotangent, land_sea, kernel, ln_gain, weight_in, bias_in, weight_out):
    samples_here, lat_rows, lon_cols, channels = fields.shape
    mask_b = land_sea.astype(jnp.bfloat16)[None, :, :, None]
    mask_f = mask_b.astype(jnp.float32)
    masked = fields * mask_b
    padded = pad_rows(extended(masked, (("lon", 2),), 3))
    conv = depthwise(padded, kernel, lat_rows, lon_cols)
    mean_c = jnp.mean(conv, axis=-1, keepdims=True)
    centered = conv - mean_c
    inv_sigma = lax.rsqrt(jnp.mean(centered * centered, axis=-1, keepdims=True) + 1e-06)
    nhat = centered * inv_sigma
    normed = (nhat * ln_gain).astype(jnp.bfloat16)
    flat = normed.reshape(-1, channels)
    pre = jnp.dot(flat, weight_in, preferred_element_type=jnp.float32) + bias_in
    act = gelu_exact(pre).astype(jnp.bfloat16)
    branch = jnp.dot(act, weight_out, preferred_element_type=jnp.float32).reshape(fields.shape)
    output = (mask_f * (fields.astype(jnp.float32) + branch)).astype(jnp.bfloat16)
    grad_m = cotangent * mask_b
    grad_flat = grad_m.reshape(-1, channels)
    d_act = lax.dot_general(
        grad_flat, weight_out, (((1,), (1,)), ((), ())), preferred_element_type=jnp.float32
    )
    d_pre = (d_act * gelu_slope(pre)).astype(jnp.bfloat16)
    part_out = lax.dot_general(
        act, grad_flat, (((0,), (0,)), ((), ())), preferred_element_type=jnp.float32
    )
    part_in = lax.dot_general(
        flat, d_pre, (((0,), (0,)), ((), ())), preferred_element_type=jnp.float32
    )
    part_bias = jnp.sum(d_pre.astype(jnp.float32), axis=0)
    d_normed = lax.dot_general(
        d_pre, weight_in, (((1,), (1,)), ((), ())), preferred_element_type=jnp.float32
    ).reshape(conv.shape)
    part_gain = jnp.sum(d_normed * nhat, axis=(0, 1, 2))
    d_hat = d_normed * ln_gain
    d_conv = (
        inv_sigma
        * (
            d_hat
            - jnp.mean(d_hat, axis=-1, keepdims=True)
            - nhat * jnp.mean(d_hat * nhat, axis=-1, keepdims=True)
        )
    ).astype(jnp.bfloat16)
    part_kernel = kernel_terms(padded, d_conv, lat_rows, lon_cols)
    grad_pad = pad_rows(extended(d_conv, (("lon", 2),), 3))
    spread = transposed(grad_pad, kernel, lat_rows, lon_cols)
    grad_fields = (grad_m.astype(jnp.float32) + mask_f * spread).astype(jnp.bfloat16)
    summed_in, summed_out = (
        lax.psum(part_in.astype(jnp.bfloat16), "lon").astype(jnp.float32),
        lax.psum(part_out.astype(jnp.bfloat16), "lon").astype(jnp.float32),
    )
    summed_in, summed_out = (
        lax.psum_scatter(
            summed_in.astype(jnp.bfloat16), "dp", scatter_dimension=0, tiled=True
        ).astype(jnp.float32),
        lax.psum_scatter(
            summed_out.astype(jnp.bfloat16), "dp", scatter_dimension=0, tiled=True
        ).astype(jnp.float32),
    )
    sum_kernel, sum_gain, sum_bias = lax.psum((part_kernel, part_gain, part_bias), ("dp", "lon"))
    scale = 1.0 / math.sqrt(
        samples_here * lat_rows * lon_cols * lax.axis_size("dp") * lax.axis_size("lon")
    )
    return (
        output,
        grad_fields,
        summed_in * scale,
        summed_out * scale,
        sum_kernel * scale,
        sum_gain * scale,
        sum_bias * scale,
    )


def solution(mesh):
    placed = (
        P("dp", None, "lon", None),
        P("dp", None, "lon", None),
        P(None, "lon"),
        P(),
        P(),
        P(),
        P(),
        P(),
    )
    return jax.shard_map(
        per_device,
        mesh=mesh,
        in_specs=placed,
        out_specs=(
            P("dp", None, "lon", None),
            P("dp", None, "lon", None),
            P("dp", None),
            P("dp", None),
            P(),
            P(),
            P(),
        ),
        check_vma=False,
    )
```

profile of v0, /device:TPU:0, one launch (start us, length us, event | category | flops | bytes accessed | tf_op | source)
XLA Modules:
  0.0 261.3 jit_solution(18319119081989484325)
XLA Ops:
  7.2 2.7 %copy.41 = bf16[1,16,128,192]{3,1,2,0:T(8,128)(2,1)} copy(bf16[1,16,128,192]{2,3,1,0:T(8,128)(2,1)} %param.9) | data formatting | bytes 1572864 | tf_op args[1]
  12.2 2.0 broadcast_multiply_fusion
  14.2 2.4 collective-permute-start.1
  18.9 1.9 copy.42
  22.0 19.3 %fusion.148 = (f32[16,128]{0,1:T(8,128)S(1)}, f32[1,16,128,192]{3,1,2,0:T(8,128)S(1)}) fusion(f32[192]{0:T(256)} %bitcast.48, bf16[1,22,134,192]{3,1,2,0:T(8,128)(2,1)S(1)} %select_maximum_fusion.2, f32[192]{0:T(256)} %bitcast.47, f32[192]{0:T(256)S(1)} %bitcast.164, f32[192]{0:T(256)S(1)} %bitcast.166, f32[192]{0:T(256)S(1)} %bitcast.168, ...), kind=kLoop, calls=%fused_computation.299 | loop fusion | flops 60160000 | bytes 35472128 | tf_op jit(solution)/shard_map/reduce_sum | solution.py:85
  43.5 1.9 copy.39
  45.4 4.1 %multiply_convert_fusion = (bf16[2048,768]{1,0:T(8,128)(2,1)}, f32[2048,768]{1,0:T(8,128)S(1)}) fusion(f32[768]{0:T(1024)S(1)} %copy-done.122, bf16[192,768]{1,0:T(8,128)(2,1)S(1)} %copy-done, bf16[24,8,16,128]{3,2,1,0:T(8,128)(2,1)} %bitcast.160), kind=kOutput, calls=%fused_computation.59 | convolution fusion | flops 613416960 | bytes 10521600 | tf_op jit(solution)/shard_map/dot_general | solution.py:91
  49.5 4.6 %convert_reduce_fusion = (f32[768]{0:T(1024)}, bf16[2048,768]{1,0:T(8,128)(2,1)S(1)}) fusion(f32[2048,768]{1,0:T(8,128)S(1)} %get-tuple-element.139, f32[768]{0:T(1024)S(1)} %copy-done.122, bf16[768,192]{0,1:T(8,128)(2,1)S(1)} %copy-done.13, bf16[24,8,16,128]{3,2,1,0:T(8,128)(2,1)S(1)} %bitcast.158), kind=kOutput, calls=%fused_computation.58 | convolution fusion | flops 625999104 | bytes 10524672 | tf_op jit(solution)/shard_map/dot_general | solution.py:97
  54.1 2.4 multiply_reduce_fusion.3
  58.0 2.9 %copy.51 = f32[24,8,16,128]{3,2,1,0:T(8,128)} copy(f32[24,8,16,128]{3,1,2,0:T(8,128)} %bitcast.157) | data formatting | bytes 3145728
  60.9 3.1 %copy.43 = f32[1,16,128,192]{3,1,2,0:T(8,128)} copy(f32[1,16,128,192]{2,1,3,0:T(8,128)} %bitcast.155) | data formatting | bytes 3145728 | tf_op jit(solution)/shard_map/reshape | solution.py:110
  64.0 3.3 %multiply_reduce_fusion = (f32[192]{0:T(256)}, f32[16,128]{0,1:T(8,128)S(1)}) fusion(f32[1,16,128,192]{3,1,2,0:T(8,128)} %copy.43, f32[1,16,128,192]{3,1,2,0:T(8,128)} %copy-done.1, f32[16,128]{0,1:T(8,128)S(1)} %add_rsqrt_fusion, f32[16,128]{0,1:T(8,128)S(1)} %broadcast_multiply_fusion.3, f32[192]{0:T(256)S(1)} %copy-done.91), kind=kLoop, calls=%fused_computation.235 | loop fusion | flops 2750272 | bytes 3171840 | tf_op jit(solution)/shard_map/reduce_sum | solution.py:111
  68.7 9.6 %fusion.128 = (f32[192]{0:T(256)}, f32[192]{0:T(256)}, f32[192]{0:T(256)}, f32[192]{0:T(256)}, f32[192]{0:T(256)}, /*index=5*/f32[192]{0:T(256)}, f32[192]{0:T(2...) fusion(bf16[1,22,134,192]{3,1,2,0:T(8,128)(2,1)S(1)} %select_ma, ...), kind=kLoop, calls=%fused_computation.233 | loop fusion | flops 24769152 | bytes 18135296 | tf_op jit(solution)/shard_map/reduce_sum | solution.py:73
  78.9 2.7 %fusion.127 = (f32[192]{0:T(256)}, f32[192]{0:T(256)}, f32[192]{0:T(256)}, f32[192]{0:T(256)}, f32[192]{0:T(256)}, /*index=5*/f32[192]{0:T(256)}) fusion(bf16[1,16,128,192]{3,1,2,0:T(8,128)(2,1)S(1)} %get-tuple-element.80, bf16[1,22,134,192]{3,1,2,0:T(8,128)(2,1)S(1)} %select_maximum_fusion.2), kind=kLoop, calls=%fused_computation.232 | loop fusion | flops 7469952 | bytes 5509632 | tf_op jit(solution)/shard_map/reduce_sum | solution.py:73
  81.6 7.3 %fusion.129 = (f32[192]{0:T(256)}, f32[192]{0:T(256)}, f32[192]{0:T(256)}, f32[192]{0:T(256)}, f32[192]{0:T(256)}, /*index=5*/f32[192]{0:T(256)}, f32[192]{0:T(2...) fusion(bf16[1,16,128,192]{3,1,2,0:T(8,128)(2,1)S(1)} %get-tuple, ...), kind=kLoop, calls=%fused_computation.234 | loop fusion | flops 21623424 | bytes 14956032 | tf_op jit(solution)/shard_map/reduce_sum | solution.py:73
  91.6 3.1 %copy.40 = f32[1,16,128,192]{3,1,2,0:T(8,128)} copy(f32[1,16,128,192]{2,1,3,0:T(8,128)} %bitcast.156) | data formatting | bytes 3145728 | tf_op jit(solution)/shard_map/reshape | solution.py:93
  97.2 3.0 %multiply_convert_fusion.2 = bf16[1,16,128,192]{3,1,2,0:T(8,128)(2,1)} fusion(f32[1,16,128,192]{3,1,2,0:T(8,128)} %copy.40, bf16[1,16,128,192]{3,1,2,0:T(8,128)(2,1)S(1)} %copy-done.6, f32[16,128]{0,1:T(8,128)S(1)} %copy.35), kind=kLoop, calls=%fused_computation.239 | loop fusion | flops 1572864 | bytes 3153920 | tf_op jit(solution)/shard_map/convert_element_type | solution.py:94
  103.2 4.9 %fusion.108 = (f32[192]{0:T(256)S(1)}, f32[192]{0:T(256)S(1)}, f32[192]{0:T(256)S(1)}, f32[192]{0:T(256)S(1)}, f32[192]{0:T(256)S(1)}, /*index=5*/f32[192]{0:T(256)S(1)}, f32[192]{0:T(256)S(1)}) fusion(bf16[1,16,128,192]{3,1,2,0:T(8,128)(2,1)S(1)} %get-tuple-element.80, bf16[1,16,3,192]{3,1,2,0:T(8,128)(2,1)S(1)} %collective-permute-done.1, ...), kind=kLoop, calls=%fused_computation.213 | loop fusion | flops 11008704 | bytes 1615104 | tf_op jit(solution)/shard_map/reduce_sum | solution.py:73
  108.6 40.8 %all-reduce.2 = (f32[7,7,192]{2,1,0:T(8,128)S(1)}, f32[192]{0:T(256)S(1)}, f32[768]{0:T(1024)S(1)}) all-reduce(f32[7,7,192]{2,1,0:T(8,128)S(1)} %constant_dynamic-update-slice_fusion, f32[192]{0:T(256)S(1)} %copy-done.115, f32[768]{0:T(1024)S(1)} %copy-done.114), channel_id=1, replica_groups=mesh['dp'=8,'lon'=4] {'dp','lon'}, use_global_device_ids=true, to_apply=%region_57.58 | all-reduce | flops 10368 | bytes 82944 | tf_op jit(solution)/shard_map/psum | solution.py:137
  150.0 3.8 %convolution_convert_fusion = bf16[768,192]{1,0:T(8,128)(2,1)} fusion(bf16[2048,768]{1,0:T(8,128)(2,1)} %get-tuple-element.138, bf16[24,8,16,128]{3,2,1,0:T(8,128)(2,1)S(1)} %bitcast.159), kind=kOutput, calls=%fused_computation.258 | convolution fusion | flops 604127232 | bytes 4227072 | tf_op jit(solution)/shard_map/dot_general | solution.py:101
  158.9 61.6 %reduce-scatter.5.cloned.1.call-done = bf16[96,192]{1,0:T(8,128)(2,1)} async-done(((bf16[768,192]{1,0:T(8,128)(2,1)}), bf16[96,192]{1,0:T(8,128)(2,1)}) %reduce-scatter.5.cloned.1.call-update) | async-done | bytes 36880 | tf_op jit(solution)/shard_map/reduce_scatter | solution.py:133
  220.9 19.7 %add_convert_fusion = bf16[1,16,128,192]{3,1,2,0:T(8,128)(2,1)} fusion(bf16[1,16,128,192]{3,1,2,0:T(8,128)(2,1)} %copy-done.4, bf16[1,16,128,192]{3,1,2,0:T(8,128)(2,1)S(1)} %get-tuple-element.80, bf16[1,16,3,192]{3,1,2,0:T(8,128)(2,1)} %collective-permute-done.2, bf16[1,16,3,192]{3,1,2,0:T(8,128)(2,1)} %collective-permute-done.3, ...), kind=kLoop, calls=%fused_computation.236 | loop fusion | flops 61341696 | bytes 35472128 | tf_op jit(solution)/shard_map/convert_element_type | solution.py:124
  240.6 2.6 copy.47
  243.2 8.7 %all-reduce.6.cloned.1.call-done = (bf16[24,768]{1,0:T(8,128)(2,1)}, bf16[96,192]{1,0:T(8,128)(2,1)}) async-done(((bf16[24,768]{1,0:T(8,128)(2,1)}, bf16[96,192]{1,0:T(8,128)(2,1)}), (bf16[24,768]{1,0:T(8,128)(2,1)}, bf16[96,192]{1,0:T(8,128)(2,1)})) %all-reduce.6.cloned.1.call-update) | async-done | bytes 73744 | tf_op jit(solution)/shard_map/psum | solution.py:126
  (301 shorter events, 27.2 us)
Async XLA Ops:
  7.2 151.7 %reduce-scatter.3.cloned.1.call-start = ((), (), s32[]{:S(2)}) async-start(), calls=%async_computation.2 | async-start | bytes 331776 | tf_op jit(solution)/shard_map/reduce_scatter | solution.py:130
  14.2 6.6 %collective-permute-start.1 = (bf16[1,16,3,192]{3,1,2,0:T(8,128)(2,1)S(1)}, bf16[1,16,3,192]{3,1,2,0:T(8,128)(2,1)S(1)}, u32[]{:S(2)}, u32[]{:S(2)}) collective-permute-start(bf16[1,16,3,192]{3,1,2,0:T(8,128)(2,1)S(1)} %get-tuple-element.86), channel_id=1, source_target_pairs={{1,0},{2,1},{3,2},{0,3},{5,4},{6,5},{7,6},{4,7},{9,8},{10,9},{11,1... | collective-permute-start | bytes 55304 | tf_op jit(solution)/shard_map/ppermute | solution.py:17
  16.6 4.2 %collective-permute-start = (bf16[1,16,3,192]{3,1,2,0:T(8,128)(2,1)S(1)}, bf16[1,16,3,192]{3,1,2,0:T(8,128)(2,1)S(1)}, u32[]{:S(2)}, u32[]{:S(2)}) collective-permute-start(bf16[1,16,3,192]{3,1,2,0:T(8,128)(2,1)S(1)} %get-tuple-element.85), channel_id=1, source_target_pairs={{0,1},{1,2},{2,3},{3,0},{4,5},{5,6},{6,7},{7,4},{8,9},{9,10},{10,1... | collective-permute-start | bytes 55304 | tf_op jit(solution)/shard_map/ppermute | solution.py:16
  94.7 62.5 %collective-permute-start.2 = (bf16[1,16,3,192]{3,1,2,0:T(8,128)(2,1)}, bf16[1,16,3,192]{3,1,2,0:T(8,128)(2,1)}, u32[]{:S(2)}, u32[]{:S(2)}) collective-permute-start(bf16[1,16,3,192]{3,1,2,0:T(8,128)(2,1)} %get-tuple-element.84), channel_id=1, source_target_pairs={{0,1},{1,2},{2,3},{3,0},{4,5},{5,6},{6,7},{7,4},{8,9},{9,10},{10,1... | collective-permute-start | bytes 55304 | tf_op jit(solution)/shard_map/ppermute | solution.py:16
  95.5 61.8 %collective-permute-start.3 = (bf16[1,16,3,192]{3,1,2,0:T(8,128)(2,1)}, bf16[1,16,3,192]{3,1,2,0:T(8,128)(2,1)}, u32[]{:S(2)}, u32[]{:S(2)}) collective-permute-start(bf16[1,16,3,192]{3,1,2,0:T(8,128)(2,1)} %get-tuple-element.83), channel_id=1, source_target_pairs={{1,0},{2,1},{3,2},{0,3},{5,4},{6,5},{7,6},{4,7},{9,8},{10,9},{11,1... | collective-permute-start | bytes 55304 | tf_op jit(solution)/shard_map/ppermute | solution.py:17
  96.5 124.0 %reduce-scatter.5.cloned.1.call-start = ((), (), s32[]{:S(2)}) async-start(), calls=%async_computation.3 | async-start | bytes 442368 | tf_op jit(solution)/shard_map/reduce_scatter | solution.py:133
  153.8 98.1 %all-reduce.6.cloned.1.call-start = ((), (), s32[]{:S(2)}) async-start(), calls=%async_computation.4 | async-start | bytes 172032 | tf_op jit(solution)/shard_map/psum | solution.py:126
  155.0 65.5 %copy-start.24 = (f32[1,1,192]{2,1,0:T(1,128)S(1)}, f32[1,1,192]{2,1,0:T(1,128)}, u32[]{:S(2)}) copy-start(f32[1,1,192]{2,1,0:T(1,128)} %copy-done.23) | copy-start | bytes 2308
  155.0 65.5 %copy-start.26 = (f32[1,1,192]{2,1,0:T(1,128)S(1)}, f32[1,1,192]{2,1,0:T(1,128)}, u32[]{:S(2)}) copy-start(f32[1,1,192]{2,1,0:T(1,128)} %copy-done.25) | copy-start | bytes 2308
  155.1 65.5 %copy-start.28 = (f32[1,1,192]{2,1,0:T(1,128)S(1)}, f32[1,1,192]{2,1,0:T(1,128)}, u32[]{:S(2)}) copy-start(f32[1,1,192]{2,1,0:T(1,128)} %copy-done.27) | copy-start | bytes 2308
  155.1 65.5 %copy-start.30 = (f32[1,1,192]{2,1,0:T(1,128)S(1)}, f32[1,1,192]{2,1,0:T(1,128)}, u32[]{:S(2)}) copy-start(f32[1,1,192]{2,1,0:T(1,128)} %copy-done.29) | copy-start | bytes 2308
  155.1 65.5 %copy-start.32 = (f32[1,1,192]{2,1,0:T(1,128)S(1)}, f32[1,1,192]{2,1,0:T(1,128)}, u32[]{:S(2)}) copy-start(f32[1,1,192]{2,1,0:T(1,128)} %copy-done.31) | copy-start | bytes 2308
  155.1 65.5 %copy-start.34 = (f32[1,1,192]{2,1,0:T(1,128)S(1)}, f32[1,1,192]{2,1,0:T(1,128)}, u32[]{:S(2)}) copy-start(f32[1,1,192]{2,1,0:T(1,128)} %copy-done.33) | copy-start | bytes 2308
  155.1 65.5 %copy-start.36 = (f32[1,1,192]{2,1,0:T(1,128)S(1)}, f32[1,1,192]{2,1,0:T(1,128)}, u32[]{:S(2)}) copy-start(f32[1,1,192]{2,1,0:T(1,128)} %copy-done.35) | copy-start | bytes 2308
  155.1 65.5 %copy-start.38 = (f32[1,1,192]{2,1,0:T(1,128)S(1)}, f32[1,1,192]{2,1,0:T(1,128)}, u32[]{:S(2)}) copy-start(f32[1,1,192]{2,1,0:T(1,128)} %copy-done.37) | copy-start | bytes 2308
  155.1 65.5 %copy-start.40 = (f32[1,1,192]{2,1,0:T(1,128)S(1)}, f32[1,1,192]{2,1,0:T(1,128)}, u32[]{:S(2)}) copy-start(f32[1,1,192]{2,1,0:T(1,128)} %copy-done.39) | copy-start | bytes 2308
  155.1 65.5 %copy-start.42 = (f32[1,1,192]{2,1,0:T(1,128)S(1)}, f32[1,1,192]{2,1,0:T(1,128)}, u32[]{:S(2)}) copy-start(f32[1,1,192]{2,1,0:T(1,128)} %copy-done.41) | copy-start | bytes 2308
  155.1 65.5 %copy-start.44 = (f32[1,1,192]{2,1,0:T(1,128)S(1)}, f32[1,1,192]{2,1,0:T(1,128)}, u32[]{:S(2)}) copy-start(f32[1,1,192]{2,1,0:T(1,128)} %copy-done.43) | copy-start | bytes 2308
  155.1 65.5 %copy-start.46 = (f32[1,1,192]{2,1,0:T(1,128)S(1)}, f32[1,1,192]{2,1,0:T(1,128)}, u32[]{:S(2)}) copy-start(f32[1,1,192]{2,1,0:T(1,128)} %copy-done.45) | copy-start | bytes 2308
  155.2 65.5 %copy-start.48 = (f32[1,1,192]{2,1,0:T(1,128)S(1)}, f32[1,1,192]{2,1,0:T(1,128)}, u32[]{:S(2)}) copy-start(f32[1,1,192]{2,1,0:T(1,128)} %copy-done.47) | copy-start | bytes 2308
  155.2 65.5 %copy-start.50 = (f32[1,1,192]{2,1,0:T(1,128)S(1)}, f32[1,1,192]{2,1,0:T(1,128)}, u32[]{:S(2)}) copy-start(f32[1,1,192]{2,1,0:T(1,128)} %copy-done.49) | copy-start | bytes 2308
  155.2 65.5 %copy-start.52 = (f32[1,1,192]{2,1,0:T(1,128)S(1)}, f32[1,1,192]{2,1,0:T(1,128)}, u32[]{:S(2)}) copy-start(f32[1,1,192]{2,1,0:T(1,128)} %copy-done.51) | copy-start | bytes 2308
  155.2 65.5 %copy-start.54 = (f32[1,1,192]{2,1,0:T(1,128)S(1)}, f32[1,1,192]{2,1,0:T(1,128)}, u32[]{:S(2)}) copy-start(f32[1,1,192]{2,1,0:T(1,128)} %copy-done.53) | copy-start | bytes 2308
  155.2 65.5 %copy-start.56 = (f32[1,1,192]{2,1,0:T(1,128)S(1)}, f32[1,1,192]{2,1,0:T(1,128)}, u32[]{:S(2)}) copy-start(f32[1,1,192]{2,1,0:T(1,128)} %copy-done.55) | copy-start | bytes 2308
  (106 other events, 1863.9 us)
Sparse Core Ops, SparseCore 0:
  96.6 59.6 reduce-scatter.2
  160.2 60.2 reduce-scatter.4
  223.0 28.8 all-reduce.5
where the time goes:
time: 262 us; the launch traced here: 261 us
  other arithmetic  81.7 us (31%)
  waiting for transfers between devices  70.4 us (27%)
  blocking collectives  40.8 us (16%)
  local copies, waits for them, and re-layouts  31 us (12%)
  matrix products  17.5 us (7%)
  between operations  15.6 us (6%)
  starting transfers between devices  4.3 us (2%)
    reduce_scatter x1, waiting for transfers between devices, per_device(): lax.psum_scatter(summed_out.astype(jnp.bfloat16), 'dp', scatter_dimension...  61.6 us
    psum x1, blocking collectives, per_device(): lax.psum((part_kernel, part_gain, part_bias), ('dp', 'lon'))  40.8 us
    reduce_sum x4, other arithmetic, kernel_terms(): cols_out.append(jnp.sum(window * d_float, axis=(0, 1, 2)))  24.6 us
    convert_element_type x1, other arithmetic, per_device(): (grad_m.astype(jnp.float32) + mask_f * spread).astype(jnp.bfloat16)  19.7 us
    reduce_sum x1, other arithmetic, per_device(): mean_c = jnp.mean(conv, axis=-1, keepdims=True)  19.3 us
    unnamed x258, local copies, waits for them, and re-layouts  16 us
    psum x1, waiting for transfers between devices, per_device(): lax.psum(part_in.astype(jnp.bfloat16), 'lon').astype(jnp.float32)  8.74 us
  transfers between devices with their start and end apart: 7, of which 2 were waited for; matrix products, arithmetic and copies ran while one was open for 18% of the time, Pallas kernels for 0%

commit v1 on v0

v1 whole, which is shorter than its diff:
```python
import functools
import math

import jax
import jax.numpy as jnp
from jax import lax
from jax.experimental import pallas as pl
from jax.experimental.pallas import tpu as pltpu
from jax.sharding import PartitionSpec as P

F32 = jnp.float32
BF16 = jnp.bfloat16
LIMIT = 56 * 2**20
EDGE = 8


def dot(lhs, rhs):
    return jnp.dot(lhs, rhs, preferred_element_type=F32)


def dot_t(lhs, rhs):
    return lax.dot_general(lhs, rhs, (((1,), (1,)), ((), ())), preferred_element_type=F32)


def t_dot(lhs, rhs):
    return lax.dot_general(lhs, rhs, (((0,), (0,)), ((), ())), preferred_element_type=F32)


def build_tiles(kernel_ref, tiles_a, tiles_b, flip):
    row = lax.broadcasted_iota(jnp.int32, (128, 128), 0)
    lane = lax.broadcasted_iota(jnp.int32, (128, 128), 1)
    eye = row == lane
    eye_half = (row & 63) == (lane & 63)
    low = lane[:1] < 64
    zero_block = jnp.zeros((128, 128), BF16)
    zero_row = jnp.zeros((1, 128), F32)
    for b in range(7):
        taps = []
        for a in range(7):
            at, bt = (6 - a, 6 - b) if flip else (a, b)
            taps.append(kernel_ref[at, bt : bt + 1, :])
        blocks = [jnp.where(eye, tap[:, :128], 0.0).astype(BF16) for tap in taps]
        rests = [jnp.concatenate([tap[:, 128:]] * 2, axis=1) for tap in taps]

        def block(a):
            return blocks[a] if 0 <= a < 7 else zero_block

        def rest(a):
            return rests[a] if 0 <= a < 7 else zero_row

        for d in range(4):
            for i in range(2):
                for o in range(2):
                    tiles_a[b * 4 + d, i * 128 : (i + 1) * 128, o * 128 : (o + 1) * 128] = block(
                        2 * d + i - o
                    )
        for d in range(3):
            for i in range(2):
                for o in range(2):
                    a = 4 * d + 2 * i - 2 * o
                    top = jnp.where(low, rest(a), rest(a - 1))
                    bottom = jnp.where(low, rest(a + 1), rest(a))
                    part = jnp.where(eye_half, jnp.where(row < 64, top, bottom), 0.0)
                    tiles_b[b * 3 + d, i * 128 : (i + 1) * 128, o * 128 : (o + 1) * 128] = (
                        part.astype(BF16)
                    )


def pack_shifts(rows_a, rows_b, packed_a, packed_b, first, width):
    for b in range(7):
        at = first + b

        def pairs(q, carry):
            packed_a[b, q] = jnp.concatenate(
                [rows_a[2 * q, at : at + width], rows_a[2 * q + 1, at : at + width]], axis=1
            ).astype(BF16)
            return carry

        def quads(q, carry):
            packed_b[b, q] = jnp.concatenate(
                [rows_b[2 * q, at : at + width], rows_b[2 * q + 1, at : at + width]], axis=1
            ).astype(BF16)
            return carry

        lax.fori_loop(0, packed_a.shape[1], pairs, 0)
        lax.fori_loop(0, packed_b.shape[1], quads, 0)


def band_products(packed_a, packed_b, tiles_a, tiles_b, out_a, out_b, width):
    halves = 2
    pairs, quads = out_a.shape[0] // halves, out_b.shape[0] // halves

    def half(h, carry):
        lhs = jnp.concatenate(
            [
                packed_a[b, pl.ds(pairs * h + d, pairs)].reshape(pairs * width, 256)
                for b in range(7)
                for d in range(4)
            ],
            axis=1,
        )
        out_a[pl.ds(pairs * h, pairs)] = dot(lhs, tiles_a[...].reshape(28 * 256, 256)).reshape(
            pairs, width, 256
        )
        lhs = jnp.concatenate(
            [
                packed_b[b, pl.ds(quads * h + d, quads)].reshape(quads * width, 256)
                for b in range(7)
                for d in range(3)
            ],
            axis=1,
        )
        out_b[pl.ds(quads * h, quads)] = dot(lhs, tiles_b[...].reshape(21 * 256, 256)).reshape(
            quads, width, 256
        )
        return carry

    lax.fori_loop(0, halves, half, 0)


def gelu_parts(z):
    u = 1.0 + (0.3275911 / math.sqrt(2.0)) * jnp.abs(z)
    t = 1.0 / u
    e = jnp.exp2(z * z * (-0.5 * math.log2(math.e)))
    poly = t * (
        0.5 * 0.254829592
        + t
        * (
            0.5 * -0.284496736
            + t * (0.5 * 1.421413741 + t * (0.5 * -1.453152027 + t * (0.5 * 1.061405429)))
        )
    )
    tail = poly * e
    cumulative = jnp.where(z >= 0.0, 1.0 - tail, tail)
    return cumulative, e * (1.0 / math.sqrt(2.0 * math.pi))


def mask_columns(mask_ref, columns):
    turned = mask_ref[...].astype(F32).T
    for i in range(mask_ref.shape[0]):
        columns[i] = jnp.broadcast_to(turned[:, i : i + 1], columns.shape[1:])


def forward_kernel(
    fields,
    cotangent,
    mask,
    halo_before,
    halo_after,
    kernel,
    gain,
    w_in,
    bias,
    w_out,
    output,
    d_rows_a,
    d_rows_b,
    payload,
    gain_sum,
    bias_sum,
    columns,
    rows_a,
    rows_b,
    tiles_a,
    tiles_b,
    packed_a,
    packed_b,
    conv_a,
    conv_b,
    wide_in,
    total_in,
    total_out,
    shards,
):
    lat, lon, channels = fields.shape
    hidden = w_in.shape[1]
    width = lon + 2 * EDGE
    build_tiles(kernel, tiles_a, tiles_b, False)
    mask_columns(mask, columns)
    wide_in[0:channels] = w_in[...]
    wide_in[channels:256] = w_in[128:channels]

    rows_a[...] = jnp.zeros_like(rows_a)
    rows_b[...] = jnp.zeros_like(rows_b)
    before, after = halo_before[...].astype(F32), halo_after[...].astype(F32)
    rest = {}
    for i in range(lat):
        m = columns[i]
        x = fields[i].astype(F32)
        rows_a[i + 3, 2 * EDGE : 2 * EDGE + lon] = x[:, :128] * m
        rows_a[i + 3, EDGE : 2 * EDGE] = before[i, :EDGE, :128]
        rows_a[i + 3, 2 * EDGE + lon : 3 * EDGE + lon] = after[i, :EDGE, :128]
        rest[i] = jnp.concatenate(
            [before[i, :EDGE, 128:], x[:, 128:] * m[:, :64], after[i, :EDGE, 128:]], axis=0
        )
    blank = jnp.zeros((width, 64), F32)
    for q in range(1, 10):
        pair = [rest.get(2 * q - 3, blank), rest.get(2 * q - 2, blank)]
        rows_b[q, EDGE : EDGE + width] = jnp.concatenate(pair, axis=1)

    pack_shifts(rows_a, rows_b, packed_a, packed_b, EDGE - 3, width)
    band_products(packed_a, packed_b, tiles_a, tiles_b, conv_a, conv_b, width)

    d_rows_a[...] = jnp.zeros_like(d_rows_a)
    d_rows_b[...] = jnp.zeros_like(d_rows_b)
    total_in[...] = jnp.zeros_like(total_in)
    total_out[...] = jnp.zeros_like(total_out)
    gain_sum[...] = jnp.zeros_like(gain_sum)
    bias_sum[...] = jnp.zeros_like(bias_sum)

    sub = lax.broadcasted_iota(jnp.int32, (EDGE, 1), 0)
    near = sub < EDGE // 2
    low = lax.broadcasted_iota(jnp.int32, (1, 128), 1) < 64
    gain_row = gain[...]
    gains = jnp.concatenate([gain_row, gain_row[:, 128:]], axis=1)
    inner = 4 * lon

    def tokens(x):
        return jnp.concatenate(
            [x[EDGE : EDGE + lon], jnp.where(near, x[EDGE + lon :], x[:EDGE])], axis=0
        )

    def quad(r, carry):
        block_a = [conv_a[2 * r], conv_a[2 * r + 1]]
        block_b = conv_b[r]
        nhats, sigmas = [], []
        for i in range(4):
            here = low if i % 2 == 0 else ~low
            xa = tokens(block_a[i // 2][:, (i % 2) * 128 : (i % 2 + 1) * 128])
            xb = tokens(block_b[:, (i // 2) * 128 : (i // 2 + 1) * 128])
            xb = jnp.where(here, xb, 0.0)
            mean = jnp.sum(xa + xb, axis=1, keepdims=True) * (1.0 / channels)
            xa = xa - mean
            xb = jnp.where(here, xb - mean, 0.0)
            var = jnp.sum(xa * xa + xb * xb, axis=1, keepdims=True) * (1.0 / channels)
            sigma = lax.rsqrt(var + 1e-6)
            nhats.append(jnp.concatenate([xa * sigma, xb * sigma], axis=1))
            sigmas.append(sigma)
        normed = jnp.concatenate(
            [n[:lon] for n in nhats] + [n[lon:] for n in nhats], axis=0
        )
        normed = (normed * gains).astype(BF16)
        masked_cot = [
            cotangent[4 * r + i].astype(F32) * columns[4 * r + i][:, :1] for i in range(4)
        ]
        for i in range(4):
            masked_cot.append(
                jnp.where(
                    near,
                    halo_after[4 * r + i].astype(F32)[EDGE:],
                    halo_before[4 * r + i].astype(F32)[EDGE:],
                )
            )
        gm = jnp.concatenate(masked_cot, axis=0).astype(BF16)
        branch, d_normed = None, None
        for h in range(0, hidden, 256):
            z = dot(normed, wide_in[:, h : h + 256]) + bias[:, h : h + 256]
            cumulative, density = gelu_parts(z)
            act = (z * cumulative)[:inner].astype(BF16)
            d_act = dot_t(gm, w_out[h : h + 256, :])
            d_pre = d_act * (cumulative + z * density)
            bias_sum[:, h : h + 256] += jnp.sum(
                d_pre[:inner].reshape(inner // 8, 8, 256), axis=0
            )
            d_pre = d_pre.astype(BF16)
            part = dot(act, w_out[h : h + 256, :])
            branch = part if branch is None else branch + part
            part = dot_t(d_pre, wide_in[:, h : h + 256])
            d_normed = part if d_normed is None else d_normed + part
            total_in[:, h : h + 256] += t_dot(normed[:inner], d_pre[:inner])
            total_out[:, h : h + 256] += t_dot(gm[:inner], act)
        gained = None
        rest_d = []
        for i in range(4):
            row = 4 * r + i
            here = low if i % 2 == 0 else ~low
            x = fields[row].astype(F32) + branch[i * lon : (i + 1) * lon]
            output[row] = (x * columns[row][:, :1]).astype(BF16)
            dn = jnp.concatenate(
                [
                    d_normed[i * lon : (i + 1) * lon],
                    d_normed[inner + i * EDGE : inner + (i + 1) * EDGE],
                ],
                axis=0,
            )
            nhat = nhats[i]
            prod = dn * nhat
            part = jnp.sum(prod[:lon].reshape(lon // 8, 8, 256), axis=0)
            gained = part if gained is None else gained + part
            d_hat = dn * gains
            da, db = d_hat[:, :128], jnp.where(here, d_hat[:, 128:], 0.0)
            mean = jnp.sum(da + db, axis=1, keepdims=True) * (1.0 / channels)
            prod = prod * gains
            corr = jnp.sum(prod[:, :128] + prod[:, 128:], axis=1, keepdims=True) * (1.0 / channels)
            da = sigmas[i] * (da - mean - nhat[:, :128] * corr)
            db = sigmas[i] * (db - mean - nhat[:, 128:] * corr)
            d_rows_a[row + 3, 2 * EDGE : 2 * EDGE + lon] = da[:lon]
            d_rows_a[row + 3, EDGE : 2 * EDGE] = jnp.where(near, 0.0, da[lon:])
            d_rows_a[row + 3, 2 * EDGE + lon : 3 * EDGE + lon] = jnp.where(near, da[lon:], 0.0)
            rest_d.append(db)
        gain_sum[...] += gained

        def spread(db):
            return jnp.concatenate(
                [jnp.where(near, 0.0, db[lon:]), db[:lon], jnp.where(near, db[lon:], 0.0)], axis=0
            )

        at = slice(EDGE, EDGE + width)
        first, second, third, fourth = [
            pltpu.roll(spread(db), 64, axis=1) for db in rest_d
        ]
        d_rows_b[2 * r + 1, at] = jnp.where(low, d_rows_b[2 * r + 1, at], first)
        d_rows_b[2 * r + 2, at] = jnp.where(low, second, third)
        d_rows_b[2 * r + 3, at] = jnp.where(low, fourth, 0.0)
        return carry

    lax.fori_loop(0, lat // 4, quad, 0)

    part_in = jnp.concatenate(
        [total_in[:128], total_in[128:192] + total_in[192:256]], axis=0
    )
    rows = channels // shards
    pieces = []
    for n in range(shards):
        mine = part_in[n * rows : (n + 1) * rows]
        pieces += [mine[:, c : c + 128] for c in range(0, hidden, 128)]
    payload[0] = jnp.concatenate(pieces, axis=0).astype(BF16)
    part_out = total_out[...].T
    rows = hidden // shards
    pieces = []
    for n in range(shards):
        mine = part_out[n * rows : (n + 1) * rows]
        pieces.append(mine[:, :128])
        pieces.append(
            jnp.concatenate([mine[: rows // 2, 128:], mine[rows // 2 :, 128:]], axis=1)
        )
    payload[1] = jnp.concatenate(pieces, axis=0).astype(BF16)


def backward_kernel(
    fields,
    cotangent,
    mask,
    kernel,
    d_rows_a,
    d_rows_b,
    gain_sum,
    bias_sum,
    grad_fields,
    small,
    columns,
    tiles_a,
    tiles_b,
    packed_a,
    packed_b,
    spread_a,
    spread_b,
    turned_a,
    turned_b,
):
    lat, lon, channels = fields.shape
    build_tiles(kernel, tiles_a, tiles_b, True)
    mask_columns(mask, columns)
    pack_shifts(d_rows_a, d_rows_b, packed_a, packed_b, 2 * EDGE - 3, lon)

    for i in range(lat):
        x = fields[i].astype(F32) * columns[i][:, :1]
        x = x.T.astype(BF16)
        s = i // 2
        turned_a[(i % 2) * 128 : (i % 2 + 1) * 128, s * lon : (s + 1) * lon] = x[:128]
        s = i // 4
        turned_b[(i % 4) * 64 : (i % 4 + 1) * 64, s * lon : (s + 1) * lon] = x[128:]

    row = lax.broadcasted_iota(jnp.int32, (128, 128), 0)
    lane = lax.broadcasted_iota(jnp.int32, (128, 128), 1)
    eye = row == lane
    eye_half = (row[:64]) == (lane[:64] & 63)
    small[...] = jnp.zeros_like(small)
    for b in range(7):
        tap = 6 - b
        blocks = {}
        for d in range(4):
            rhs = packed_a[b, 3 - d : 3 - d + lat // 2].reshape(lat // 2 * lon, 256)
            g = dot(turned_a[...], rhs)
            for i in range(2):
                for o in range(2):
                    a = 2 * d + i - o
                    part = g[i * 128 : (i + 1) * 128, o * 128 : (o + 1) * 128]
                    if 0 <= a < 7:
                        blocks[a] = part if a not in blocks else blocks[a] + part
        for a in range(7):
            small[a, tap : tap + 1, :128] = jnp.sum(
                jnp.where(eye, blocks[a], 0.0), axis=0, keepdims=True
            )
        lines = []
        for d in range(3):
            rhs = packed_b[b, 2 - d : 2 - d + lat // 4].reshape(lat // 4 * lon, 256)
            g = dot(turned_b[...], rhs)
            for i in range(4):
                part = g[i * 64 : (i + 1) * 64]
                lines.append(
                    [
                        jnp.sum(
                            jnp.where(eye_half, part[:, c : c + 128], 0.0), axis=0, keepdims=True
                        )
                        for c in (0, 128)
                    ]
                )
        for a in range(7):
            total = None
            for o in range(4):
                line = lines[a + 2 + o][o // 2][:, (o % 2) * 64 : (o % 2 + 1) * 64]
                total = line if total is None else total + line
            small[a, tap : tap + 1, 128:channels] = total
    gained = jnp.sum(gain_sum[...], axis=0, keepdims=True)
    small[0, 7:8, :128] = gained[:, :128]
    small[0, 7:8, 128:channels] = gained[:, 128:192] + gained[:, 192:256]
    biased = jnp.sum(bias_sum[...], axis=0, keepdims=True)
    for k in range(biased.shape[1] // 256):
        small[1 + k, 7:8, :] = biased[:, k * 256 : (k + 1) * 256]

    band_products(packed_a, packed_b, tiles_a, tiles_b, spread_a, spread_b, lon)
    for i in range(lat):
        a = spread_a[i // 2][:, (i % 2) * 128 : (i % 2 + 1) * 128]
        b = spread_b[i // 4][:, (i % 4) * 64 : (i % 4 + 1) * 64]
        x = cotangent[i].astype(F32) + jnp.concatenate([a, b], axis=1)
        grad_fields[i] = (x * columns[i][:, :1]).astype(BF16)


def swapped(x, axis, bit):
    peers = lax.axis_size(axis)
    return lax.ppermute(x, axis, [(i, i ^ bit) for i in range(peers)])


def bits_of(count):
    return [1 << k for k in range(count.bit_length() - 1)]


def reduced(payload, small):
    shards, tiles = lax.axis_size("dp"), lax.axis_size("lon")
    me, tile = lax.axis_index("dp"), lax.axis_index("lon")
    core = tile & 1

    def both(x, y):
        return (x.astype(F32) + y.astype(F32)).astype(BF16)

    def pick(x, axis, at):
        return lax.dynamic_index_in_dim(x, at, axis, keepdims=False)

    mine = both(pick(payload, 0, core), swapped(pick(payload, 0, 1 - core), "lon", 1))
    small = small + swapped(small, "lon", 1)
    mine = mine.reshape(shards, -1, 128)
    for bit in bits_of(shards):
        have = (me // bit) & 1
        split = mine.reshape(mine.shape[0] // 2, 2, -1, 128)
        mine = both(pick(split, 1, have), swapped(pick(split, 1, 1 - have), "dp", bit))
        small = small + swapped(small, "dp", bit)
    mine = mine.reshape(-1, 128)
    for bit in bits_of(tiles)[1:]:
        mine = both(mine, swapped(mine, "lon", bit))
        small = small + swapped(small, "lon", bit)
    other = swapped(mine, "lon", 1)
    first = core == 0
    return jnp.where(first, mine, other), jnp.where(first, other, mine), small


def per_device(fields, cotangent, land_sea, kernel, ln_gain, weight_in, bias_in, weight_out):
    samples, lat, lon, channels = fields.shape
    hidden = weight_in.shape[1]
    shards, tiles = lax.axis_size("dp"), lax.axis_size("lon")
    width = lon + 2 * EDGE
    mask_b = land_sea.astype(BF16)[:, :, None]
    fields3, cot3 = fields[0], cotangent[0]

    def edge(cols):
        m = mask_b[:, cols]
        return jnp.concatenate([fields3[:, cols] * m, cot3[:, cols] * m], axis=1)

    up = [(i, (i + 1) % tiles) for i in range(tiles)]
    before = lax.ppermute(edge(slice(lon - EDGE, lon)), "lon", up)
    after = lax.ppermute(edge(slice(0, EDGE)), "lon", [(j, i) for i, j in up])

    tiles_shapes = [pltpu.VMEM((28, 256, 256), BF16), pltpu.VMEM((21, 256, 256), BF16)]
    output, d_rows_a, d_rows_b, payload, gain_sum, bias_sum = pl.pallas_call(
        functools.partial(forward_kernel, shards=shards),
        out_shape=[
            jax.ShapeDtypeStruct((lat, lon, channels), BF16),
            jax.ShapeDtypeStruct((lat + 6, width + 16, 128), F32),
            jax.ShapeDtypeStruct((lat // 2 + 4, width + 16, 128), F32),
            jax.ShapeDtypeStruct((2, channels * hidden // 128, 128), BF16),
            jax.ShapeDtypeStruct((8, 256), F32),
            jax.ShapeDtypeStruct((8, hidden), F32),
        ],
        scratch_shapes=[
            pltpu.VMEM((lat, lon, 128), F32),
            pltpu.VMEM((lat + 6, width + 16, 128), F32),
            pltpu.VMEM((lat // 2 + 4, width + 16, 128), F32),
            *tiles_shapes,
            pltpu.VMEM((7, lat // 2 + 3, width, 256), BF16),
            pltpu.VMEM((7, lat // 4 + 2, width, 256), BF16),
            pltpu.VMEM((lat // 2, width, 256), F32),
            pltpu.VMEM((lat // 4, width, 256), F32),
            pltpu.VMEM((256, hidden), BF16),
            pltpu.VMEM((256, hidden), F32),
            pltpu.VMEM((channels, hidden), F32),
        ],
        compiler_params=pltpu.CompilerParams(vmem_limit_bytes=LIMIT),
        name="forward",
    )(
        fields3,
        cot3,
        land_sea,
        before,
        after,
        kernel,
        ln_gain[None],
        weight_in,
        bias_in[None],
        weight_out,
    )
    grad_fields, small = pl.pallas_call(
        backward_kernel,
        out_shape=[
            jax.ShapeDtypeStruct((lat, lon, channels), BF16),
            jax.ShapeDtypeStruct((7, 8, 256), F32),
        ],
        scratch_shapes=[
            pltpu.VMEM((lat, lon, 128), F32),
            *tiles_shapes,
            pltpu.VMEM((7, lat // 2 + 3, lon, 256), BF16),
            pltpu.VMEM((7, lat // 4 + 2, lon, 256), BF16),
            pltpu.VMEM((lat // 2, lon, 256), F32),
            pltpu.VMEM((lat // 4, lon, 256), F32),
            pltpu.VMEM((256, lat // 2 * lon), BF16),
            pltpu.VMEM((256, lat // 4 * lon), BF16),
        ],
        compiler_params=pltpu.CompilerParams(vmem_limit_bytes=LIMIT),
        name="backward",
    )(fields3, cot3, land_sea, kernel, d_rows_a, d_rows_b, gain_sum, bias_sum)

    sum_in, sum_out, small = reduced(payload, small)
    scale = 1.0 / math.sqrt(samples * lat * lon * shards * tiles)
    rows = channels // shards
    sum_in = sum_in.reshape(hidden // 128, rows, 128).transpose(1, 0, 2).reshape(rows, hidden)
    rows = hidden // shards
    rest = sum_out[rows:]
    sum_out = jnp.concatenate(
        [sum_out[:rows], jnp.concatenate([rest[:, :64], rest[:, 64:]], axis=0)], axis=1
    )
    return (
        output[None],
        grad_fields[None],
        sum_in.astype(F32) * scale,
        sum_out.astype(F32) * scale,
        small[:, :7, :channels] * scale,
        small[0, 7, :channels] * scale,
        small[1 : 1 + hidden // 256, 7].reshape(hidden) * scale,
    )


def solution(mesh):
    placed = (
        P("dp", None, "lon", None),
        P("dp", None, "lon", None),
        P(None, "lon"),
        P(),
        P(),
        P(),
        P(),
        P(),
    )
    return jax.shard_map(
        per_device,
        mesh=mesh,
        in_specs=placed,
        out_specs=(
            P("dp", None, "lon", None),
            P("dp", None, "lon", None),
            P("dp", None),
            P("dp", None),
            P(),
            P(),
            P(),
        ),
        check_vma=False,
    )
```

time: 262 us -> 90.3 us (0.34)
  other arithmetic: 81.7 us -> 3.08 us
  waiting for transfers between devices: 70.4 us -> 14.3 us
  Pallas kernels: 0 us -> 44.4 us
  blocking collectives: 40.8 us -> 0 us
  local copies, waits for them, and re-layouts: 31 us -> 9.4 us
  matrix products: 17.5 us -> 0 us
  between operations: 15.6 us -> 0.87 us
  starting transfers between devices: 4.3 us -> 18 us
    reduce_scatter x2 -> x0, waiting for transfers between devices: 61.6 us -> none  [the longest x1 61.6 us: per_device(): lax.psum_scatter(summed_out.astype(jnp.bfloat16), 'dp', scatter_dimension...]
    reduce_sum x7 -> x0, other arithmetic: 47.8 us -> none  [the longest x4 24.6 us: kernel_terms(): cols_out.append(jnp.sum(window * d_float, axis=(0, 1, 2)))]
    pallas_call x0 -> x2, Pallas kernels: none -> 44.4 us  [the longest x1 26.4 us: per_device(): pl.pallas_call(functools.partial(forward_kernel, shards=shards), out_shap...]
    psum x1 -> x0, blocking collectives: 40.8 us -> none  [per_device(): lax.psum((part_kernel, part_gain, part_bias), ('dp', 'lon'))]
    convert_element_type x4, other arithmetic: 24.1 us -> 0.17 us  [both(): return (x.astype(F32) + y.astype(F32)).astype(BF16)]
    dot_general x6 -> x0, matrix products: 17.5 us -> none  [the longest x1 4.64 us: per_device(): lax.dot_general(grad_flat, weight_out, (((1,), (1,)), ((), ())), preferre...]
    ppermute x4 -> x13, waiting for transfers between devices: 0.01 us -> 14.3 us  [the longest x11 12.1 us: swapped(): return lax.ppermute(x, axis, [(i, i ^ bit) for i in range(peers)])]
    ppermute x4 -> x13, starting transfers between devices: 4.18 us -> 18 us  [the longest x11 15.5 us: swapped(): return lax.ppermute(x, axis, [(i, i ^ bit) for i in range(peers)])]
  transfers between devices with their start and end apart: 7 -> 13, of which waited for: 2 -> 9; matrix products, arithmetic and copies ran while one was open for 18% -> 8% of each run, Pallas kernels for 0% -> 20%
where the time goes in v1:
time: 90.3 us; the launch traced here: 90.1 us
  Pallas kernels  44.4 us (49%)
  starting transfers between devices  18 us (20%)
  waiting for transfers between devices  14.3 us (16%)
  local copies, waits for them, and re-layouts  9.4 us (10%)
  other arithmetic  3.08 us (3%)
    pallas_call x1, Pallas kernels, per_device(): pl.pallas_call(functools.partial(forward_kernel, shards=shards), out_shap...  26.4 us
    pallas_call x1, Pallas kernels, per_device(): pl.pallas_call(backward_kernel, out_shape=[jax.ShapeDtypeStruct((lat, lon...  18.1 us
    ppermute x11, starting transfers between devices, swapped(): return lax.ppermute(x, axis, [(i, i ^ bit) for i in range(peers)])  15.5 us
    ppermute x11, waiting for transfers between devices, swapped(): return lax.ppermute(x, axis, [(i, i ^ bit) for i in range(peers)])  12.1 us
    unnamed x29, local copies, waits for them, and re-layouts  6.92 us
    ppermute x1, starting transfers between devices, per_device(): after = lax.ppermute(edge(slice(0, EDGE)), 'lon', [(j, i) for i, j in up])  2 us
  transfers between devices with their start and end apart: 13, of which 9 were waited for; matrix products, arithmetic and copies ran while one was open for 8% of the time, Pallas kernels for 20%

profile of v1, /device:TPU:0, one launch (start us, length us, event | category | flops | bytes accessed | tf_op | source)
XLA Modules:
  0.0 90.1 jit_solution(2070718425715829509)
XLA Ops:
  0.7 1.5 %copy.24 = bf16[1,16,128,192]{3,2,1,0:T(8,128)(2,1)S(1)} copy(bf16[1,16,128,192]{2,3,1,0:T(8,128)(2,1)} %param.8) | data formatting | bytes 1572864 | tf_op args[0]
  3.7 2.0 %collective-permute-start.1 = (bf16[16,16,192]{2,1,0:T(8,128)(2,1)S(1)}, bf16[16,16,192]{2,1,0:T(8,128)(2,1)S(1)}, u32[]{:S(2)}, u32[]{:S(2)}) collective-permute-start(bf16[16,16,192]{2,1,0:T(8,128)(2,1)S(1)} %pad_maximum_fusion.1), channel_id=1, source_target_pairs={{1,0},{2,1},{3,2},{0,3},{5,4},{6,5},{7,6},{4,7},{9,8},{10,9},{11,1... | collective-permute-start | bytes 294920 | tf_op jit(solution)/shard_map/ppermute | solution.py:481
  6.3 0.9 %copy.29.w_out = bf16[768,192]{1,0:T(8,128)(2,1)} copy(bf16[768,192]{0,1:T(8,128)(2,1)S(1)} %copy-done.6) | data formatting | bytes 589824 | tf_op args[7]
  7.2 1.1 %collective-permute-done.halo_before = bf16[16,16,192]{2,1,0:T(8,128)(2,1)S(1)} collective-permute-done((bf16[16,16,192]{2,1,0:T(8,128)(2,1)S(1)}, bf16[16,16,192]{2,1,0:T(8,128)(2,1)S(1)}, u32[]{:S(2)}, u32[]{:S(2)}) %collective-permute-start) | collective-permute-done | bytes 98336 | tf_op jit(solution)/shard_map/ppermute | solution.py:480
  8.3 1.2 %collective-permute-done.1.halo_after = bf16[16,16,192]{2,1,0:T(8,128)(2,1)S(1)} collective-permute-done((bf16[16,16,192]{2,1,0:T(8,128)(2,1)S(1)}, bf16[16,16,192]{2,1,0:T(8,128)(2,1)S(1)}, u32[]{:S(2)}, u32[]{:S(2)}) %collective-permute-start.1) | collective-permute-done | bytes 98336 | tf_op jit(solution)/shard_map/ppermute | solution.py:481
  10.2 26.4 %forward.1 = (bf16[16,128,192]{2,1,0:T(8,128)(2,1)}, f32[22,160,128]{2,1,0:T(8,128)}, f32[12,160,128]{2,1,0:T(8,128)}, bf16[2,1152,128]{2,1,0:T(8,128)(2,1)}, f32[8,256]{1,0:T(8,128)}, /*index=5*/f32[8,768]{1,0:T(8,128)}) custom-call(bf16[16,128,192]{2,1,0:T(8,128)(2,1)} %bitcast.40, bf16[16,128,192]{2,1,0:T(8,128)(2,1)} %bitcast.43, s32[16,128]{1,0:T(8,128)} %mask.3, ...), custom_call_target="tpu_custom_call" | custom-call | tf_op jit(solution)/shard_map/forward/pallas_call | solution.py:484
  36.6 1.0 %dynamic-slice_bitcast_fusion = bf16[1152,128]{1,0:T(8,128)(2,1)S(1)} fusion(bf16[2,1152,128]{2,1,0:T(8,128)(2,1)} %get-tuple-element.21, s32[]{:T(128)S(6)} %select_n.51), kind=kLoop, calls=%fused_computation.4 | loop fusion | bytes 589828 | tf_op jit(solution)/shard_map/jit(dynamic_index_in_dim)/squeeze | solution.py:448
  37.5 1.3 %collective-permute-start.2 = (bf16[1152,128]{1,0:T(8,128)(2,1)S(1)}, bf16[1152,128]{1,0:T(8,128)(2,1)S(1)}, u32[]{:S(2)}, u32[]{:S(2)}) collective-permute-start(bf16[1152,128]{1,0:T(8,128)(2,1)S(1)} %dynamic-slice_bitcast_fusion), channel_id=1, source_target_pairs={{0,1},{1,0},{2,3},{3,2},{4,5},{5,4},{6,7},{7,6},{8,9},{9,8},{10,11... | collective-permute-start | bytes 884744 | tf_op jit(solution)/shard_map/ppermute | solution.py:432
  38.9 18.1 %backward.1 = (bf16[16,128,192]{2,1,0:T(8,128)(2,1)}, f32[7,8,256]{2,1,0:T(8,128)}) custom-call(bf16[16,128,192]{2,1,0:T(8,128)(2,1)} %bitcast.41, bf16[16,128,192]{2,1,0:T(8,128)(2,1)} %bitcast.44, s32[16,128]{1,0:T(8,128)} %mask.3, f32[7,7,192]{2,1,0:T(8,128)} %kernel.3, f32[22,160,128]{2,1,0:T(8,128)} %get-tuple-element.16.d_rows_a, ...), custom_call_target="tpu_custom_call" | custom-call | tf_op jit(solution)/shard_map/backward/pallas_call | solution.py:521
  57.1 1.6 %collective-permute-start.3 = (bf16[4,144,128]{2,1,0:T(8,128)(2,1)S(1)}, bf16[4,144,128]{2,1,0:T(8,128)(2,1)S(1)}, u32[]{:S(2)}, u32[]{:S(2)}) collective-permute-start(bf16[4,144,128]{2,1,0:T(8,128)(2,1)S(1)} %dynamic-slice_bitcast_fusion.1), channel_id=1, source_target_pairs={{0,4},{4,0},{8,12},{12,8},{16,20},{20,16},{24,28},{28,24},{1,5},{5... | collective-permute-start | bytes 442376 | tf_op jit(solution)/shard_map/ppermute | solution.py:432
  58.7 0.8 add.78
  59.5 1.2 %collective-permute-start.9 = (f32[7,8,256]{2,1,0:T(8,128)S(1)}, f32[7,8,256]{2,1,0:T(8,128)S(1)}, u32[]{:S(2)}, u32[]{:S(2)}) collective-permute-start(f32[7,8,256]{2,1,0:T(8,128)S(1)} %add.78), channel_id=1, source_target_pairs={{0,4},{4,0},{8,12},{12,8},{16,20},{20,16},{24,28},{28,24},{1,5},{5... | collective-permute-start | bytes 172040 | tf_op jit(solution)/shard_map/ppermute | solution.py:432
  60.8 3.9 %collective-permute-done.9 = f32[7,8,256]{2,1,0:T(8,128)S(1)} collective-permute-done((f32[7,8,256]{2,1,0:T(8,128)S(1)}, f32[7,8,256]{2,1,0:T(8,128)S(1)}, u32[]{:S(2)}, u32[]{:S(2)}) %collective-permute-start.9) | collective-permute-done | bytes 57376 | tf_op jit(solution)/shard_map/ppermute | solution.py:432
  64.6 1.6 %collective-permute-start.10 = (f32[7,8,256]{2,1,0:T(8,128)S(1)}, f32[7,8,256]{2,1,0:T(8,128)S(1)}, u32[]{:S(2)}, u32[]{:S(2)}) collective-permute-start(f32[7,8,256]{2,1,0:T(8,128)S(1)} %add.79), channel_id=1, source_target_pairs={{0,8},{4,12},{8,0},{12,4},{16,24},{20,28},{24,16},{28,20},{1,9},{5... | collective-permute-start | bytes 172040 | tf_op jit(solution)/shard_map/ppermute | solution.py:432
  66.3 2.6 %collective-permute-done.10 = f32[7,8,256]{2,1,0:T(8,128)S(1)} collective-permute-done((f32[7,8,256]{2,1,0:T(8,128)S(1)}, f32[7,8,256]{2,1,0:T(8,128)S(1)}, u32[]{:S(2)}, u32[]{:S(2)}) %collective-permute-start.10) | collective-permute-done | bytes 57376 | tf_op jit(solution)/shard_map/ppermute | solution.py:432
  68.9 2.7 %collective-permute-start.11 = (f32[7,8,256]{2,1,0:T(8,128)S(1)}, f32[7,8,256]{2,1,0:T(8,128)S(1)}, u32[]{:S(2)}, u32[]{:S(2)}) collective-permute-start(f32[7,8,256]{2,1,0:T(8,128)S(1)} %add.80), channel_id=1, source_target_pairs={{0,16},{4,20},{8,24},{12,28},{16,0},{20,4},{24,8},{28,12},{1,17},{... | collective-permute-start | bytes 172040 | tf_op jit(solution)/shard_map/ppermute | solution.py:432
  71.6 1.6 %collective-permute-start.4 = (bf16[2,144,128]{2,1,0:T(8,128)(2,1)S(1)}, bf16[2,144,128]{2,1,0:T(8,128)(2,1)S(1)}, u32[]{:S(2)}, u32[]{:S(2)}) collective-permute-start(bf16[2,144,128]{2,1,0:T(8,128)(2,1)S(1)} %dynamic-slice_bitcast_fusion.2), channel_id=1, source_target_pairs={{0,8},{4,12},{8,0},{12,4},{16,24},{20,28},{24,16},{28,20},{1,9},{5... | collective-permute-start | bytes 221192 | tf_op jit(solution)/shard_map/ppermute | solution.py:432
  74.1 1.3 %collective-permute-start.12 = (f32[7,8,256]{2,1,0:T(8,128)S(1)}, f32[7,8,256]{2,1,0:T(8,128)S(1)}, u32[]{:S(2)}, u32[]{:S(2)}) collective-permute-start(f32[7,8,256]{2,1,0:T(8,128)S(1)} %add.81), channel_id=1, source_target_pairs={{0,2},{1,3},{2,0},{3,1},{4,6},{5,7},{6,4},{7,5},{8,10},{9,11},{10,... | collective-permute-start | bytes 172040 | tf_op jit(solution)/shard_map/ppermute | solution.py:432
  75.3 1.2 %copy.32 = bf16[1,16,128,192]{2,3,1,0:T(8,128)(2,1)} copy(bf16[1,16,128,192]{3,2,1,0:T(8,128)(2,1)S(1)} %bitcast.47) | data formatting | bytes 1572864
  76.6 1.2 %copy.33 = bf16[1,16,128,192]{2,3,1,0:T(8,128)(2,1)} copy(bf16[1,16,128,192]{3,2,1,0:T(8,128)(2,1)S(1)} %bitcast.48) | data formatting | bytes 1572864
  78.4 2.7 %collective-permute-start.5 = (bf16[1,144,128]{2,1,0:T(8,128)(2,1)S(1)}, bf16[1,144,128]{2,1,0:T(8,128)(2,1)S(1)}, u32[]{:S(2)}, u32[]{:S(2)}) collective-permute-start(bf16[1,144,128]{2,1,0:T(8,128)(2,1)S(1)} %constant_dynamic-slice_fusion), channel_id=1, source_target_pairs={{0,16},{4,20},{8,24},{12,28},{16,0},{20,4},{24,8},{28,12},{1,17},{... | collective-permute-start | bytes 110600 | tf_op jit(solution)/shard_map/ppermute | solution.py:432
  81.7 1.6 %collective-permute-done.5 = bf16[1,144,128]{2,1,0:T(8,128)(2,1)S(1)} collective-permute-done((bf16[1,144,128]{2,1,0:T(8,128)(2,1)S(1)}, bf16[1,144,128]{2,1,0:T(8,128)(2,1)S(1)}, u32[]{:S(2)}, u32[]{:S(2)}) %collective-permute-start.5) | collective-permute-done | bytes 36896 | tf_op jit(solution)/shard_map/ppermute | solution.py:432
  83.3 1.3 %collective-permute-start.6 = (bf16[144,128]{1,0:T(8,128)(2,1)S(1)}, bf16[144,128]{1,0:T(8,128)(2,1)S(1)}, u32[]{:S(2)}, u32[]{:S(2)}) collective-permute-start(bf16[144,128]{1,0:T(8,128)(2,1)S(1)} %fusion.3), channel_id=1, source_target_pairs={{0,2},{1,3},{2,0},{3,1},{4,6},{5,7},{6,4},{7,5},{8,10},{9,11},{10,... | collective-permute-start | bytes 110600 | tf_op jit(solution)/shard_map/ppermute | solution.py:432
  85.2 2.2 %collective-permute-done.6 = bf16[144,128]{1,0:T(8,128)(2,1)S(1)} collective-permute-done((bf16[144,128]{1,0:T(8,128)(2,1)S(1)}, bf16[144,128]{1,0:T(8,128)(2,1)S(1)}, u32[]{:S(2)}, u32[]{:S(2)}) %collective-permute-start.6) | collective-permute-done | bytes 36896 | tf_op jit(solution)/shard_map/ppermute | solution.py:432
  (65 shorter events, 8.2 us)
Async XLA Ops:
  0.6 1.5 %copy-start.4 = (bf16[1,16,128,192]{2,3,1,0:T(8,128)(2,1)S(1)}, bf16[1,16,128,192]{2,3,1,0:T(8,128)(2,1)}, u32[]{:S(2)}) copy-start(bf16[1,16,128,192]{2,3,1,0:T(8,128)(2,1)} %param.9) | copy-start | bytes 2359300
  0.6 2.1 %copy-start.9 = (s32[16,128]{1,0:T(8,128)S(1)}, s32[16,128]{1,0:T(8,128)}, u32[]{:S(2)}) copy-start(s32[16,128]{1,0:T(8,128)} %mask.3) | copy-start | bytes 24580
  2.2 5.0 %copy-start = (bf16[1,16,128,192]{3,2,1,0:T(8,128)(2,1)}, bf16[1,16,128,192]{3,2,1,0:T(8,128)(2,1)S(1)}, u32[]{:S(2)}) copy-start(bf16[1,16,128,192]{3,2,1,0:T(8,128)(2,1)S(1)} %copy.24) | copy-start | bytes 2359300
  2.2 3.5 %copy-start.10 = (f32[768]{0:T(1024)S(1)}, f32[768]{0:T(1024)}, u32[]{:S(2)}) copy-start(f32[768]{0:T(1024)} %param.14) | copy-start | bytes 9220
  2.2 4.1 %copy-start.6 = (bf16[768,192]{0,1:T(8,128)(2,1)S(1)}, bf16[768,192]{0,1:T(8,128)(2,1)}, u32[]{:S(2)}) copy-start(bf16[768,192]{0,1:T(8,128)(2,1)} %param.15) | copy-start | bytes 884740
  2.8 6.8 %copy-start.1 = (bf16[1,16,128,192]{3,2,1,0:T(8,128)(2,1)}, bf16[1,16,128,192]{3,2,1,0:T(8,128)(2,1)S(1)}, u32[]{:S(2)}) copy-start(bf16[1,16,128,192]{3,2,1,0:T(8,128)(2,1)S(1)} %copy.25) | copy-start | bytes 2359300
  3.2 5.1 %collective-permute-start = (bf16[16,16,192]{2,1,0:T(8,128)(2,1)S(1)}, bf16[16,16,192]{2,1,0:T(8,128)(2,1)S(1)}, u32[]{:S(2)}, u32[]{:S(2)}) collective-permute-start(bf16[16,16,192]{2,1,0:T(8,128)(2,1)S(1)} %pad_maximum_fusion), channel_id=1, source_target_pairs={{0,1},{1,2},{2,3},{3,0},{4,5},{5,6},{6,7},{7,4},{8,9},{9,10},{10,1... | collective-permute-start | bytes 294920 | tf_op jit(solution)/shard_map/ppermute | solution.py:480
  3.7 5.8 %collective-permute-start.1 = (bf16[16,16,192]{2,1,0:T(8,128)(2,1)S(1)}, bf16[16,16,192]{2,1,0:T(8,128)(2,1)S(1)}, u32[]{:S(2)}, u32[]{:S(2)}) collective-permute-start(bf16[16,16,192]{2,1,0:T(8,128)(2,1)S(1)} %pad_maximum_fusion.1), channel_id=1, source_target_pairs={{1,0},{2,1},{3,2},{0,3},{5,4},{6,5},{7,6},{4,7},{9,8},{10,9},{11,1... | collective-permute-start | bytes 294920 | tf_op jit(solution)/shard_map/ppermute | solution.py:481
  8.3 1.2 %copy-start.7 = (bf16[16,16,192]{2,1,0:T(8,128)(2,1)}, bf16[16,16,192]{2,1,0:T(8,128)(2,1)S(1)}, u32[]{:S(2)}) copy-start(bf16[16,16,192]{2,1,0:T(8,128)(2,1)S(1)} %collective-permute-done.halo_before) | copy-start | bytes 294916
  9.5 0.7 copy-start.8
  37.5 19.4 %collective-permute-start.2 = (bf16[1152,128]{1,0:T(8,128)(2,1)S(1)}, bf16[1152,128]{1,0:T(8,128)(2,1)S(1)}, u32[]{:S(2)}, u32[]{:S(2)}) collective-permute-start(bf16[1152,128]{1,0:T(8,128)(2,1)S(1)} %dynamic-slice_bitcast_fusion), channel_id=1, source_target_pairs={{0,1},{1,0},{2,3},{3,2},{4,5},{5,4},{6,7},{7,6},{8,9},{9,8},{10,11... | collective-permute-start | bytes 884744 | tf_op jit(solution)/shard_map/ppermute | solution.py:432
  38.9 18.1 %copy-start.5 = (bf16[2,1152,128]{2,1,0:T(8,128)(2,1)S(1)}, bf16[2,1152,128]{2,1,0:T(8,128)(2,1)}, u32[]{:S(2)}) copy-start(bf16[2,1152,128]{2,1,0:T(8,128)(2,1)} %get-tuple-element.21) | copy-start | bytes 1769476
  56.9 18.4 %copy-start.2 = (bf16[16,128,192]{2,1,0:T(8,128)(2,1)S(1)}, bf16[16,128,192]{2,1,0:T(8,128)(2,1)}, u32[]{:S(2)}) copy-start(bf16[16,128,192]{2,1,0:T(8,128)(2,1)} %get-tuple-element.15) | copy-start | bytes 2359300
  57.0 1.7 %collective-permute-start.8 = (f32[7,8,256]{2,1,0:T(8,128)}, f32[7,8,256]{2,1,0:T(8,128)S(1)}, u32[]{:S(2)}, u32[]{:S(2)}) collective-permute-start(f32[7,8,256]{2,1,0:T(8,128)} %get-tuple-element.22), channel_id=1, source_target_pairs={{0,1},{1,0},{2,3},{3,2},{4,5},{5,4},{6,7},{7,6},{8,9},{9,8},{10,11... | collective-permute-start | bytes 172040 | tf_op jit(solution)/shard_map/ppermute | solution.py:432
  57.1 19.5 %copy-start.3 = (bf16[16,128,192]{2,1,0:T(8,128)(2,1)S(1)}, bf16[16,128,192]{2,1,0:T(8,128)(2,1)}, u32[]{:S(2)}) copy-start(bf16[16,128,192]{2,1,0:T(8,128)(2,1)} %get-tuple-element.20) | copy-start | bytes 2359300
  57.1 14.5 %collective-permute-start.3 = (bf16[4,144,128]{2,1,0:T(8,128)(2,1)S(1)}, bf16[4,144,128]{2,1,0:T(8,128)(2,1)S(1)}, u32[]{:S(2)}, u32[]{:S(2)}) collective-permute-start(bf16[4,144,128]{2,1,0:T(8,128)(2,1)S(1)} %dynamic-slice_bitcast_fusion.1), channel_id=1, source_target_pairs={{0,4},{4,0},{8,12},{12,8},{16,20},{20,16},{24,28},{28,24},{1,5},{5... | collective-permute-start | bytes 442376 | tf_op jit(solution)/shard_map/ppermute | solution.py:432
  59.5 5.1 %collective-permute-start.9 = (f32[7,8,256]{2,1,0:T(8,128)S(1)}, f32[7,8,256]{2,1,0:T(8,128)S(1)}, u32[]{:S(2)}, u32[]{:S(2)}) collective-permute-start(f32[7,8,256]{2,1,0:T(8,128)S(1)} %add.78), channel_id=1, source_target_pairs={{0,4},{4,0},{8,12},{12,8},{16,20},{20,16},{24,28},{28,24},{1,5},{5... | collective-permute-start | bytes 172040 | tf_op jit(solution)/shard_map/ppermute | solution.py:432
  64.6 4.2 %collective-permute-start.10 = (f32[7,8,256]{2,1,0:T(8,128)S(1)}, f32[7,8,256]{2,1,0:T(8,128)S(1)}, u32[]{:S(2)}, u32[]{:S(2)}) collective-permute-start(f32[7,8,256]{2,1,0:T(8,128)S(1)} %add.79), channel_id=1, source_target_pairs={{0,8},{4,12},{8,0},{12,4},{16,24},{20,28},{24,16},{28,20},{1,9},{5... | collective-permute-start | bytes 172040 | tf_op jit(solution)/shard_map/ppermute | solution.py:432
  68.9 5.1 %collective-permute-start.11 = (f32[7,8,256]{2,1,0:T(8,128)S(1)}, f32[7,8,256]{2,1,0:T(8,128)S(1)}, u32[]{:S(2)}, u32[]{:S(2)}) collective-permute-start(f32[7,8,256]{2,1,0:T(8,128)S(1)} %add.80), channel_id=1, source_target_pairs={{0,16},{4,20},{8,24},{12,28},{16,0},{20,4},{24,8},{28,12},{1,17},{... | collective-permute-start | bytes 172040 | tf_op jit(solution)/shard_map/ppermute | solution.py:432
  71.6 6.7 %collective-permute-start.4 = (bf16[2,144,128]{2,1,0:T(8,128)(2,1)S(1)}, bf16[2,144,128]{2,1,0:T(8,128)(2,1)S(1)}, u32[]{:S(2)}, u32[]{:S(2)}) collective-permute-start(bf16[2,144,128]{2,1,0:T(8,128)(2,1)S(1)} %dynamic-slice_bitcast_fusion.2), channel_id=1, source_target_pairs={{0,8},{4,12},{8,0},{12,4},{16,24},{20,28},{24,16},{28,20},{1,9},{5... | collective-permute-start | bytes 221192 | tf_op jit(solution)/shard_map/ppermute | solution.py:432
  74.1 4.2 %collective-permute-start.12 = (f32[7,8,256]{2,1,0:T(8,128)S(1)}, f32[7,8,256]{2,1,0:T(8,128)S(1)}, u32[]{:S(2)}, u32[]{:S(2)}) collective-permute-start(f32[7,8,256]{2,1,0:T(8,128)S(1)} %add.81), channel_id=1, source_target_pairs={{0,2},{1,3},{2,0},{3,1},{4,6},{5,7},{6,4},{7,5},{8,10},{9,11},{10,... | collective-permute-start | bytes 172040 | tf_op jit(solution)/shard_map/ppermute | solution.py:432
  78.4 4.9 %collective-permute-start.5 = (bf16[1,144,128]{2,1,0:T(8,128)(2,1)S(1)}, bf16[1,144,128]{2,1,0:T(8,128)(2,1)S(1)}, u32[]{:S(2)}, u32[]{:S(2)}) collective-permute-start(bf16[1,144,128]{2,1,0:T(8,128)(2,1)S(1)} %constant_dynamic-slice_fusion), channel_id=1, source_target_pairs={{0,16},{4,20},{8,24},{12,28},{16,0},{20,4},{24,8},{28,12},{1,17},{... | collective-permute-start | bytes 110600 | tf_op jit(solution)/shard_map/ppermute | solution.py:432
  83.3 4.0 %collective-permute-start.6 = (bf16[144,128]{1,0:T(8,128)(2,1)S(1)}, bf16[144,128]{1,0:T(8,128)(2,1)S(1)}, u32[]{:S(2)}, u32[]{:S(2)}) collective-permute-start(bf16[144,128]{1,0:T(8,128)(2,1)S(1)} %fusion.3), channel_id=1, source_target_pairs={{0,2},{1,3},{2,0},{3,1},{4,6},{5,7},{6,4},{7,5},{8,10},{9,11},{10,... | collective-permute-start | bytes 110600 | tf_op jit(solution)/shard_map/ppermute | solution.py:432
  87.4 1.3 %collective-permute-start.7 = (bf16[144,128]{1,0:T(8,128)(2,1)S(1)}, bf16[144,128]{1,0:T(8,128)(2,1)S(1)}, u32[]{:S(2)}, u32[]{:S(2)}) collective-permute-start(bf16[144,128]{1,0:T(8,128)(2,1)S(1)} %add_convert_fusion), channel_id=1, source_target_pairs={{0,1},{1,0},{2,3},{3,2},{4,5},{5,4},{6,7},{7,6},{8,9},{9,8},{10,11... | collective-permute-start | bytes 110600 | tf_op jit(solution)/shard_map/ppermute | solution.py:432

commit v2 on v0

v2 whole, which is shorter than its diff:
```python
import functools
import math

import jax
import jax.numpy as jnp
from jax import lax
from jax.experimental import pallas as pl
from jax.experimental.pallas import tpu as pltpu
from jax.sharding import PartitionSpec as P

F32 = jnp.float32
BF16 = jnp.bfloat16
LIMIT = 56 * 2**20
EDGE = 8
GROUP = 16


def dot(lhs, rhs):
    return jnp.dot(lhs, rhs, preferred_element_type=F32)


def dot_t(lhs, rhs):
    return lax.dot_general(lhs, rhs, (((1,), (1,)), ((), ())), preferred_element_type=F32)


def iota(shape, axis):
    return lax.broadcasted_iota(jnp.int32, shape, axis)


def identity(size):
    return jnp.where(iota((size, size), 0) == iota((size, size), 1), 1.0, 0.0).astype(BF16)


def masked_row(array, mask, i):
    return (array[i].astype(F32) * mask[i : i + 1].astype(F32)).astype(BF16)


def group_of(rows, g):
    return jnp.concatenate([row[GROUP * g : GROUP * (g + 1)] for row in rows], axis=0)


def band_mask(i):
    shape = (GROUP, 256)
    lane = iota(shape, 1)
    same = (lane & (GROUP - 1)) == iota(shape, 0)
    return same & (jnp.abs((lane >> 4) - i) <= 3)


def unrolled(count, body):
    for k in range(count):
        body(k)


def build_tiles(lines, rolled, tiles):
    for i in range(16):
        rolled[i] = pltpu.roll(lines[...], ((i - 3) * GROUP) % 256, axis=1)
    masks = [band_mask(i) for i in range(16)]

    def group(g):
        for b in range(7):
            for i in range(16):
                line = rolled[i, 7 * g + b : 7 * g + b + 1, :]
                at = b * 256 + i * GROUP
                tiles[g, at : at + GROUP, :] = jnp.where(masks[i], line, 0.0).astype(BF16)

    unrolled(tiles.shape[0], group)


def pack_shifts(cells, packed, lon, edges):
    near = iota((EDGE, 1), 0) < EDGE // 2

    def group(g):
        for half in range(2):
            source = 2 * g + half
            for b in range(7):
                s = b - 3
                x = cells[source, pl.ds(2 * EDGE + s, lon), :]
                if edges:
                    left = cells[source, pl.ds(EDGE + s, EDGE), :]
                    right = cells[source, pl.ds(2 * EDGE + lon + s, EDGE), :]
                    edge = jnp.where(near, right, left)
                    x = jnp.concatenate([x, edge, edge], axis=0)
                at = b * 256 + half * 128
                packed[g, :, at : at + 128] = x.astype(BF16)

    unrolled(packed.shape[0], group)


def gelu_parts(z):
    cumulative = 0.5 + 0.5 * lax.erf(z * math.sqrt(0.5))
    density = jnp.exp2(z * z * (-0.5 * math.log2(math.e))) * (1.0 / math.sqrt(2.0 * math.pi))
    return cumulative, density


def edge_kernel(fields, cotangent, mask, first, last):
    lat, channels, lon = fields.shape
    groups = channels // GROUP
    row, lane = iota((2 * EDGE, lon), 0), iota((2 * EDGE, lon), 1)
    ends = jnp.where(lane == jnp.where(row < EDGE, row, row + lon - 2 * EDGE), 1.0, 0.0)
    ends = ends.astype(BF16)
    rows = [masked_row(fields, mask, i) for i in range(lat)]
    cells = [dot_t(ends, group_of(rows, g)) for g in range(groups)]
    column, lane = iota((lon, 256), 0), iota((lon, 256), 1)
    column = jnp.where(
        lane < 128,
        jnp.where(column < EDGE, column, -1),
        jnp.where(column >= lon - EDGE, column - (lon - EDGE), -1),
    )
    lane = lane & 127
    total = None
    for i in range(lat):
        place = (column >= 0) & (lane == column + EDGE * i)
        part = dot(masked_row(cotangent, mask, i), jnp.where(place, 1.0, 0.0).astype(BF16))
        total = part if total is None else total + part
    for k, out in enumerate((first, last)):
        for half in range(2):
            at = slice(half * 128, (half + 1) * 128)
            x = [cell[k * EDGE : (k + 1) * EDGE, at] for cell in cells]
            count = groups * EDGE
            out[half * count : (half + 1) * count] = jnp.concatenate(x, axis=0).astype(BF16)
        out[2 * groups * EDGE :] = total[:, k * 128 : (k + 1) * 128].astype(BF16)


def forward_kernel(
    core,
    fields,
    cotangent,
    mask,
    halo_before,
    halo_after,
    lines,
    gain,
    w_in,
    bias,
    w_out,
    output,
    d_conv,
    d_edge,
    keep,
    send,
    sums,
    rolled,
    tiles,
    cells,
    packed,
    conv,
    conv_edge,
    turned_in,
    turned_out,
    gain_columns,
    total_in,
    total_out,
    total_gain,
    shards,
):
    lat, channels, lon = fields.shape
    hidden = w_in.shape[1]
    groups = channels // GROUP
    build_tiles(lines, rolled, tiles)

    gain_row = gain[...].reshape(1, channels)
    gain_columns[...] = jnp.broadcast_to(gain_row, (128, channels)).T
    bias_row = bias[...].reshape(1, hidden)
    bias_columns = jnp.broadcast_to(bias_row, (64, hidden)).T
    lane = iota((hidden, 64), 1)
    high = bias_columns.astype(BF16).astype(F32)
    middle = (bias_columns - high).astype(BF16).astype(F32)
    low = bias_columns - high - middle
    bias_columns = jnp.where(
        lane == 0, high, jnp.where(lane == 1, middle, jnp.where(lane == 2, low, 0.0))
    )
    turned_in[...] = jnp.concatenate([w_in[...].astype(F32).T, bias_columns], axis=1).astype(BF16)
    turned_out[...] = w_out[...].T

    eye = identity(lon)
    before, after = halo_before[...].astype(F32), halo_after[...].astype(F32)
    blank = jnp.zeros((EDGE, 128), F32)
    rows = [masked_row(fields, mask, i) for i in range(lat)]
    for g in range(groups):
        x = dot_t(eye, group_of(rows, g))
        for half in range(2):
            at = half * groups * EDGE + g * EDGE
            cells[2 * g + half] = jnp.concatenate(
                [
                    blank,
                    before[at : at + EDGE],
                    x[:, half * 128 : (half + 1) * 128],
                    after[at : at + EDGE],
                    blank,
                ],
                axis=0,
            )
    pack_shifts(cells, packed, lon, True)

    def band(g):
        y = dot(packed[g], tiles[g])
        conv[g] = y[:lon].T
        conv_edge[g] = y[lon : lon + EDGE]

    unrolled(groups, band)

    total_in[...] = jnp.zeros_like(total_in)
    total_out[...] = jnp.zeros_like(total_out)
    total_gain[...] = jnp.zeros_like(total_gain)

    def block(y, gm, inner):
        cols = y.shape[1]
        gains = jnp.concatenate([gain_columns[...]] * (cols // 128), axis=1)
        y = y - jnp.sum(y, axis=0, keepdims=True) * (1.0 / channels)
        var = jnp.sum(y * y, axis=0, keepdims=True) * (1.0 / channels)
        sigma = lax.rsqrt(var + 1e-6)
        nhat = y * sigma
        normed = (nhat * gains).astype(BF16)
        normed = jnp.concatenate([normed, jnp.ones((64, cols), BF16)], axis=0)
        if inner:
            upright, gm_upright = normed.T, gm.T
        branch, d_normed = None, None
        for h in range(0, hidden, 256):
            at = slice(h, h + 256)
            z = dot(turned_in[at, :], normed)
            cumulative, density = gelu_parts(z)
            d_act = dot(turned_out[at, :], gm)
            d_pre = (d_act * (cumulative + z * density)).astype(BF16)
            part = dot(w_in[:, at], d_pre)
            d_normed = part if d_normed is None else d_normed + part
            if inner:
                act = (z * cumulative).astype(BF16)
                part = dot(w_out[:, at], act)
                branch = part if branch is None else branch + part
                total_in[at, :] += dot(d_pre, upright)
                total_out[at, :] += dot(act, gm_upright)
        prod = d_normed * nhat
        if inner:
            part = prod[:, :128]
            for c in range(128, cols, 128):
                part = part + prod[:, c : c + 128]
            total_gain[...] += part
        d_hat = d_normed * gains
        mean = jnp.sum(d_hat, axis=0, keepdims=True) * (1.0 / channels)
        corr = jnp.sum(prod * gains, axis=0, keepdims=True) * (1.0 / channels)
        return (sigma * (d_hat - mean - nhat * corr)).astype(BF16), branch

    count = 4

    def rows_block(r):
        y, gm, masks = [], [], []
        for k in range(count):
            i = count * r + k
            at = slice(i * GROUP, (i + 1) * GROUP)
            y.append(jnp.concatenate([conv[g, at, :] for g in range(groups)], axis=0))
            m = mask[i : i + 1].astype(F32)
            masks.append(m)
            gm.append((cotangent[i].astype(F32) * m).astype(BF16))
        d, branch = block(jnp.concatenate(y, axis=1), jnp.concatenate(gm, axis=1), True)
        for k in range(count):
            i = count * r + k
            at = slice(k * lon, (k + 1) * lon)
            output[i] = ((fields[i].astype(F32) + branch[:, at]) * masks[k]).astype(BF16)
            d_conv[i] = d[:, at]

    unrolled(lat // count, rows_block)

    lane = iota((1, 128), 1)
    y = []
    for i in range(lat):
        half, k = (i * GROUP) // 128 * 128, i % 8
        line = []
        for tile in range(0, channels, 128):
            x = jnp.zeros((EDGE, 128), F32)
            for g in range(tile // GROUP, min(tile + 128, channels) // GROUP):
                piece = pltpu.roll(conv_edge[g, :, half : half + 128], (g - k) % 8 * GROUP, axis=1)
                x = jnp.where((lane >> 4) == g % 8, piece, x)
            line.append(x)
        y.append(jnp.concatenate(line, axis=1))
    y = jnp.concatenate(y, axis=0).T[:channels]
    at = 2 * groups * EDGE
    gm = jnp.where((lane & (EDGE - 1)) < EDGE // 2, after[at:], before[at:]).astype(BF16)
    d_edge[...], _ = block(y, gm, False)

    first = core[0] == 0
    rows = channels // shards
    sum_in = total_in[...].T
    parts_in, parts_out = [], []
    for n in range(shards):
        mine = sum_in[n * rows : (n + 1) * rows]
        parts_in += [mine[:, c : c + 128] for c in range(0, hidden, 128)]
    rows = hidden // shards
    for n in range(shards):
        mine = total_out[n * rows : (n + 1) * rows]
        parts_out.append(mine[:, :128])
        parts_out.append(
            jnp.concatenate([mine[: rows // 2, 128:], mine[rows // 2 :, 128:]], axis=1)
        )
    parts_in, parts_out = jnp.concatenate(parts_in, axis=0), jnp.concatenate(parts_out, axis=0)
    keep[...] = jnp.where(first, parts_in, parts_out).astype(BF16)
    send[...] = jnp.where(first, parts_out, parts_in).astype(BF16)
    sums[:, :hidden] = sum_in[channels : channels + 8]
    sums[:, hidden:] = jnp.broadcast_to(
        jnp.sum(total_gain[...].T, axis=0, keepdims=True), (8, channels)
    )


def lay_cells(d_conv, d_edge, cells):
    lat, channels, lon = d_conv.shape
    eye = identity(lon)
    rows = [d_conv[i] for i in range(lat)]
    near = iota((EDGE, 1), 0) < EDGE // 2
    lane = iota((1, 128), 1) >> 4
    blank = jnp.zeros((EDGE, 128), F32)
    edges = d_edge[...].astype(F32).T
    for g in range(channels // GROUP):
        x = dot_t(eye, group_of(rows, g))
        tile = (g * GROUP) // 128 * 128
        for half in range(2):
            edge = blank
            for k in range(8):
                i = 8 * half + k
                piece = edges[i * EDGE : (i + 1) * EDGE, tile : min(tile + 128, channels)]
                if piece.shape[1] < 128:
                    piece = jnp.concatenate([piece, piece], axis=1)
                shift = (k * GROUP - (g * GROUP - tile)) % 128
                edge = jnp.where(lane == k, pltpu.roll(piece, shift, axis=1), edge)
            cells[2 * g + half] = jnp.concatenate(
                [
                    blank,
                    jnp.where(near, 0.0, edge),
                    x[:, half * 128 : (half + 1) * 128],
                    jnp.where(near, edge, 0.0),
                    blank,
                ],
                axis=0,
            )


def taps_kernel(core, fields, mask, d_conv, d_edge, sums, keep, send, cells, packed, masked, small):
    lat, channels, lon = fields.shape
    groups = channels // GROUP
    lay_cells(d_conv, d_edge, cells)
    pack_shifts(cells, packed, lon, False)
    rows = [masked_row(fields, mask, i) for i in range(lat)]
    for g in range(groups):
        masked[g] = group_of(rows, g)
    bands = [band_mask(i) for i in range(lat)]
    sub, lane = iota((8, 1), 0), iota((1, 128), 1) >> 4
    small[...] = jnp.zeros_like(small)

    for g in range(groups):
        g_all = dot(masked[g], packed[g])
        taps = jnp.zeros((8, 128), F32)
        for b in range(7):
            total = None
            for i in range(lat):
                part = g_all[i * GROUP : (i + 1) * GROUP, b * 256 : (b + 1) * 256]
                part = jnp.where(bands[i], part, 0.0)
                part = part[:8] + part[8:]
                part = pltpu.roll(part, ((3 - i) * GROUP) % 256, axis=1)[:, :128]
                total = part if total is None else total + part
            total = jnp.sum(total, axis=0, keepdims=True)
            taps = jnp.where(sub == 6 - b, total, taps)
        place = g * GROUP // 128
        for a in range(7):
            shift = (g * GROUP - (6 - a) * GROUP) % 128
            moved = pltpu.roll(taps, shift, axis=1)
            small[a, place] = jnp.where(lane == g % 8, moved, small[a, place])

    line = sums[0:1]
    hidden = line.shape[1] - channels
    pieces = [line[:, c : c + 128] for c in range(0, hidden, 128)]
    pieces.append(line[:, hidden : hidden + 128])
    pieces.append(
        jnp.concatenate([line[:, hidden + 128 :], jnp.zeros((1, 256 - channels), F32)], axis=1)
    )
    for k, piece in enumerate(pieces):
        small[k // 2, k % 2, 7:8] = piece
    flat = small[...].reshape(112, 128)
    first = core[0] == 0
    keep[...] = jnp.where(first, flat[:56], flat[56:])
    send[...] = jnp.where(first, flat[56:], flat[:56])


def spread_kernel(cotangent, mask, lines, d_conv, d_edge, grad_fields, rolled, tiles, cells, packed, spread):
    lat, channels, lon = cotangent.shape
    groups = channels // GROUP
    build_tiles(lines, rolled, tiles)
    lay_cells(d_conv, d_edge, cells)
    pack_shifts(cells, packed, lon, False)

    def band(g):
        spread[g] = dot(packed[g], tiles[g]).T

    unrolled(groups, band)
    for i in range(lat):
        x = jnp.concatenate(
            [spread[g, i * GROUP : (i + 1) * GROUP, :] for g in range(groups)], axis=0
        )
        x = cotangent[i].astype(F32) + x
        grad_fields[i] = (x * mask[i : i + 1].astype(F32)).astype(BF16)


def final_kernel(core, mine, other, small_mine, small_other, grad_in, grad_out, grad_kernel, grad_gain, grad_bias, scale):
    first = core[0] == 0
    mine, other = mine[...].astype(F32) * scale, other[...].astype(F32) * scale
    sum_in, sum_out = jnp.where(first, mine, other), jnp.where(first, other, mine)
    mine, other = small_mine[...] * scale, small_other[...] * scale
    small = jnp.concatenate(
        [jnp.where(first, mine, other), jnp.where(first, other, mine)], axis=0
    )
    rows, hidden = grad_in.shape
    for k in range(hidden // 128):
        grad_in[:, k * 128 : (k + 1) * 128] = sum_in[k * rows : (k + 1) * rows]
    rows, channels = grad_out.shape
    grad_out[:, :128] = sum_out[:rows]
    rest = sum_out[rows:]
    grad_out[:, 128:] = jnp.concatenate([rest[:, :64], rest[:, 64:]], axis=0)
    for a in range(7):
        grad_kernel[a, :, :128] = small[16 * a : 16 * a + 7]
        grad_kernel[a, :, 128:] = small[16 * a + 8 : 16 * a + 15, : channels - 128]
    lines = [small[8 * k + 7 : 8 * k + 8] for k in range(hidden // 128 + 2)]
    grad_bias[...] = jnp.concatenate(lines[:-2], axis=1).reshape(hidden)
    grad_gain[...] = jnp.concatenate([lines[-2], lines[-1][:, : channels - 128]], axis=1).reshape(
        channels
    )


def swapped(x, axis, bit):
    peers = lax.axis_size(axis)
    return lax.ppermute(x, axis, [(i, i ^ bit) for i in range(peers)])


def bits_of(count):
    return [1 << k for k in range(count.bit_length() - 1)]


def pick(x, axis, at):
    return lax.dynamic_index_in_dim(x, at, axis, keepdims=False)


def both(x, y):
    return (x.astype(F32) + y.astype(F32)).astype(BF16)


def halved(mine, bit):
    have = (lax.axis_index("dp") // bit) & 1
    split = mine.reshape(mine.shape[0] // 2, 2, -1, 128)
    kept, sent = pick(split, 1, have), pick(split, 1, 1 - have)
    return kept, sent.reshape(-1, 128)


def two_parts(x):
    high = lax.reduce_precision(x, exponent_bits=8, mantissa_bits=7)
    return jnp.concatenate([high, x - high], axis=0).astype(BF16)


def one_part(x):
    rows = x.shape[0] // 2
    return x[:rows].astype(F32) + x[rows:].astype(F32)


def call(body, name, outs, scratch=(), specs=None):
    extra = {} if specs is None else {"in_specs": specs}
    return pl.pallas_call(
        body,
        out_shape=[jax.ShapeDtypeStruct(shape, dtype) for shape, dtype in outs],
        scratch_shapes=[pltpu.VMEM(shape, dtype) for shape, dtype in scratch],
        compiler_params=pltpu.CompilerParams(vmem_limit_bytes=LIMIT),
        name=name,
        **extra,
    )


def with_core(count):
    vmem = pl.BlockSpec(memory_space=pltpu.VMEM)
    return [pl.BlockSpec(memory_space=pltpu.SMEM)] + [vmem] * count


def lines_of(kernel):
    taps, cols, channels = kernel.shape
    lines = kernel.reshape(taps, cols, channels // GROUP, GROUP).transpose(2, 1, 0, 3)
    lines = lines.reshape(-1, taps * GROUP)
    return jnp.pad(lines, ((0, (-lines.shape[0]) % 8), (0, 256 - lines.shape[1])))


def shapes(lat, channels, lon, hidden, shards):
    groups = channels // GROUP
    rows = channels * hidden // 128
    tiles = [((16, 88, 256), F32), ((groups, 7 * 256, 256), BF16)]
    cells = ((2 * groups, lon + 4 * EDGE, 128), F32)
    wide = ((groups, lon + 2 * EDGE, 7 * 256), BF16)
    packed = ((groups, lon, 7 * 256), BF16)
    field = ((lat, channels, lon), BF16)
    edge = ((channels, 128), BF16)
    return {
        "edges": ([((2 * channels, 128), BF16)] * 2, []),
        "forward": (
            [
                field,
                field,
                edge,
                ((rows, 128), BF16),
                ((rows, 128), BF16),
                ((8, hidden + channels), F32),
            ],
            [
                *tiles,
                cells,
                wide,
                ((groups, 256, lon), F32),
                ((groups, EDGE, 256), F32),
                ((hidden, 256), BF16),
                ((hidden, channels), BF16),
                ((channels, 128), F32),
                ((hidden, 256), F32),
                ((hidden, channels), F32),
                ((channels, 128), F32),
            ],
        ),
        "taps": (
            [((56, 128), F32)] * 2,
            [cells, packed, ((groups, 256, lon), BF16), ((7, 2, 8, 128), F32)],
        ),
        "spread": ([field], [*tiles, cells, packed, ((groups, 256, lon), F32)]),
        "final": (
            [
                ((channels // shards, hidden), F32),
                ((hidden // shards, channels), F32),
                ((7, 7, channels), F32),
                ((channels,), F32),
                ((hidden,), F32),
            ],
            [],
        ),
    }


def per_device(fields, cotangent, land_sea, kernel, ln_gain, weight_in, bias_in, weight_out):
    samples, lat, lon, channels = fields.shape
    hidden = weight_in.shape[1]
    shards, tiles = lax.axis_size("dp"), lax.axis_size("lon")
    core = (lax.axis_index("lon") & 1).reshape(1)
    fields = fields[0].transpose(0, 2, 1)
    cotangent = cotangent[0].transpose(0, 2, 1)
    w_out = weight_out.T
    of = shapes(lat, channels, lon, hidden, shards)

    first, last = call(edge_kernel, "edges", *of["edges"])(fields, cotangent, land_sea)
    up = [(i, (i + 1) % tiles) for i in range(tiles)]
    before = lax.ppermute(last, "lon", up)
    after = lax.ppermute(first, "lon", [(j, i) for i, j in up])
    lines, flipped = lines_of(kernel[::-1]), lines_of(kernel[:, ::-1])

    output, d_conv, d_edge, keep, send, sums = call(
        functools.partial(forward_kernel, shards=shards),
        "forward",
        *of["forward"],
        specs=with_core(10),
    )(core, fields, cotangent, land_sea, before, after, lines, ln_gain, weight_in, bias_in, w_out)

    dp_bits, lon_bits = bits_of(shards), bits_of(tiles)
    mine = both(keep, swapped(send, "lon", 1)).reshape(shards, -1, 128)
    kept, sent = halved(mine, dp_bits[0])
    arrived = swapped(sent, "dp", dp_bits[0])

    small, send = call(taps_kernel, "taps", *of["taps"], specs=with_core(5))(
        core, fields, land_sea, d_conv, d_edge, sums
    )
    small = small + swapped(send, "lon", 1)

    (grad_fields,) = call(spread_kernel, "spread", *of["spread"])(
        cotangent, land_sea, flipped, d_conv, d_edge
    )

    mine = both(kept, arrived.reshape(kept.shape))
    for bit in dp_bits[1:]:
        kept, sent = halved(mine, bit)
        arrived = swapped(jnp.concatenate([sent, two_parts(small)], axis=0), "dp", bit)
        mine = both(kept, arrived[: sent.shape[0]].reshape(kept.shape))
        small = small + one_part(arrived[sent.shape[0] :])
    mine = mine.reshape(-1, 128)
    for bit in lon_bits[1:]:
        arrived = swapped(jnp.concatenate([mine, two_parts(small)], axis=0), "lon", bit)
        small = small + one_part(arrived[mine.shape[0] :])
        mine = both(mine, arrived[: mine.shape[0]])
    small = small + one_part(swapped(two_parts(small), "dp", dp_bits[0]))
    other = swapped(mine, "lon", 1)
    small_other = swapped(small, "lon", 1)

    scale = 1.0 / math.sqrt(samples * lat * lon * shards * tiles)
    grads = call(
        functools.partial(final_kernel, scale=scale), "final", *of["final"], specs=with_core(4)
    )(core, mine, other, small, small_other)
    return (output.transpose(0, 2, 1)[None], grad_fields.transpose(0, 2, 1)[None], *grads)


def solution(mesh):
    placed = (
        P("dp", None, "lon", None),
        P("dp", None, "lon", None),
        P(None, "lon"),
        P(),
        P(),
        P(),
        P(),
        P(),
    )
    return jax.shard_map(
        per_device,
        mesh=mesh,
        in_specs=placed,
        out_specs=(
            P("dp", None, "lon", None),
            P("dp", None, "lon", None),
            P("dp", None),
            P("dp", None),
            P(),
            P(),
            P(),
        ),
        check_vma=False,
    )
```

time: 262 us -> 66.9 us (0.26)
  other arithmetic: 81.7 us -> 0.29 us
  waiting for transfers between devices: 70.4 us -> 18.4 us
  blocking collectives: 40.8 us -> 0 us
  Pallas kernels: 0 us -> 29.1 us
  local copies, waits for them, and re-layouts: 31 us -> 4.51 us
  matrix products: 17.5 us -> 0 us
  between operations: 15.6 us -> 0.89 us
  starting transfers between devices: 4.3 us -> 13.5 us
    reduce_scatter x2 -> x0, waiting for transfers between devices: 61.6 us -> none  [the longest x1 61.6 us: per_device(): lax.psum_scatter(summed_out.astype(jnp.bfloat16), 'dp', scatter_dimension...]
    reduce_sum x7 -> x0, other arithmetic: 47.8 us -> none  [the longest x4 24.6 us: kernel_terms(): cols_out.append(jnp.sum(window * d_float, axis=(0, 1, 2)))]
    psum x1 -> x0, blocking collectives: 40.8 us -> none  [per_device(): lax.psum((part_kernel, part_gain, part_bias), ('dp', 'lon'))]
    pallas_call x0 -> x5, Pallas kernels: none -> 29.1 us  [the longest x1 13.2 us: per_device(): call(functools.partial(forward_kernel, shards=shards), 'forward', *of['fo...]
    convert_element_type x4 -> x5, other arithmetic: 24.1 us -> 0.18 us  [both(): return (x.astype(F32) + y.astype(F32)).astype(BF16)]
    ppermute x4 -> x11, waiting for transfers between devices: 0.01 us -> 18.4 us  [the longest x9 15.9 us: swapped(): return lax.ppermute(x, axis, [(i, i ^ bit) for i in range(peers)])]
    dot_general x6 -> x0, matrix products: 17.5 us -> none  [the longest x1 4.64 us: per_device(): lax.dot_general(grad_flat, weight_out, (((1,), (1,)), ((), ())), preferre...]
    unnamed x258 -> x18, local copies, waits for them, and re-layouts: 16 us -> 2.27 us
  transfers between devices with their start and end apart: 7 -> 11, of which waited for: 2 -> 8; matrix products, arithmetic and copies ran while one was open for 18% -> 3% of each run, Pallas kernels for 0% -> 17%
where the time goes in v2:
time: 66.9 us; the launch traced here: 66.6 us
  Pallas kernels  29.1 us (43%)
  waiting for transfers between devices  18.4 us (28%)
  starting transfers between devices  13.5 us (20%)
  local copies, waits for them, and re-layouts  4.51 us (7%)
  between operations  0.89 us (1%)
    ppermute x9, waiting for transfers between devices, swapped(): return lax.ppermute(x, axis, [(i, i ^ bit) for i in range(peers)])  15.9 us
    pallas_call x1, Pallas kernels, per_device(): call(functools.partial(forward_kernel, shards=shards), 'forward', *of['fo...  13.2 us
    ppermute x9, starting transfers between devices, swapped(): return lax.ppermute(x, axis, [(i, i ^ bit) for i in range(peers)])  11.1 us
    pallas_call x1, Pallas kernels, per_device(): call(taps_kernel, 'taps', *of['taps'], specs=with_core(5))  6.44 us
    pallas_call x1, Pallas kernels, per_device(): call(spread_kernel, 'spread', *of['spread'])  5.08 us
    pallas_call x1, Pallas kernels, per_device(): call(edge_kernel, 'edges', *of['edges'])(fields, cotangent, land_sea)  2.83 us
    unnamed x18, local copies, waits for them, and re-layouts  2.27 us
    ppermute x1, starting transfers between devices, per_device(): after = lax.ppermute(first, 'lon', [(j, i) for i, j in up])  1.92 us
  transfers between devices with their start and end apart: 11, of which 8 were waited for; matrix products, arithmetic and copies ran while one was open for 3% of the time, Pallas kernels for 17%

profile of v2, /device:TPU:0, one launch (start us, length us, event | category | flops | bytes accessed | tf_op | source)
XLA Modules:
  0.0 66.6 jit_solution(8430821179128305938)
XLA Ops:
  0.6 2.8 %edges.1 = (bf16[384,128]{1,0:T(8,128)(2,1)}, bf16[384,128]{1,0:T(8,128)(2,1)}) custom-call(bf16[16,192,128]{2,1,0:T(8,128)(2,1)} %bitcast.42, bf16[16,192,128]{2,1,0:T(8,128)(2,1)} %bitcast.39, s32[16,128]{1,0:T(8,128)} %mask.7), custom_call_target="tpu_custom_call" | custom-call | tf_op jit(solution)/shard_map/edges/pallas_call | solution.py:545
  3.9 1.9 %collective-permute-start.1 = (bf16[384,128]{1,0:T(8,128)(2,1)}, bf16[384,128]{1,0:T(8,128)(2,1)S(1)}, u32[]{:S(2)}, u32[]{:S(2)}) collective-permute-start(bf16[384,128]{1,0:T(8,128)(2,1)} %get-tuple-element.23), channel_id=1, source_target_pairs={{1,0},{2,1},{3,2},{0,3},{5,4},{6,5},{7,6},{4,7},{9,8},{10,9},{11,1... | collective-permute-start | bytes 294920 | tf_op jit(solution)/shard_map/ppermute | solution.py:548
  6.3 0.6 pad.7.lines
  6.9 1.4 %collective-permute-done.halo_before = bf16[384,128]{1,0:T(8,128)(2,1)S(1)} collective-permute-done((bf16[384,128]{1,0:T(8,128)(2,1)}, bf16[384,128]{1,0:T(8,128)(2,1)S(1)}, u32[]{:S(2)}, u32[]{:S(2)}) %collective-permute-start) | collective-permute-done | bytes 98336 | tf_op jit(solution)/shard_map/ppermute | solution.py:547
  8.4 1.0 %collective-permute-done.1.halo_after = bf16[384,128]{1,0:T(8,128)(2,1)S(1)} collective-permute-done((bf16[384,128]{1,0:T(8,128)(2,1)}, bf16[384,128]{1,0:T(8,128)(2,1)S(1)}, u32[]{:S(2)}, u32[]{:S(2)}) %collective-permute-start.1) | collective-permute-done | bytes 98336 | tf_op jit(solution)/shard_map/ppermute | solution.py:548
  9.3 0.6 copy-done.5
  10.0 13.2 %forward.1 = (bf16[16,192,128]{2,1,0:T(8,128)(2,1)}, bf16[16,192,128]{2,1,0:T(8,128)(2,1)}, bf16[192,128]{1,0:T(8,128)(2,1)}, bf16[1152,128]{1,0:T(8,128)(2,1)},...) custom-call(s32[1]{0:T(128)} %bitcast.core, bf16[16,192,128]{2,1,0:T(8,128)(2,1)} %bitcast.43, ...), custom_call_target="tpu_custom_call" | custom-call | tf_op jit(solution)/shard_map/forward/pallas_call | solution.py:551
  23.2 1.4 %collective-permute-start.2 = (bf16[1152,128]{1,0:T(8,128)(2,1)}, bf16[1152,128]{1,0:T(8,128)(2,1)S(1)}, u32[]{:S(2)}, u32[]{:S(2)}) collective-permute-start(bf16[1152,128]{1,0:T(8,128)(2,1)} %get-tuple-element.28), channel_id=1, source_target_pairs={{0,1},{1,0},{2,3},{3,2},{4,5},{5,4},{6,7},{7,6},{8,9},{9,8},{10,11... | collective-permute-start | bytes 884744 | tf_op jit(solution)/shard_map/ppermute | solution.py:427
  24.6 6.4 %taps.1 = (f32[56,128]{1,0:T(8,128)}, f32[56,128]{1,0:T(8,128)}) custom-call(s32[1]{0:T(128)} %bitcast.core, bf16[16,192,128]{2,1,0:T(8,128)(2,1)} %bitcast.44, s32[16,128]{1,0:T(8,128)} %mask.7, bf16[16,192,128]{2,1,0:T(8,128)(2,1)} %get-tuple-element.25.d_conv, bf16[192,128]{1,0:T(8,128)(2,1)} %get-tuple-element.26.d_edge, f32[8,960]{1,0:T(8,128)} %get-tuple-element.29.sums), custom_call_target="tpu_custom_call" | custom-call | tf_op jit(solution)/shard_map/taps/pallas_call | solution.py:563
  31.1 1.4 %collective-permute-done.4 = f32[56,128]{1,0:T(8,128)S(1)} collective-permute-done((f32[56,128]{1,0:T(8,128)}, f32[56,128]{1,0:T(8,128)S(1)}, u32[]{:S(2)}, u32[]{:S(2)}) %collective-permute-start.4) | collective-permute-done | bytes 28704 | tf_op jit(solution)/shard_map/ppermute | solution.py:427
  32.6 1.6 %collective-permute-start.3 = (bf16[576,128]{1,0:T(8,128)(2,1)S(1)}, bf16[576,128]{1,0:T(8,128)(2,1)S(1)}, u32[]{:S(2)}, u32[]{:S(2)}) collective-permute-start(bf16[576,128]{1,0:T(8,128)(2,1)S(1)} %bitcast.54), channel_id=1, source_target_pairs={{0,4},{4,0},{8,12},{12,8},{16,20},{20,16},{24,28},{28,24},{1,5},{5... | collective-permute-start | bytes 442376 | tf_op jit(solution)/shard_map/ppermute | solution.py:427
  34.2 4.4 %collective-permute-done.3 = bf16[576,128]{1,0:T(8,128)(2,1)S(1)} collective-permute-done((bf16[576,128]{1,0:T(8,128)(2,1)S(1)}, bf16[576,128]{1,0:T(8,128)(2,1)S(1)}, u32[]{:S(2)}, u32[]{:S(2)}) %collective-permute-start.3) | collective-permute-done | bytes 147488 | tf_op jit(solution)/shard_map/ppermute | solution.py:427
  38.7 1.6 %collective-permute-start.5 = (bf16[400,128]{1,0:T(8,128)(2,1)S(1)}, bf16[400,128]{1,0:T(8,128)(2,1)S(1)}, u32[]{:S(2)}, u32[]{:S(2)}) collective-permute-start(bf16[400,128]{1,0:T(8,128)(2,1)S(1)} %pad_maximum_fusion), channel_id=1, source_target_pairs={{0,8},{4,12},{8,0},{12,4},{16,24},{20,28},{24,16},{28,20},{1,9},{5... | collective-permute-start | bytes 307208 | tf_op jit(solution)/shard_map/ppermute | solution.py:427
  40.3 3.1 %collective-permute-done.5 = bf16[400,128]{1,0:T(8,128)(2,1)S(1)} collective-permute-done((bf16[400,128]{1,0:T(8,128)(2,1)S(1)}, bf16[400,128]{1,0:T(8,128)(2,1)S(1)}, u32[]{:S(2)}, u32[]{:S(2)}) %collective-permute-start.5) | collective-permute-done | bytes 102432 | tf_op jit(solution)/shard_map/ppermute | solution.py:427
  43.5 2.6 %collective-permute-start.6 = (bf16[256,128]{1,0:T(8,128)(2,1)S(1)}, bf16[256,128]{1,0:T(8,128)(2,1)S(1)}, u32[]{:S(2)}, u32[]{:S(2)}) collective-permute-start(bf16[256,128]{1,0:T(8,128)(2,1)S(1)} %pad_maximum_fusion.1), channel_id=1, source_target_pairs={{0,16},{4,20},{8,24},{12,28},{16,0},{20,4},{24,8},{28,12},{1,17},{... | collective-permute-start | bytes 196616 | tf_op jit(solution)/shard_map/ppermute | solution.py:427
  46.2 2.6 %collective-permute-done.6 = bf16[256,128]{1,0:T(8,128)(2,1)S(1)} collective-permute-done((bf16[256,128]{1,0:T(8,128)(2,1)S(1)}, bf16[256,128]{1,0:T(8,128)(2,1)S(1)}, u32[]{:S(2)}, u32[]{:S(2)}) %collective-permute-start.6) | collective-permute-done | bytes 65568 | tf_op jit(solution)/shard_map/ppermute | solution.py:427
  48.8 2.1 %collective-permute-start.7 = (bf16[256,128]{1,0:T(8,128)(2,1)S(1)}, bf16[256,128]{1,0:T(8,128)(2,1)S(1)}, u32[]{:S(2)}, u32[]{:S(2)}) collective-permute-start(bf16[256,128]{1,0:T(8,128)(2,1)S(1)} %pad_maximum_fusion.2), channel_id=1, source_target_pairs={{0,2},{1,3},{2,0},{3,1},{4,6},{5,7},{6,4},{7,5},{8,10},{9,11},{10,... | collective-permute-start | bytes 196616 | tf_op jit(solution)/shard_map/ppermute | solution.py:427
  50.9 2.3 %collective-permute-done.7 = bf16[256,128]{1,0:T(8,128)(2,1)S(1)} collective-permute-done((bf16[256,128]{1,0:T(8,128)(2,1)S(1)}, bf16[256,128]{1,0:T(8,128)(2,1)S(1)}, u32[]{:S(2)}, u32[]{:S(2)}) %collective-permute-start.7) | collective-permute-done | bytes 65568 | tf_op jit(solution)/shard_map/ppermute | solution.py:427
  53.2 1.6 %collective-permute-start.9 = (bf16[112,128]{1,0:T(8,128)(2,1)S(1)}, bf16[112,128]{1,0:T(8,128)(2,1)S(1)}, u32[]{:S(2)}, u32[]{:S(2)}) collective-permute-start(bf16[112,128]{1,0:T(8,128)(2,1)S(1)} %pad_maximum_fusion.3), channel_id=1, source_target_pairs={{0,4},{4,0},{8,12},{12,8},{16,20},{20,16},{24,28},{28,24},{1,5},{5... | collective-permute-start | bytes 86024 | tf_op jit(solution)/shard_map/ppermute | solution.py:427
  54.9 2.2 %collective-permute-done.9 = bf16[112,128]{1,0:T(8,128)(2,1)S(1)} collective-permute-done((bf16[112,128]{1,0:T(8,128)(2,1)S(1)}, bf16[112,128]{1,0:T(8,128)(2,1)S(1)}, u32[]{:S(2)}, u32[]{:S(2)}) %collective-permute-start.9) | collective-permute-done | bytes 28704 | tf_op jit(solution)/shard_map/ppermute | solution.py:427
  58.2 0.6 pad.8.lines
  58.8 5.1 %spread.1 = bf16[16,192,128]{2,1,0:T(8,128)(2,1)} custom-call(bf16[16,192,128]{2,1,0:T(8,128)(2,1)} %bitcast.41, s32[16,128]{1,0:T(8,128)} %mask.7, f32[88,256]{1,0:T(8,128)} %pad.8.lines, bf16[16,192,128]{2,1,0:T(8,128)(2,1)} %get-tuple-element.25.d_conv, bf16[192,128]{1,0:T(8,128)(2,1)} %get-tuple-element.26.d_edge), custom_call_target="tpu_custom_call" | custom-call | tf_op jit(solution)/shard_map/spread/pallas_call | solution.py:568
  63.9 0.6 copy-done.6
  65.1 1.5 %final.1 = (f32[24,768]{1,0:T(8,128)}, f32[96,192]{1,0:T(8,128)}, f32[7,7,192]{2,1,0:T(8,128)}, f32[192]{0:T(256)}, f32[768]{0:T(1024)}) custom-call(s32[1]{0:T(128)} %bitcast.core, bf16[144,128]{1,0:T(8,128)(2,1)} %copy-done.2, bf16[144,128]{1,0:T(8,128)(2,1)} %copy-done.6, f32[56,128]{1,0:T(8,128)} %copy-done.3, f32[56,128]{1,0:T(8,128)} %copy-done.8), custom_call_target="tpu_custom_call" | custom-call | tf_op jit(solution)/shard_map/final/pallas_call | solution.py:588
  (51 shorter events, 2.9 us)
Async XLA Ops:
  0.6 5.2 %copy-start.1 = (f32[7,7,192]{2,1,0:T(8,128)S(1)}, f32[7,7,192]{2,1,0:T(8,128)}, u32[]{:S(2)}) copy-start(f32[7,7,192]{2,1,0:T(8,128)} %param.11) | copy-start | bytes 112900
  3.5 4.9 %collective-permute-start = (bf16[384,128]{1,0:T(8,128)(2,1)}, bf16[384,128]{1,0:T(8,128)(2,1)S(1)}, u32[]{:S(2)}, u32[]{:S(2)}) collective-permute-start(bf16[384,128]{1,0:T(8,128)(2,1)} %get-tuple-element.22), channel_id=1, source_target_pairs={{0,1},{1,2},{2,3},{3,0},{4,5},{5,6},{6,7},{7,4},{8,9},{9,10},{10,1... | collective-permute-start | bytes 294920 | tf_op jit(solution)/shard_map/ppermute | solution.py:547
  3.9 5.4 %collective-permute-start.1 = (bf16[384,128]{1,0:T(8,128)(2,1)}, bf16[384,128]{1,0:T(8,128)(2,1)S(1)}, u32[]{:S(2)}, u32[]{:S(2)}) collective-permute-start(bf16[384,128]{1,0:T(8,128)(2,1)} %get-tuple-element.23), channel_id=1, source_target_pairs={{1,0},{2,1},{3,2},{0,3},{5,4},{6,5},{7,6},{4,7},{9,8},{10,9},{11,1... | collective-permute-start | bytes 294920 | tf_op jit(solution)/shard_map/ppermute | solution.py:548
  8.4 1.0 %copy-start.4 = (bf16[384,128]{1,0:T(8,128)(2,1)}, bf16[384,128]{1,0:T(8,128)(2,1)S(1)}, u32[]{:S(2)}) copy-start(bf16[384,128]{1,0:T(8,128)(2,1)S(1)} %collective-permute-done.halo_before) | copy-start | bytes 294916
  9.3 0.6 copy-start.5
  23.2 9.3 %collective-permute-start.2 = (bf16[1152,128]{1,0:T(8,128)(2,1)}, bf16[1152,128]{1,0:T(8,128)(2,1)S(1)}, u32[]{:S(2)}, u32[]{:S(2)}) collective-permute-start(bf16[1152,128]{1,0:T(8,128)(2,1)} %get-tuple-element.28), channel_id=1, source_target_pairs={{0,1},{1,0},{2,3},{3,2},{4,5},{5,4},{6,7},{7,6},{8,9},{9,8},{10,11... | collective-permute-start | bytes 884744 | tf_op jit(solution)/shard_map/ppermute | solution.py:427
  24.6 7.9 %copy-start = (bf16[1152,128]{1,0:T(8,128)(2,1)S(1)}, bf16[1152,128]{1,0:T(8,128)(2,1)}, u32[]{:S(2)}) copy-start(bf16[1152,128]{1,0:T(8,128)(2,1)} %get-tuple-element.27) | copy-start | bytes 884740
  31.1 1.4 %collective-permute-start.4 = (f32[56,128]{1,0:T(8,128)}, f32[56,128]{1,0:T(8,128)S(1)}, u32[]{:S(2)}, u32[]{:S(2)}) collective-permute-start(f32[56,128]{1,0:T(8,128)} %get-tuple-element.31), channel_id=1, source_target_pairs={{0,1},{1,0},{2,3},{3,2},{4,5},{5,4},{6,7},{7,6},{8,9},{9,8},{10,11... | collective-permute-start | bytes 86024 | tf_op jit(solution)/shard_map/ppermute | solution.py:427
  31.1 1.4 %copy-start.7 = (f32[56,128]{1,0:T(8,128)S(1)}, f32[56,128]{1,0:T(8,128)}, u32[]{:S(2)}) copy-start(f32[56,128]{1,0:T(8,128)} %get-tuple-element.30) | copy-start | bytes 86020
  32.6 6.0 %collective-permute-start.3 = (bf16[576,128]{1,0:T(8,128)(2,1)S(1)}, bf16[576,128]{1,0:T(8,128)(2,1)S(1)}, u32[]{:S(2)}, u32[]{:S(2)}) collective-permute-start(bf16[576,128]{1,0:T(8,128)(2,1)S(1)} %bitcast.54), channel_id=1, source_target_pairs={{0,4},{4,0},{8,12},{12,8},{16,20},{20,16},{24,28},{28,24},{1,5},{5... | collective-permute-start | bytes 442376 | tf_op jit(solution)/shard_map/ppermute | solution.py:427
  38.7 4.7 %collective-permute-start.5 = (bf16[400,128]{1,0:T(8,128)(2,1)S(1)}, bf16[400,128]{1,0:T(8,128)(2,1)S(1)}, u32[]{:S(2)}, u32[]{:S(2)}) collective-permute-start(bf16[400,128]{1,0:T(8,128)(2,1)S(1)} %pad_maximum_fusion), channel_id=1, source_target_pairs={{0,8},{4,12},{8,0},{12,4},{16,24},{20,28},{24,16},{28,20},{1,9},{5... | collective-permute-start | bytes 307208 | tf_op jit(solution)/shard_map/ppermute | solution.py:427
  43.5 5.2 %collective-permute-start.6 = (bf16[256,128]{1,0:T(8,128)(2,1)S(1)}, bf16[256,128]{1,0:T(8,128)(2,1)S(1)}, u32[]{:S(2)}, u32[]{:S(2)}) collective-permute-start(bf16[256,128]{1,0:T(8,128)(2,1)S(1)} %pad_maximum_fusion.1), channel_id=1, source_target_pairs={{0,16},{4,20},{8,24},{12,28},{16,0},{20,4},{24,8},{28,12},{1,17},{... | collective-permute-start | bytes 196616 | tf_op jit(solution)/shard_map/ppermute | solution.py:427
  48.8 4.3 %collective-permute-start.7 = (bf16[256,128]{1,0:T(8,128)(2,1)S(1)}, bf16[256,128]{1,0:T(8,128)(2,1)S(1)}, u32[]{:S(2)}, u32[]{:S(2)}) collective-permute-start(bf16[256,128]{1,0:T(8,128)(2,1)S(1)} %pad_maximum_fusion.2), channel_id=1, source_target_pairs={{0,2},{1,3},{2,0},{3,1},{4,6},{5,7},{6,4},{7,5},{8,10},{9,11},{10,... | collective-permute-start | bytes 196616 | tf_op jit(solution)/shard_map/ppermute | solution.py:427
  53.2 3.9 %collective-permute-start.9 = (bf16[112,128]{1,0:T(8,128)(2,1)S(1)}, bf16[112,128]{1,0:T(8,128)(2,1)S(1)}, u32[]{:S(2)}, u32[]{:S(2)}) collective-permute-start(bf16[112,128]{1,0:T(8,128)(2,1)S(1)} %pad_maximum_fusion.3), channel_id=1, source_target_pairs={{0,4},{4,0},{8,12},{12,8},{16,20},{20,16},{24,28},{28,24},{1,5},{5... | collective-permute-start | bytes 86024 | tf_op jit(solution)/shard_map/ppermute | solution.py:427
  54.8 2.3 %copy-start.2 = (bf16[144,128]{1,0:T(8,128)(2,1)}, bf16[144,128]{1,0:T(8,128)(2,1)S(1)}, u32[]{:S(2)}) copy-start(bf16[144,128]{1,0:T(8,128)(2,1)S(1)} %add_convert_fusion.1.mine) | copy-start | bytes 110596
  54.8 9.1 %collective-permute-start.8 = (bf16[144,128]{1,0:T(8,128)(2,1)S(1)}, bf16[144,128]{1,0:T(8,128)(2,1)S(1)}, u32[]{:S(2)}, u32[]{:S(2)}) collective-permute-start(bf16[144,128]{1,0:T(8,128)(2,1)S(1)} %add_convert_fusion.1.mine), channel_id=1, source_target_pairs={{0,1},{1,0},{2,3},{3,2},{4,5},{5,4},{6,7},{7,6},{8,9},{9,8},{10,11... | collective-permute-start | bytes 110600 | tf_op jit(solution)/shard_map/ppermute | solution.py:427
  57.1 0.6 copy-start.3
  57.2 6.7 %collective-permute-start.10 = (f32[56,128]{1,0:T(8,128)S(1)}, f32[56,128]{1,0:T(8,128)S(1)}, u32[]{:S(2)}, u32[]{:S(2)}) collective-permute-start(f32[56,128]{1,0:T(8,128)S(1)} %add_add_fusion.small_mine), channel_id=1, source_target_pairs={{0,1},{1,0},{2,3},{3,2},{4,5},{5,4},{6,7},{7,6},{8,9},{9,8},{10,11... | collective-permute-start | bytes 86024 | tf_op jit(solution)/shard_map/ppermute | solution.py:427
  63.9 0.6 copy-start.6
  64.5 0.6 copy-start.8

commit v3 on v2

v3 whole, which is shorter than its diff:
```python
import functools
import math

import jax
import jax.numpy as jnp
from jax import lax
from jax.experimental import pallas as pl
from jax.experimental.pallas import tpu as pltpu
from jax.sharding import PartitionSpec as P

F32 = jnp.float32
BF16 = jnp.bfloat16
EDGE = 8
GROUP = 16


def dot(lhs, rhs):
    return jnp.dot(lhs, rhs, preferred_element_type=F32)


def dot_t(lhs, rhs):
    return lax.dot_general(lhs, rhs, (((1,), (1,)), ((), ())), preferred_element_type=F32)


def iota(shape, axis):
    return lax.broadcasted_iota(jnp.int32, shape, axis)


def identity(size):
    return jnp.where(iota((size, size), 0) == iota((size, size), 1), 1.0, 0.0).astype(BF16)


def masked_row(array, mask, i):
    return (array[i].astype(F32) * mask[i : i + 1].astype(F32)).astype(BF16)


def group_of(rows, g):
    return jnp.concatenate([row[GROUP * g : GROUP * (g + 1)] for row in rows], axis=0)


def band_mask(i):
    shape = (GROUP, 256)
    lane = iota(shape, 1)
    same = (lane & (GROUP - 1)) == iota(shape, 0)
    return same & (jnp.abs((lane >> 4) - i) <= 3)


def unrolled(count, body):
    for k in range(count):
        body(k)


def lay_lines(kernel, lines):
    taps, cols, channels = kernel.shape
    lane = iota((1, 128), 1) >> 4
    zero = jnp.zeros((1, channels), F32)
    rows = [jnp.concatenate([kernel[a], zero], axis=0) for a in range(taps)]
    for g in range(channels // GROUP):
        tile = g * GROUP // 128 * 128
        halves = [jnp.zeros((8, 128), F32)] * 2
        for a in range(taps):
            piece = rows[a][:, tile : min(tile + 128, channels)]
            if piece.shape[1] < 128:
                piece = jnp.concatenate([piece, piece], axis=1)
            for half, slot in ((0, taps - 1 - a), (1, a)):
                moved = pltpu.roll(piece, (slot - g) % 8 * GROUP, axis=1)
                halves[half] = jnp.where(lane == slot, moved, halves[half])
        lines[8 * g : 8 * g + 8] = jnp.concatenate(halves, axis=1)


def build_tiles(lines, rolled, tiles, flip):
    here = iota((1, 256), 1) < 128
    own = jnp.where(here, pltpu.roll(lines[...], 128, axis=1) if flip else lines[...], 0.0)
    for i in range(16):
        rolled[i] = pltpu.roll(own, ((i - 3) * GROUP) % 256, axis=1)
    masks = [band_mask(i) for i in range(16)]

    def group(g):
        for b in range(7):
            for i in range(16):
                k = 8 * g + (6 - b if flip else b)
                line = rolled[i, k : k + 1, :]
                at = b * 256 + i * GROUP
                tiles[g, at : at + GROUP, :] = jnp.where(masks[i], line, 0.0).astype(BF16)

    unrolled(tiles.shape[0], group)


def pack_shifts(cells, packed, lon):
    def group(g):
        for half in range(2):
            for b in range(7):
                x = cells[2 * g + half, 2 * EDGE + b - 3 : 2 * EDGE + b - 3 + lon, :]
                at = b * 256 + half * 128
                packed[g, :, at : at + 128] = x.astype(BF16)

    unrolled(packed.shape[0], group)


BORDER = 24


def pack_borders(before, after, borders, left, right, packed):
    groups = packed.shape[0]
    near = iota((EDGE, 1), 0) < EDGE // 2
    blank = jnp.zeros((EDGE, 128), F32)

    def group(g):
        for half in range(2):
            k = 2 * g + half
            at = half * groups * EDGE + g * EDGE
            halo = slice(at, at + EDGE)
            left[k] = jnp.concatenate([blank, before[halo], borders[k, :BORDER]], axis=0)
            right[k] = jnp.concatenate([borders[k, BORDER:], after[halo], blank], axis=0)
            for b in range(7):
                s = b - 3
                inner = left[k, 2 * EDGE + s : 2 * EDGE + s + 16, :]
                outer = right[k, BORDER - 16 + s : BORDER + s, :]
                beyond = jnp.where(
                    near,
                    right[k, BORDER + s : BORDER + s + EDGE, :],
                    left[k, EDGE + s : 2 * EDGE + s, :],
                )
                x = jnp.concatenate([inner, outer, beyond, beyond], axis=0)
                at = b * 256 + half * 128
                packed[g, :, at : at + 128] = x.astype(BF16)

    unrolled(groups, group)


def gelu_parts(z):
    cumulative = 0.5 + 0.5 * lax.erf(z * math.sqrt(0.5))
    density = jnp.exp2(z * z * (-0.5 * math.log2(math.e))) * (1.0 / math.sqrt(2.0 * math.pi))
    return cumulative, density


def edge_kernel(fields, cotangent, mask, first, last, masked, gm):
    lat, channels, lon = fields.shape
    groups = channels // GROUP
    row, lane = iota((2 * EDGE, lon), 0), iota((2 * EDGE, lon), 1)
    ends = jnp.where(lane == jnp.where(row < EDGE, row, row + lon - 2 * EDGE), 1.0, 0.0)
    ends = ends.astype(BF16)
    rows = [masked_row(fields, mask, i) for i in range(lat)]
    cells = [dot_t(ends, group_of(rows, g)) for g in range(groups)]
    turned = [masked_row(cotangent, mask, i) for i in range(lat)]
    outer = [dot_t(ends, g) for g in turned]
    for i in range(lat):
        masked[i] = rows[i]
        gm[i] = turned[i]
    for k, out in enumerate((first, last)):
        for half in range(2):
            at = slice(half * 128, (half + 1) * 128)
            x = [cell[k * EDGE : (k + 1) * EDGE, at] for cell in cells]
            count = groups * EDGE
            out[half * count : (half + 1) * count] = jnp.concatenate(x, axis=0).astype(BF16)
        g = jnp.concatenate([x[k * EDGE : (k + 1) * EDGE] for x in outer], axis=0)
        out[2 * groups * EDGE :] = g.T.astype(BF16)


def prepare_kernel(
    masked,
    kernel,
    gain,
    w_in,
    bias,
    w_out,
    tiles,
    packed,
    borders,
    turned_in,
    turned_out,
    near_in,
    near_out,
    gain_columns,
    lines,
    rolled,
    cells,
):
    lat, channels, lon = masked.shape
    hidden = w_in.shape[1]
    groups = channels // GROUP
    lay_lines(kernel, lines)
    build_tiles(lines, rolled, tiles, False)
    gain_row = gain[...].reshape(1, channels)
    gain_columns[...] = jnp.broadcast_to(gain_row, (128, channels)).T
    bias_row = bias[...].reshape(1, hidden)
    bias_columns = jnp.broadcast_to(bias_row, (64, hidden)).T
    lane = iota((hidden, 64), 1)
    high = bias_columns.astype(BF16).astype(F32)
    middle = (bias_columns - high).astype(BF16).astype(F32)
    low = bias_columns - high - middle
    bias_columns = jnp.where(
        lane == 0, high, jnp.where(lane == 1, middle, jnp.where(lane == 2, low, 0.0))
    )
    turned_in[...] = jnp.concatenate([w_in[...].astype(F32).T, bias_columns], axis=1).astype(BF16)
    turned_out[...] = w_out[...].T
    near_in[...] = w_in[...]
    near_out[...] = w_out[...]

    rows = [masked[i] for i in range(lat)]
    blank = jnp.zeros((2 * EDGE, 128), F32)
    for g in range(groups):
        x = group_of(rows, g).astype(F32).T
        for half in range(2):
            k = 2 * g + half
            part = x[:, half * 128 : (half + 1) * 128]
            cells[k] = jnp.concatenate([blank, part, blank], axis=0)
            borders[k] = jnp.concatenate([part[:BORDER], part[lon - BORDER :]], axis=0)
    pack_shifts(cells, packed, lon)


def forward_kernel(
    core,
    halo_before,
    halo_after,
    masked,
    gm,
    mask,
    tiles,
    packed,
    borders,
    turned_in,
    turned_out,
    w_in,
    w_out,
    gain_columns,
    output,
    d_conv,
    d_edge,
    keep,
    send,
    sums,
    left,
    right,
    packed_border,
    conv,
    conv_edge,
    total_in,
    total_out,
    total_gain,
    rows_out,
    sent,
    shards,
):
    lat, channels, lon = masked.shape
    hidden = w_in.shape[1]
    groups = channels // GROUP
    before, after = halo_before[...].astype(F32), halo_after[...].astype(F32)
    pack_borders(before, after, borders, left, right, packed_border)

    def band(g):
        border = packed_border[g]
        x = jnp.concatenate([border[:16], packed[g, 16 : lon - 16], border[16:]], axis=0)
        y = dot(x, tiles[g])
        conv[g] = y[:lon].T
        conv_edge[g] = y[lon : lon + EDGE]

    unrolled(groups, band)

    total_in[...] = jnp.zeros_like(total_in)
    total_out[...] = jnp.zeros_like(total_out)
    total_gain[...] = jnp.zeros_like(total_gain)

    def block(y, g, inner):
        cols = y.shape[1]
        gains = jnp.concatenate([gain_columns[...]] * (cols // 128), axis=1)
        y = y - jnp.sum(y, axis=0, keepdims=True) * (1.0 / channels)
        var = jnp.sum(y * y, axis=0, keepdims=True) * (1.0 / channels)
        sigma = lax.rsqrt(var + 1e-6)
        nhat = y * sigma
        normed = (nhat * gains).astype(BF16)
        normed = jnp.concatenate([normed, jnp.ones((64, cols), BF16)], axis=0)
        if inner:
            upright, g_upright = normed.T, g.T
        branch, d_normed = None, None
        for h in range(0, hidden, 256):
            at = slice(h, h + 256)
            z = dot(turned_in[at, :], normed)
            cumulative, density = gelu_parts(z)
            d_act = dot(turned_out[at, :], g)
            d_pre = (d_act * (cumulative + z * density)).astype(BF16)
            part = dot(w_in[:, at], d_pre)
            d_normed = part if d_normed is None else d_normed + part
            if inner:
                act = (z * cumulative).astype(BF16)
                part = dot(w_out[:, at], act)
                branch = part if branch is None else branch + part
                total_in[at, :] += dot(d_pre, upright)
                total_out[at, :] += dot(act, g_upright)
        prod = d_normed * nhat
        if inner:
            part = prod[:, :128]
            for c in range(128, cols, 128):
                part = part + prod[:, c : c + 128]
            total_gain[...] += part
        d_hat = d_normed * gains
        mean = jnp.sum(d_hat, axis=0, keepdims=True) * (1.0 / channels)
        corr = jnp.sum(prod * gains, axis=0, keepdims=True) * (1.0 / channels)
        return (sigma * (d_hat - mean - nhat * corr)).astype(BF16), branch

    count = 4
    copies = []

    def rows_block(r):
        rows = range(count * r, count * (r + 1))
        y = []
        for i in rows:
            at = slice(i * GROUP, (i + 1) * GROUP)
            y.append(jnp.concatenate([conv[g, at, :] for g in range(groups)], axis=0))
        d, branch = block(
            jnp.concatenate(y, axis=1), jnp.concatenate([gm[i] for i in rows], axis=1), True
        )
        for k, i in enumerate(rows):
            at = slice(k * lon, (k + 1) * lon)
            m = mask[i : i + 1].astype(F32)
            rows_out[i] = ((masked[i].astype(F32) + branch[:, at]) * m).astype(BF16)
            d_conv[i] = d[:, at]
        copies.append(
            pltpu.make_async_copy(
                rows_out.at[count * r : count * (r + 1)],
                output.at[count * r : count * (r + 1)],
                sent.at[r],
            )
        )
        copies[-1].start()

    unrolled(lat // count, rows_block)

    lane = iota((1, 128), 1)
    y = []
    for i in range(lat):
        half, k = (i * GROUP) // 128 * 128, i % 8
        line = []
        for tile in range(0, channels, 128):
            x = jnp.zeros((EDGE, 128), F32)
            for g in range(tile // GROUP, min(tile + 128, channels) // GROUP):
                piece = pltpu.roll(conv_edge[g, :, half : half + 128], (g - k) % 8 * GROUP, axis=1)
                x = jnp.where((lane >> 4) == g % 8, piece, x)
            line.append(x)
        y.append(jnp.concatenate(line, axis=1))
    y = jnp.concatenate(y, axis=0).T[:channels]
    at = 2 * groups * EDGE
    g = jnp.where((lane & (EDGE - 1)) < EDGE // 2, after[at:], before[at:]).astype(BF16)
    d_edge[...], _ = block(y, g, False)

    first = core[0] == 0
    rows = channels // shards
    sum_in = total_in[...].T
    parts_in, parts_out = [], []
    for n in range(shards):
        mine = sum_in[n * rows : (n + 1) * rows]
        parts_in += [mine[:, c : c + 128] for c in range(0, hidden, 128)]
    rows = hidden // shards
    for n in range(shards):
        mine = total_out[n * rows : (n + 1) * rows]
        parts_out.append(mine[:, :128])
        parts_out.append(
            jnp.concatenate([mine[: rows // 2, 128:], mine[rows // 2 :, 128:]], axis=1)
        )
    parts_in, parts_out = jnp.concatenate(parts_in, axis=0), jnp.concatenate(parts_out, axis=0)
    keep[...] = jnp.where(first, parts_in, parts_out).astype(BF16)
    send[...] = jnp.where(first, parts_out, parts_in).astype(BF16)
    sums[:, :hidden] = sum_in[channels : channels + 8]
    sums[:, hidden:] = jnp.broadcast_to(
        jnp.sum(total_gain[...].T, axis=0, keepdims=True), (8, channels)
    )
    for copy in copies:
        copy.wait()


def lay_cells(d_conv, d_edge, cells):
    lat, channels, lon = d_conv.shape
    rows = [d_conv[i] for i in range(lat)]
    near = iota((EDGE, 1), 0) < EDGE // 2
    lane = iota((1, 128), 1) >> 4
    blank = jnp.zeros((EDGE, 128), F32)
    edges = d_edge[...].astype(F32).T
    for g in range(channels // GROUP):
        x = group_of(rows, g).astype(F32).T
        tile = (g * GROUP) // 128 * 128
        for half in range(2):
            edge = blank
            for k in range(8):
                i = 8 * half + k
                piece = edges[i * EDGE : (i + 1) * EDGE, tile : min(tile + 128, channels)]
                if piece.shape[1] < 128:
                    piece = jnp.concatenate([piece, piece], axis=1)
                shift = (k * GROUP - (g * GROUP - tile)) % 128
                edge = jnp.where(lane == k, pltpu.roll(piece, shift, axis=1), edge)
            cells[2 * g + half] = jnp.concatenate(
                [
                    blank,
                    jnp.where(near, 0.0, edge),
                    x[:, half * 128 : (half + 1) * 128],
                    jnp.where(near, edge, 0.0),
                    blank,
                ],
                axis=0,
            )


def taps_kernel(core, masked, d_conv, d_edge, sums, keep, send, cells, packed, small):
    lat, channels, lon = masked.shape
    groups = channels // GROUP
    lay_cells(d_conv, d_edge, cells)
    pack_shifts(cells, packed, lon)
    rows = [masked[i] for i in range(lat)]
    bands = [band_mask(i) for i in range(lat)]
    sub, lane = iota((8, 1), 0), iota((1, 128), 1) >> 4
    small[...] = jnp.zeros_like(small)

    for g in range(groups):
        g_all = dot(group_of(rows, g), packed[g])
        taps = jnp.zeros((8, 128), F32)
        for b in range(7):
            total = None
            for i in range(lat):
                part = g_all[i * GROUP : (i + 1) * GROUP, b * 256 : (b + 1) * 256]
                part = jnp.where(bands[i], part, 0.0)
                part = part[:8] + part[8:]
                part = pltpu.roll(part, ((3 - i) * GROUP) % 256, axis=1)[:, :128]
                total = part if total is None else total + part
            total = jnp.sum(total, axis=0, keepdims=True)
            taps = jnp.where(sub == 6 - b, total, taps)
        place = g * GROUP // 128
        for a in range(7):
            shift = (g * GROUP - (6 - a) * GROUP) % 128
            moved = pltpu.roll(taps, shift, axis=1)
            small[a, place] = jnp.where(lane == g % 8, moved, small[a, place])

    line = sums[0:1]
    hidden = line.shape[1] - channels
    pieces = [line[:, c : c + 128] for c in range(0, hidden, 128)]
    pieces.append(line[:, hidden : hidden + 128])
    pieces.append(
        jnp.concatenate([line[:, hidden + 128 :], jnp.zeros((1, 256 - channels), F32)], axis=1)
    )
    for k, piece in enumerate(pieces):
        small[k // 2, k % 2, 7:8] = piece
    flat = small[...].reshape(112, 128)
    first = core[0] == 0
    keep[...] = jnp.where(first, flat[:56], flat[56:])
    send[...] = jnp.where(first, flat[56:], flat[:56])


def spread_kernel(gm, mask, lines, d_conv, d_edge, grad_fields, rolled, tiles, cells, packed, spread):
    lat, channels, lon = gm.shape
    groups = channels // GROUP
    build_tiles(lines, rolled, tiles, True)
    lay_cells(d_conv, d_edge, cells)
    pack_shifts(cells, packed, lon)

    def band(g):
        spread[g] = dot(packed[g], tiles[g]).T

    unrolled(groups, band)
    for i in range(lat):
        x = jnp.concatenate(
            [spread[g, i * GROUP : (i + 1) * GROUP, :] for g in range(groups)], axis=0
        )
        x = gm[i].astype(F32) + x * mask[i : i + 1].astype(F32)
        grad_fields[i] = x.astype(BF16)


def final_kernel(core, mine, other, small_mine, small_other, grad_in, grad_out, grad_kernel, grad_gain, grad_bias, scale):
    first = core[0] == 0
    mine, other = mine[...].astype(F32) * scale, other[...].astype(F32) * scale
    sum_in, sum_out = jnp.where(first, mine, other), jnp.where(first, other, mine)
    mine, other = small_mine[...] * scale, small_other[...] * scale
    small = jnp.concatenate(
        [jnp.where(first, mine, other), jnp.where(first, other, mine)], axis=0
    )
    rows, hidden = grad_in.shape
    for k in range(hidden // 128):
        grad_in[:, k * 128 : (k + 1) * 128] = sum_in[k * rows : (k + 1) * rows]
    rows, channels = grad_out.shape
    grad_out[:, :128] = sum_out[:rows]
    rest = sum_out[rows:]
    grad_out[:, 128:] = jnp.concatenate([rest[:, :64], rest[:, 64:]], axis=0)
    for a in range(7):
        grad_kernel[a, :, :128] = small[16 * a : 16 * a + 7]
        grad_kernel[a, :, 128:] = small[16 * a + 8 : 16 * a + 15, : channels - 128]
    lines = [small[8 * k + 7 : 8 * k + 8] for k in range(hidden // 128 + 2)]
    grad_bias[...] = jnp.concatenate(lines[:-2], axis=1).reshape(hidden)
    grad_gain[...] = jnp.concatenate([lines[-2], lines[-1][:, : channels - 128]], axis=1).reshape(
        channels
    )


def swapped(x, axis, bit):
    peers = lax.axis_size(axis)
    return lax.ppermute(x, axis, [(i, i ^ bit) for i in range(peers)])


def bits_of(count):
    return [1 << k for k in range(count.bit_length() - 1)]


def pick(x, axis, at):
    return lax.dynamic_index_in_dim(x, at, axis, keepdims=False)


def both(x, y):
    return (x.astype(F32) + y.astype(F32)).astype(BF16)


def halved(mine, bit):
    have = (lax.axis_index("dp") // bit) & 1
    split = mine.reshape(mine.shape[0] // 2, 2, -1, 128)
    kept, sent = pick(split, 1, have), pick(split, 1, 1 - have)
    return kept, sent.reshape(-1, 128)


def two_parts(x):
    high = lax.reduce_precision(x, exponent_bits=8, mantissa_bits=7)
    return jnp.concatenate([high, x - high], axis=0).astype(BF16)


def one_part(x):
    rows = x.shape[0] // 2
    return x[:rows].astype(F32) + x[rows:].astype(F32)


HBM, VMEM, SMEM = pltpu.HBM, pltpu.VMEM, pltpu.SMEM


def call(body, name, outs, scratch, megabytes, spaces, out_spaces):
    def held(space, shape, dtype):
        return VMEM(shape, dtype) if space is VMEM else jax.ShapeDtypeStruct(shape, dtype)

    def spec(space):
        return pl.BlockSpec(memory_space={SMEM: SMEM, pl.ANY: pl.ANY}.get(space, VMEM))

    kernel = pl.pallas_call(
        body,
        out_shape=[held(space, *out) for space, out in zip(out_spaces, outs, strict=True)],
        in_specs=[spec(space) for space in spaces],
        out_specs=[spec(space) for space in out_spaces],
        scratch_shapes=[x if not isinstance(x, tuple) else VMEM(*x) for x in scratch],
        compiler_params=pltpu.CompilerParams(vmem_limit_bytes=megabytes * 2**20),
        name=name,
    )

    def run(*args):
        return kernel(
            *[
                pltpu.with_memory_space_constraint(x, space) if space in (HBM, VMEM) else x
                for x, space in zip(args, spaces, strict=True)
            ]
        )

    return run


def per_device(fields, cotangent, land_sea, kernel, ln_gain, weight_in, bias_in, weight_out):
    samples, lat, lon, channels = fields.shape
    hidden = weight_in.shape[1]
    shards, tiles = lax.axis_size("dp"), lax.axis_size("lon")
    groups = channels // GROUP
    rows = channels * hidden // 128
    core = (lax.axis_index("lon") & 1).reshape(1)
    fields = fields[0].transpose(0, 2, 1)
    cotangent = cotangent[0].transpose(0, 2, 1)
    w_out = weight_out.T

    field = ((lat, channels, lon), BF16)
    halo = ((2 * channels, 128), BF16)
    edge = ((channels, 128), BF16)
    rolled = ((16, 8 * groups, 256), F32)
    tile = ((groups, 7 * 256, 256), BF16)
    cells = ((2 * groups, lon + 4 * EDGE, 128), F32)
    packed = ((groups, lon, 7 * 256), BF16)
    border = ((2 * groups, 2 * EDGE + BORDER, 128), F32)
    held = ((groups, 256, lon), F32)

    first, last, masked, gm = call(
        edge_kernel, "edges", [halo, halo, field, field], [], 8, [HBM] * 3, [None, None, VMEM, VMEM]
    )(fields, cotangent, land_sea)
    up = [(i, (i + 1) % tiles) for i in range(tiles)]
    before = lax.ppermute(last, "lon", up)
    after = lax.ppermute(first, "lon", [(j, i) for i, j in up])

    ready = call(
        prepare_kernel,
        "prepare",
        [
            tile,
            packed,
            ((2 * groups, 2 * BORDER, 128), F32),
            ((hidden, 256), BF16),
            ((hidden, channels), BF16),
            ((channels, hidden), BF16),
            ((channels, hidden), BF16),
            ((channels, 128), F32),
            ((8 * groups, 256), F32),
        ],
        [rolled, cells],
        16,
        [VMEM] + [HBM] * 5,
        [VMEM] * 9,
    )(masked, kernel, ln_gain, weight_in, bias_in, w_out)
    lines = ready[-1]

    output, d_conv, d_edge, keep, send, sums = call(
        functools.partial(forward_kernel, shards=shards),
        "forward",
        [
            field,
            field,
            edge,
            ((rows, 128), BF16),
            ((rows, 128), BF16),
            ((8, hidden + channels), F32),
        ],
        [
            border,
            border,
            ((groups, 48, 7 * 256), BF16),
            held,
            ((groups, EDGE, 256), F32),
            ((hidden, 256), F32),
            ((hidden, channels), F32),
            ((channels, 128), F32),
            field,
            pltpu.SemaphoreType.DMA((lat // 4,)),
        ],
        20,
        [SMEM, HBM, HBM, VMEM, VMEM, HBM] + [VMEM] * 8,
        [pl.ANY] + [VMEM] * 2 + [None] * 2 + [VMEM],
    )(core, before, after, masked, gm, land_sea, *ready[:-1])

    dp_bits, lon_bits = bits_of(shards), bits_of(tiles)
    arrived = swapped(send, "lon", 1)
    small, send = call(
        taps_kernel,
        "taps",
        [((56, 128), F32)] * 2,
        [cells, packed, ((7, 2, 8, 128), F32)],
        20,
        [SMEM] + [VMEM] * 4,
        [None] * 2,
    )(core, masked, d_conv, d_edge, sums)
    small = small + swapped(send, "lon", 1)
    mine = both(keep, arrived).reshape(shards, -1, 128)
    for bit in dp_bits:
        kept, sent = halved(mine, bit)
        sent = jnp.concatenate([sent, two_parts(small)], axis=0)
        if bit == 1:
            sent, d_conv = lax.optimization_barrier((sent, d_conv))
        arrived = swapped(sent, "dp", bit)
        if bit == 1:
            (grad_fields,) = call(
                spread_kernel,
                "spread",
                [field],
                [rolled, tile, cells, packed, held],
                32,
                [VMEM, HBM] + [VMEM] * 3,
                [None],
            )(gm, land_sea, lines, d_conv, d_edge)
            arrived, grad_fields = lax.optimization_barrier((arrived, grad_fields))
        count = kept.size // 128
        mine = both(kept, arrived[:count].reshape(kept.shape))
        small = small + one_part(arrived[count:])
    mine = mine.reshape(-1, 128)
    for bit in lon_bits[1:]:
        arrived = swapped(jnp.concatenate([mine, two_parts(small)], axis=0), "lon", bit)
        small = small + one_part(arrived[mine.shape[0] :])
        mine = both(mine, arrived[: mine.shape[0]])
    other = swapped(mine, "lon", 1)
    small_other = swapped(small, "lon", 1)

    scale = 1.0 / math.sqrt(samples * lat * lon * shards * tiles)
    grads = call(
        functools.partial(final_kernel, scale=scale),
        "final",
        [
            ((channels // shards, hidden), F32),
            ((hidden // shards, channels), F32),
            ((7, 7, channels), F32),
            ((channels,), F32),
            ((hidden,), F32),
        ],
        [],
        8,
        [SMEM] + [None] * 4,
        [None] * 5,
    )(core, mine, other, small, small_other)
    return (output.transpose(0, 2, 1)[None], grad_fields.transpose(0, 2, 1)[None], *grads)


def solution(mesh):
    placed = (
        P("dp", None, "lon", None),
        P("dp", None, "lon", None),
        P(None, "lon"),
        P(),
        P(),
        P(),
        P(),
        P(),
    )
    return jax.shard_map(
        per_device,
        mesh=mesh,
        in_specs=placed,
        out_specs=(
            P("dp", None, "lon", None),
            P("dp", None, "lon", None),
            P("dp", None),
            P("dp", None),
            P(),
            P(),
            P(),
        ),
        check_vma=False,
    )
```

time: 66.9 us -> 52.5 us (0.78)
  waiting for transfers between devices: 18.4 us -> 10.9 us
  local copies, waits for them, and re-layouts: 4.51 us -> 0.72 us
  Pallas kernels: 29.1 us -> 27.3 us
  starting transfers between devices: 13.5 us -> 12.3 us
    ppermute x9 -> x8, waiting for transfers between devices: 15.9 us -> 10.9 us  [swapped(): return lax.ppermute(x, axis, [(i, i ^ bit) for i in range(peers)])]
    pallas_call x5 -> x6, Pallas kernels: 29.1 us -> 27.3 us  [run(): kernel(*[pltpu.with_memory_space_constraint(x, space) if space in (HBM, V...]
    unnamed x18 -> x4, local copies, waits for them, and re-layouts: 2.27 us -> 0.65 us
    ppermute x1, waiting for transfers between devices: 1.43 us -> 0.01 us  [per_device(): before = lax.ppermute(last, 'lon', up)]
    ppermute x9 -> x8, starting transfers between devices: 11.1 us -> 9.76 us  [swapped(): return lax.ppermute(x, axis, [(i, i ^ bit) for i in range(peers)])]
    pad x2 -> x0, local copies, waits for them, and re-layouts: 1.29 us -> none  [lines_of(): return jnp.pad(lines, ((0, -lines.shape[0] % 8), (0, 256 - lines.shape[1])))]
    ppermute x1, waiting for transfers between devices: 0.98 us -> 0.01 us  [per_device(): after = lax.ppermute(first, 'lon', [(j, i) for i, j in up])]
  transfers between devices with their start and end apart: 11 -> 10, of which waited for: 8 -> 7; matrix products, arithmetic and copies ran while one was open for 3% -> 0% of each run, Pallas kernels for 17% -> 16%
where the time goes in v3:
time: 52.5 us; the launch traced here: 52.3 us
  Pallas kernels  27.3 us (52%)
  starting transfers between devices  12.3 us (23%)
  waiting for transfers between devices  10.9 us (21%)
  between operations  0.83 us (2%)
  local copies, waits for them, and re-layouts  0.72 us (1%)
    pallas_call x6, Pallas kernels, run(): kernel(*[pltpu.with_memory_space_constraint(x, space) if space in (HBM, V...  27.3 us
    ppermute x8, waiting for transfers between devices, swapped(): return lax.ppermute(x, axis, [(i, i ^ bit) for i in range(peers)])  10.9 us
    ppermute x8, starting transfers between devices, swapped(): return lax.ppermute(x, axis, [(i, i ^ bit) for i in range(peers)])  9.76 us
    ppermute x1, starting transfers between devices, per_device(): after = lax.ppermute(first, 'lon', [(j, i) for i, j in up])  1.99 us
  transfers between devices with their start and end apart: 10, of which 7 were waited for; matrix products, arithmetic and copies ran while one was open for 0% of the time, Pallas kernels for 16%

profile of v3, /device:TPU:0, one launch (start us, length us, event | category | flops | bytes accessed | tf_op | source)
XLA Modules:
  0.0 52.3 jit_solution(5626482828573914183)
XLA Ops:
  0.6 2.2 %edges.1 = (bf16[384,128]{1,0:T(8,128)(2,1)S(1)}, bf16[384,128]{1,0:T(8,128)(2,1)S(1)}, bf16[16,192,128]{2,1,0:T(8,128)(2,1)S(1)}, bf16[16,192,128]{2,1,0:T(8,128)(2,1)S(1)}) custom-call(bf16[16,192,128]{2,1,0:T(8,128)(2,1)} %bitcast.41, bf16[16,192,128]{2,1,0:T(8,128)(2,1)} %bitcast.42, s32[16,128]{1,0:T(8,128)} %mask.5), custom_call_target="tpu_custom_call" | custom-call | tf_op jit(solution)/shard_map/edges/pallas_call | solution.py:545
  2.8 0.5 collective-permute-start
  3.3 2.0 %collective-permute-start.1 = (bf16[384,128]{1,0:T(8,128)(2,1)S(1)}, bf16[384,128]{1,0:T(8,128)(2,1)S(1)}, u32[]{:S(2)}, u32[]{:S(2)}) collective-permute-start(bf16[384,128]{1,0:T(8,128)(2,1)S(1)} %get-tuple-element.38), channel_id=1, source_target_pairs={{1,0},{2,1},{3,2},{0,3},{5,4},{6,5},{7,6},{4,7},{9,8},{10,9},{11,1... | collective-permute-start | bytes 294920 | tf_op jit(solution)/shard_map/ppermute | solution.py:581
  5.3 4.2 %prepare.1 = (bf16[12,1792,256]{2,1,0:T(8,128)(2,1)S(1)}, bf16[12,128,1792]{2,1,0:T(8,128)(2,1)S(1)}, f32[24,48,128]{2,1,0:T(8,128)S(1)}, bf16[768,256]{1,0:T(8,...) custom-call(bf16[16,192,128]{2,1,0:T(8,128)(2,1)S(1)} %get-tuple-ele, ...), custom_call_target="tpu_custom_call" | custom-call | tf_op jit(solution)/shard_map/prepare/pallas_call | solution.py:545
  9.6 0.6 %copy-done = bf16[384,128]{1,0:T(8,128)(2,1)} copy-done((bf16[384,128]{1,0:T(8,128)(2,1)}, bf16[384,128]{1,0:T(8,128)(2,1)S(1)}, u32[]{:S(2)}) %copy-start) | copy-done | bytes 98328
  10.2 11.4 %forward.1 = (bf16[16,192,128]{2,1,0:T(8,128)(2,1)}, bf16[16,192,128]{2,1,0:T(8,128)(2,1)S(1)}, bf16[192,128]{1,0:T(8,128)(2,1)S(1)}, bf16[1152,128]{1,0:T(8,128...) custom-call(s32[1]{0:T(128)} %bitcast.core, bf16[384,128]{1,0:T(8,128)(2,1)} %copy-done, ...), custom_call_target="tpu_custom_call" | custom-call | tf_op jit(solution)/shard_map/forward/pallas_call | solution.py:545
  21.6 4.6 %taps.1 = (f32[56,128]{1,0:T(8,128)S(1)}, f32[56,128]{1,0:T(8,128)S(1)}) custom-call(s32[1]{0:T(128)} %bitcast.core, bf16[16,192,128]{2,1,0:T(8,128)(2,1)S(1)} %get-tuple-element.39.masked, bf16[16,192,128]{2,1,0:T(8,128)(2,1)S(1)} %get-tuple-element.59.d_conv, bf16[192,128]{1,0:T(8,128)(2,1)S(1)} %get-tuple-element.53.d_edge, ...), custom_call_target="tpu_custom_call" | custom-call | tf_op jit(solution)/shard_map/taps/pallas_call | solution.py:545
  26.2 0.7 %collective-permute-start.3 = (f32[56,128]{1,0:T(8,128)S(1)}, f32[56,128]{1,0:T(8,128)S(1)}, u32[]{:S(2)}, u32[]{:S(2)}) collective-permute-start(f32[56,128]{1,0:T(8,128)S(1)} %get-tuple-element.56), channel_id=1, source_target_pairs={{0,1},{1,0},{2,3},{3,2},{4,5},{5,4},{6,7},{7,6},{8,9},{9,8},{10,11... | collective-permute-start | bytes 86024 | tf_op jit(solution)/shard_map/ppermute | solution.py:492
  26.8 0.1 collective-permute-start.2
  26.9 0.8 %collective-permute-done.3 = f32[56,128]{1,0:T(8,128)S(1)} collective-permute-done((f32[56,128]{1,0:T(8,128)S(1)}, f32[56,128]{1,0:T(8,128)S(1)}, u32[]{:S(2)}, u32[]{:S(2)}) %collective-permute-start.3) | collective-permute-done | bytes 28704 | tf_op jit(solution)/shard_map/ppermute | solution.py:492
  27.7 0.7 %collective-permute-done.2 = bf16[1152,128]{1,0:T(8,128)(2,1)S(1)} collective-permute-done((bf16[1152,128]{1,0:T(8,128)(2,1)S(1)}, bf16[1152,128]{1,0:T(8,128)(2,1)S(1)}, u32[]{:S(2)}, u32[]{:S(2)}) %collective-permute-start.2) | collective-permute-done | bytes 294944 | tf_op jit(solution)/shard_map/ppermute | solution.py:492
  28.4 0.1 add_convert_fusion
  28.6 1.9 %collective-permute-start.4 = (bf16[688,128]{1,0:T(8,128)(2,1)S(1)}, bf16[688,128]{1,0:T(8,128)(2,1)S(1)}, u32[]{:S(2)}, u32[]{:S(2)}) collective-permute-start(bf16[688,128]{1,0:T(8,128)(2,1)S(1)} %pad_maximum_fusion), channel_id=1, source_target_pairs={{0,4},{4,0},{8,12},{12,8},{16,20},{20,16},{24,28},{28,24},{1,5},{5... | collective-permute-start | bytes 528392 | tf_op jit(solution)/shard_map/ppermute | solution.py:492
  30.4 4.2 %spread.1 = bf16[16,192,128]{2,1,0:T(8,128)(2,1)} custom-call(bf16[16,192,128]{2,1,0:T(8,128)(2,1)S(1)} %get-tuple-element.40.gm, s32[16,128]{1,0:T(8,128)} %mask.5, f32[96,256]{1,0:T(8,128)S(1)} %get-tuple-element.58.lines, bf16[16,192,128]{2,1,0:T(8,128)(2,1)S(1)} %get-tuple-element.59.d_conv, bf16[192,128]{1,0:T(8,128)(2,1)S(1)} %get-tuple-element.53.d_edge), custom_call_target="tpu_custom_call" | custom-call | tf_op jit(solution)/shard_map/spread/pallas_call | solution.py:545
  34.7 0.8 %collective-permute-done.4 = bf16[688,128]{1,0:T(8,128)(2,1)S(1)} collective-permute-done((bf16[688,128]{1,0:T(8,128)(2,1)S(1)}, bf16[688,128]{1,0:T(8,128)(2,1)S(1)}, u32[]{:S(2)}, u32[]{:S(2)}) %collective-permute-start.4) | collective-permute-done | bytes 176160 | tf_op jit(solution)/shard_map/ppermute | solution.py:492
  35.6 1.9 %collective-permute-start.5 = (bf16[400,128]{1,0:T(8,128)(2,1)S(1)}, bf16[400,128]{1,0:T(8,128)(2,1)S(1)}, u32[]{:S(2)}, u32[]{:S(2)}) collective-permute-start(bf16[400,128]{1,0:T(8,128)(2,1)S(1)} %pad_maximum_fusion.1), channel_id=1, source_target_pairs={{0,8},{4,12},{8,0},{12,4},{16,24},{20,28},{24,16},{28,20},{1,9},{5... | collective-permute-start | bytes 307208 | tf_op jit(solution)/shard_map/ppermute | solution.py:492
  37.4 2.9 %collective-permute-done.5 = bf16[400,128]{1,0:T(8,128)(2,1)S(1)} collective-permute-done((bf16[400,128]{1,0:T(8,128)(2,1)S(1)}, bf16[400,128]{1,0:T(8,128)(2,1)S(1)}, u32[]{:S(2)}, u32[]{:S(2)}) %collective-permute-start.5) | collective-permute-done | bytes 102432 | tf_op jit(solution)/shard_map/ppermute | solution.py:492
  40.4 2.9 %collective-permute-start.6 = (bf16[256,128]{1,0:T(8,128)(2,1)S(1)}, bf16[256,128]{1,0:T(8,128)(2,1)S(1)}, u32[]{:S(2)}, u32[]{:S(2)}) collective-permute-start(bf16[256,128]{1,0:T(8,128)(2,1)S(1)} %pad_maximum_fusion.2), channel_id=1, source_target_pairs={{0,16},{4,20},{8,24},{12,28},{16,0},{20,4},{24,8},{28,12},{1,17},{... | collective-permute-start | bytes 196616 | tf_op jit(solution)/shard_map/ppermute | solution.py:492
  43.3 2.4 %collective-permute-done.6 = bf16[256,128]{1,0:T(8,128)(2,1)S(1)} collective-permute-done((bf16[256,128]{1,0:T(8,128)(2,1)S(1)}, bf16[256,128]{1,0:T(8,128)(2,1)S(1)}, u32[]{:S(2)}, u32[]{:S(2)}) %collective-permute-start.6) | collective-permute-done | bytes 65568 | tf_op jit(solution)/shard_map/ppermute | solution.py:492
  45.7 1.8 %collective-permute-start.7 = (bf16[256,128]{1,0:T(8,128)(2,1)S(1)}, bf16[256,128]{1,0:T(8,128)(2,1)S(1)}, u32[]{:S(2)}, u32[]{:S(2)}) collective-permute-start(bf16[256,128]{1,0:T(8,128)(2,1)S(1)} %pad_maximum_fusion.3), channel_id=1, source_target_pairs={{0,2},{1,3},{2,0},{3,1},{4,6},{5,7},{6,4},{7,5},{8,10},{9,11},{10,... | collective-permute-start | bytes 196616 | tf_op jit(solution)/shard_map/ppermute | solution.py:492
  47.5 2.6 %collective-permute-done.7 = bf16[256,128]{1,0:T(8,128)(2,1)S(1)} collective-permute-done((bf16[256,128]{1,0:T(8,128)(2,1)S(1)}, bf16[256,128]{1,0:T(8,128)(2,1)S(1)}, u32[]{:S(2)}, u32[]{:S(2)}) %collective-permute-start.7) | collective-permute-done | bytes 65568 | tf_op jit(solution)/shard_map/ppermute | solution.py:492
  50.1 0.6 %collective-permute-start.9 = (f32[56,128]{1,0:T(8,128)S(1)}, f32[56,128]{1,0:T(8,128)S(1)}, u32[]{:S(2)}, u32[]{:S(2)}) collective-permute-start(f32[56,128]{1,0:T(8,128)S(1)} %add_add_fusion.small_mine), channel_id=1, source_target_pairs={{0,1},{1,0},{2,3},{3,2},{4,5},{5,4},{6,7},{7,6},{8,9},{9,8},{10,11... | collective-permute-start | bytes 86024 | tf_op jit(solution)/shard_map/ppermute | solution.py:492
  50.7 0.9 %collective-permute-done.9.small_other = f32[56,128]{1,0:T(8,128)S(1)} collective-permute-done((f32[56,128]{1,0:T(8,128)S(1)}, f32[56,128]{1,0:T(8,128)S(1)}, u32[]{:S(2)}, u32[]{:S(2)}) %collective-permute-start.9) | collective-permute-done | bytes 28704 | tf_op jit(solution)/shard_map/ppermute | solution.py:492
  51.5 0.7 %final.1 = (f32[24,768]{1,0:T(8,128)}, f32[96,192]{1,0:T(8,128)}, f32[7,7,192]{2,1,0:T(8,128)}, f32[192]{0:T(256)}, f32[768]{0:T(1024)}) custom-call(s32[1]{0:T(128)} %bitcast.core, bf16[144,128]{1,0:T(8,128)(2,1)S(1)} %add_convert_fusion.1.mine, bf16[144,128]{1,0:T(8,128)(2,1)S(1)} %collective-permute-done.8.other, f32[56,128]{1,0:T(8,128)S(1)} %add_add_fusion.small_mine, ...), custom_call_target="tpu_custom_call" | custom-call | tf_op jit(solution)/shard_map/final/pallas_call | solution.py:545
  (27 shorter events, 0.4 us)
Async XLA Ops:
  2.8 6.7 %collective-permute-start = (bf16[384,128]{1,0:T(8,128)(2,1)S(1)}, bf16[384,128]{1,0:T(8,128)(2,1)S(1)}, u32[]{:S(2)}, u32[]{:S(2)}) collective-permute-start(bf16[384,128]{1,0:T(8,128)(2,1)S(1)} %get-tuple-element.37), channel_id=1, source_target_pairs={{0,1},{1,2},{2,3},{3,0},{4,5},{5,6},{6,7},{7,4},{8,9},{9,10},{10,1... | collective-permute-start | bytes 294920 | tf_op jit(solution)/shard_map/ppermute | solution.py:580
  3.3 6.2 %collective-permute-start.1 = (bf16[384,128]{1,0:T(8,128)(2,1)S(1)}, bf16[384,128]{1,0:T(8,128)(2,1)S(1)}, u32[]{:S(2)}, u32[]{:S(2)}) collective-permute-start(bf16[384,128]{1,0:T(8,128)(2,1)S(1)} %get-tuple-element.38), channel_id=1, source_target_pairs={{1,0},{2,1},{3,2},{0,3},{5,4},{6,5},{7,6},{4,7},{9,8},{10,9},{11,1... | collective-permute-start | bytes 294920 | tf_op jit(solution)/shard_map/ppermute | solution.py:581
  9.5 0.6 %copy-start = (bf16[384,128]{1,0:T(8,128)(2,1)}, bf16[384,128]{1,0:T(8,128)(2,1)S(1)}, u32[]{:S(2)}) copy-start(bf16[384,128]{1,0:T(8,128)(2,1)S(1)} %collective-permute-done.halo_before) | copy-start | bytes 294916
  9.5 0.7 %copy-start.1 = (bf16[384,128]{1,0:T(8,128)(2,1)}, bf16[384,128]{1,0:T(8,128)(2,1)S(1)}, u32[]{:S(2)}) copy-start(bf16[384,128]{1,0:T(8,128)(2,1)S(1)} %collective-permute-done.1.halo_after) | copy-start | bytes 294916
  26.2 1.5 %collective-permute-start.3 = (f32[56,128]{1,0:T(8,128)S(1)}, f32[56,128]{1,0:T(8,128)S(1)}, u32[]{:S(2)}, u32[]{:S(2)}) collective-permute-start(f32[56,128]{1,0:T(8,128)S(1)} %get-tuple-element.56), channel_id=1, source_target_pairs={{0,1},{1,0},{2,3},{3,2},{4,5},{5,4},{6,7},{7,6},{8,9},{9,8},{10,11... | collective-permute-start | bytes 86024 | tf_op jit(solution)/shard_map/ppermute | solution.py:492
  26.8 1.6 %collective-permute-start.2 = (bf16[1152,128]{1,0:T(8,128)(2,1)S(1)}, bf16[1152,128]{1,0:T(8,128)(2,1)S(1)}, u32[]{:S(2)}, u32[]{:S(2)}) collective-permute-start(bf16[1152,128]{1,0:T(8,128)(2,1)S(1)} %get-tuple-element.51), channel_id=1, source_target_pairs={{0,1},{1,0},{2,3},{3,2},{4,5},{5,4},{6,7},{7,6},{8,9},{9,8},{10,11... | collective-permute-start | bytes 884744 | tf_op jit(solution)/shard_map/ppermute | solution.py:492
  28.6 6.9 %collective-permute-start.4 = (bf16[688,128]{1,0:T(8,128)(2,1)S(1)}, bf16[688,128]{1,0:T(8,128)(2,1)S(1)}, u32[]{:S(2)}, u32[]{:S(2)}) collective-permute-start(bf16[688,128]{1,0:T(8,128)(2,1)S(1)} %pad_maximum_fusion), channel_id=1, source_target_pairs={{0,4},{4,0},{8,12},{12,8},{16,20},{20,16},{24,28},{28,24},{1,5},{5... | collective-permute-start | bytes 528392 | tf_op jit(solution)/shard_map/ppermute | solution.py:492
  35.6 4.7 %collective-permute-start.5 = (bf16[400,128]{1,0:T(8,128)(2,1)S(1)}, bf16[400,128]{1,0:T(8,128)(2,1)S(1)}, u32[]{:S(2)}, u32[]{:S(2)}) collective-permute-start(bf16[400,128]{1,0:T(8,128)(2,1)S(1)} %pad_maximum_fusion.1), channel_id=1, source_target_pairs={{0,8},{4,12},{8,0},{12,4},{16,24},{20,28},{24,16},{28,20},{1,9},{5... | collective-permute-start | bytes 307208 | tf_op jit(solution)/shard_map/ppermute | solution.py:492
  40.4 5.2 %collective-permute-start.6 = (bf16[256,128]{1,0:T(8,128)(2,1)S(1)}, bf16[256,128]{1,0:T(8,128)(2,1)S(1)}, u32[]{:S(2)}, u32[]{:S(2)}) collective-permute-start(bf16[256,128]{1,0:T(8,128)(2,1)S(1)} %pad_maximum_fusion.2), channel_id=1, source_target_pairs={{0,16},{4,20},{8,24},{12,28},{16,0},{20,4},{24,8},{28,12},{1,17},{... | collective-permute-start | bytes 196616 | tf_op jit(solution)/shard_map/ppermute | solution.py:492
  45.7 4.3 %collective-permute-start.7 = (bf16[256,128]{1,0:T(8,128)(2,1)S(1)}, bf16[256,128]{1,0:T(8,128)(2,1)S(1)}, u32[]{:S(2)}, u32[]{:S(2)}) collective-permute-start(bf16[256,128]{1,0:T(8,128)(2,1)S(1)} %pad_maximum_fusion.3), channel_id=1, source_target_pairs={{0,2},{1,3},{2,0},{3,1},{4,6},{5,7},{6,4},{7,5},{8,10},{9,11},{10,... | collective-permute-start | bytes 196616 | tf_op jit(solution)/shard_map/ppermute | solution.py:492
  50.0 1.5 %collective-permute-start.8 = (bf16[144,128]{1,0:T(8,128)(2,1)S(1)}, bf16[144,128]{1,0:T(8,128)(2,1)S(1)}, u32[]{:S(2)}, u32[]{:S(2)}) collective-permute-start(bf16[144,128]{1,0:T(8,128)(2,1)S(1)} %add_convert_fusion.1.mine), channel_id=1, source_target_pairs={{0,1},{1,0},{2,3},{3,2},{4,5},{5,4},{6,7},{7,6},{8,9},{9,8},{10,11... | collective-permute-start | bytes 110600 | tf_op jit(solution)/shard_map/ppermute | solution.py:492
  50.1 1.4 %collective-permute-start.9 = (f32[56,128]{1,0:T(8,128)S(1)}, f32[56,128]{1,0:T(8,128)S(1)}, u32[]{:S(2)}, u32[]{:S(2)}) collective-permute-start(f32[56,128]{1,0:T(8,128)S(1)} %add_add_fusion.small_mine), channel_id=1, source_target_pairs={{0,1},{1,0},{2,3},{3,2},{4,5},{5,4},{6,7},{7,6},{8,9},{9,8},{10,11... | collective-permute-start | bytes 86024 | tf_op jit(solution)/shard_map/ppermute | solution.py:492

commit v4 on v3

--- a/solution.py
+++ b/solution.py
@@ -31,7 +31,7 @@
 
 
 def masked_row(array, mask, i):
-    return (array[i].astype(F32) * mask[i : i + 1].astype(F32)).astype(BF16)
+    return (array[i].astype(F32) * mask[i : i + 1]).astype(BF16)
 
 
 def group_of(rows, g):
@@ -86,18 +86,16 @@
     unrolled(tiles.shape[0], group)
 
 
-def pack_shifts(cells, packed, lon):
-    def group(g):
-        for half in range(2):
-            for b in range(7):
-                x = cells[2 * g + half, 2 * EDGE + b - 3 : 2 * EDGE + b - 3 + lon, :]
-                at = b * 256 + half * 128
-                packed[g, :, at : at + 128] = x.astype(BF16)
-
-    unrolled(packed.shape[0], group)
+def pack_group(cells, packed, lon, g):
+    for half in range(2):
+        for b in range(7):
+            x = cells[2 * g + half, 2 * EDGE + b - 3 : 2 * EDGE + b - 3 + lon, :]
+            at = b * 256 + half * 128
+            packed[g, :, at : at + 128] = x.astype(BF16)
 
 
 BORDER = 24
+SMALL = 64
 
 
 def pack_borders(before, after, borders, left, right, packed):
@@ -105,7 +103,7 @@
     near = iota((EDGE, 1), 0) < EDGE // 2
     blank = jnp.zeros((EDGE, 128), F32)
 
-    def group(g):
+    def place(g):
         for half in range(2):
             k = 2 * g + half
             at = half * groups * EDGE + g * EDGE
@@ -125,7 +123,7 @@
                 at = b * 256 + half * 128
                 packed[g, :, at : at + 128] = x.astype(BF16)
 
-    unrolled(groups, group)
+    return place
 
 
 def gelu_parts(z):
@@ -134,19 +132,37 @@
     return cumulative, density
 
 
-def edge_kernel(fields, cotangent, mask, first, last, masked, gm):
+def edge_kernel(
+    fields, cotangent, mask, first, last, masked, gm, near_mask, held_x, held_g, held_mask, arrived
+):
     lat, channels, lon = fields.shape
     groups = channels // GROUP
+    count = lat // 4
+    copies = [pltpu.make_async_copy(mask, held_mask, arrived.at[0])]
+    for r in range(4):
+        at = slice(count * r, count * (r + 1))
+        for k, (far, held) in enumerate(((fields, held_x), (cotangent, held_g))):
+            copies.append(
+                pltpu.make_async_copy(far.at[at], held.at[at], arrived.at[1 + 2 * r + k])
+            )
+    for copy in copies:
+        copy.start()
     row, lane = iota((2 * EDGE, lon), 0), iota((2 * EDGE, lon), 1)
     ends = jnp.where(lane == jnp.where(row < EDGE, row, row + lon - 2 * EDGE), 1.0, 0.0)
     ends = ends.astype(BF16)
-    rows = [masked_row(fields, mask, i) for i in range(lat)]
+    copies[0].wait()
+    near_mask[...] = held_mask[...].astype(F32)
+    rows, outer = [], []
+    for r in range(4):
+        copies[1 + 2 * r].wait()
+        copies[2 + 2 * r].wait()
+        for i in range(count * r, count * (r + 1)):
+            rows.append(masked_row(held_x, near_mask, i))
+            turned = masked_row(held_g, near_mask, i)
+            outer.append(dot_t(ends, turned))
+            masked[i] = rows[i]
+            gm[i] = turned
     cells = [dot_t(ends, group_of(rows, g)) for g in range(groups)]
-    turned = [masked_row(cotangent, mask, i) for i in range(lat)]
-    outer = [dot_t(ends, g) for g in turned]
-    for i in range(lat):
-        masked[i] = rows[i]
-        gm[i] = turned[i]
     for k, out in enumerate((first, last)):
         for half in range(2):
             at = slice(half * 128, (half + 1) * 128)
@@ -175,27 +191,22 @@
     lines,
     rolled,
     cells,
+    near_kernel,
+    near_gain,
+    near_bias,
+    arrived,
 ):
     lat, channels, lon = masked.shape
     hidden = w_in.shape[1]
     groups = channels // GROUP
-    lay_lines(kernel, lines)
-    build_tiles(lines, rolled, tiles, False)
-    gain_row = gain[...].reshape(1, channels)
-    gain_columns[...] = jnp.broadcast_to(gain_row, (128, channels)).T
-    bias_row = bias[...].reshape(1, hidden)
-    bias_columns = jnp.broadcast_to(bias_row, (64, hidden)).T
-    lane = iota((hidden, 64), 1)
-    high = bias_columns.astype(BF16).astype(F32)
-    middle = (bias_columns - high).astype(BF16).astype(F32)
-    low = bias_columns - high - middle
-    bias_columns = jnp.where(
-        lane == 0, high, jnp.where(lane == 1, middle, jnp.where(lane == 2, low, 0.0))
-    )
-    turned_in[...] = jnp.concatenate([w_in[...].astype(F32).T, bias_columns], axis=1).astype(BF16)
-    turned_out[...] = w_out[...].T
-    near_in[...] = w_in[...]
-    near_out[...] = w_out[...]
+    far = (kernel, gain, w_in, bias, w_out)
+    near = (near_kernel, near_gain, near_in, near_bias, near_out)
+    copies = [
+        pltpu.make_async_copy(x, y, arrived.at[k])
+        for k, (x, y) in enumerate(zip(far, near, strict=True))
+    ]
+    for copy in copies:
+        copy.start()
 
     rows = [masked[i] for i in range(lat)]
     blank = jnp.zeros((2 * EDGE, 128), F32)
@@ -206,7 +217,27 @@
             part = x[:, half * 128 : (half + 1) * 128]
             cells[k] = jnp.concatenate([blank, part, blank], axis=0)
             borders[k] = jnp.concatenate([part[:BORDER], part[lon - BORDER :]], axis=0)
-    pack_shifts(cells, packed, lon)
+        pack_group(cells, packed, lon, g)
+
+    for copy in copies:
+        copy.wait()
+    lay_lines(near_kernel, lines)
+    build_tiles(lines, rolled, tiles, False)
+    gain_row = near_gain[...].reshape(1, channels)
+    gain_columns[...] = jnp.broadcast_to(gain_row, (128, channels)).T
+    bias_row = near_bias[...].reshape(1, hidden)
+    bias_columns = jnp.broadcast_to(bias_row, (64, hidden)).T
+    lane = iota((hidden, 64), 1)
+    high = bias_columns.astype(BF16).astype(F32)
+    middle = (bias_columns - high).astype(BF16).astype(F32)
+    low = bias_columns - high - middle
+    bias_columns = jnp.where(
+        lane == 0, high, jnp.where(lane == 1, middle, jnp.where(lane == 2, low, 0.0))
+    )
+    turned_in[...] = jnp.concatenate(
+        [near_in[...].astype(F32).T, bias_columns], axis=1
+    ).astype(BF16)
+    turned_out[...] = near_out[...].T
 
 
 def forward_kernel(
@@ -242,13 +273,14 @@
     sent,
     shards,
 ):
-    lat, channels, lon = masked.shape
+    lat, channels, lon = gm.shape
     hidden = w_in.shape[1]
     groups = channels // GROUP
     before, after = halo_before[...].astype(F32), halo_after[...].astype(F32)
-    pack_borders(before, after, borders, left, right, packed_border)
+    place_borders = pack_borders(before, after, borders, left, right, packed_border)
 
     def band(g):
+        place_borders(g)
         border = packed_border[g]
         x = jnp.concatenate([border[:16], packed[g, 16 : lon - 16], border[16:]], axis=0)
         y = dot(x, tiles[g])
@@ -261,87 +293,112 @@
     total_out[...] = jnp.zeros_like(total_out)
     total_gain[...] = jnp.zeros_like(total_gain)
 
-    def block(y, g, inner):
+    gain_tile = gain_columns[...]
+
+    def normalise(y, g, inner):
         cols = y.shape[1]
-        gains = jnp.concatenate([gain_columns[...]] * (cols // 128), axis=1)
+        gains = jnp.concatenate([gain_tile] * (cols // 128), axis=1)
         y = y - jnp.sum(y, axis=0, keepdims=True) * (1.0 / channels)
         var = jnp.sum(y * y, axis=0, keepdims=True) * (1.0 / channels)
         sigma = lax.rsqrt(var + 1e-6)
         nhat = y * sigma
         normed = (nhat * gains).astype(BF16)
         normed = jnp.concatenate([normed, jnp.ones((64, cols), BF16)], axis=0)
+        state = dict(inner=inner, gains=gains, sigma=sigma, nhat=nhat, normed=normed, g=g)
         if inner:
-            upright, g_upright = normed.T, g.T
-        branch, d_normed = None, None
-        for h in range(0, hidden, 256):
-            at = slice(h, h + 256)
-            z = dot(turned_in[at, :], normed)
-            cumulative, density = gelu_parts(z)
-            d_act = dot(turned_out[at, :], g)
-            d_pre = (d_act * (cumulative + z * density)).astype(BF16)
-            part = dot(w_in[:, at], d_pre)
-            d_normed = part if d_normed is None else d_normed + part
-            if inner:
-                act = (z * cumulative).astype(BF16)
-                part = dot(w_out[:, at], act)
-                branch = part if branch is None else branch + part
-                total_in[at, :] += dot(d_pre, upright)
-                total_out[at, :] += dot(act, g_upright)
-        prod = d_normed * nhat
-        if inner:
+            state.update(upright=normed.T, g_upright=g.T)
+        return state
+
+    def head(state, h):
+        at = slice(h, h + 256)
+        return dot(turned_in[at, :], state["normed"]), dot(turned_out[at, :], state["g"])
+
+    def tail(state, h, z, d_act):
+        at = slice(h, h + 256)
+        cumulative, density = gelu_parts(z)
+        d_pre = (d_act * (cumulative + z * density)).astype(BF16)
+        part = dot(w_in[:, at], d_pre)
+        state["d_normed"] = part if h == 0 else state["d_normed"] + part
+        if state["inner"]:
+            act = (z * cumulative).astype(BF16)
+            part = dot(w_out[:, at], act)
+            state["branch"] = part if h == 0 else state["branch"] + part
+            total_in[at, :] += dot(d_pre, state["upright"])
+            total_out[at, :] += dot(act, state["g_upright"])
+
+    def finish(state):
+        nhat, gains = state["nhat"], state["gains"]
+        prod = state["d_normed"] * nhat
+        if state["inner"]:
             part = prod[:, :128]
-            for c in range(128, cols, 128):
+            for c in range(128, prod.shape[1], 128):
                 part = part + prod[:, c : c + 128]
             total_gain[...] += part
-        d_hat = d_normed * gains
+        d_hat = state["d_normed"] * gains
         mean = jnp.sum(d_hat, axis=0, keepdims=True) * (1.0 / channels)
         corr = jnp.sum(prod * gains, axis=0, keepdims=True) * (1.0 / channels)
-        return (sigma * (d_hat - mean - nhat * corr)).astype(BF16), branch
+        return (state["sigma"] * (d_hat - mean - nhat * corr)).astype(BF16)
 
     count = 4
+    blocks = lat // count
     copies = []
 
-    def rows_block(r):
+    def start(r):
         rows = range(count * r, count * (r + 1))
         y = []
         for i in rows:
             at = slice(i * GROUP, (i + 1) * GROUP)
             y.append(jnp.concatenate([conv[g, at, :] for g in range(groups)], axis=0))
-        d, branch = block(
+        return normalise(
             jnp.concatenate(y, axis=1), jnp.concatenate([gm[i] for i in rows], axis=1), True
         )
-        for k, i in enumerate(rows):
+
+    def start_edges():
+        lane = iota((1, 128), 1)
+        y = []
+        for i in range(lat):
+            half, k = (i * GROUP) // 128 * 128, i % 8
+            line = []
+            for tile in range(0, channels, 128):
+                x = jnp.zeros((EDGE, 128), F32)
+                for g in range(tile // GROUP, min(tile + 128, channels) // GROUP):
+                    piece = conv_edge[g, :, half : half + 128]
+                    piece = pltpu.roll(piece, (g - k) % 8 * GROUP, axis=1)
+                    x = jnp.where((lane >> 4) == g % 8, piece, x)
+                line.append(x)
+            y.append(jnp.concatenate(line, axis=1))
+        y = jnp.concatenate(y, axis=0).T[:channels]
+        at = 2 * groups * EDGE
+        g = jnp.where((lane & (EDGE - 1)) < EDGE // 2, after[at:], before[at:]).astype(BF16)
+        return normalise(y, g, False)
+
+    def end(r, state):
+        d = finish(state)
+        if r == blocks:
+            d_edge[...] = d
+            return
+        for k in range(count):
+            i = count * r + k
             at = slice(k * lon, (k + 1) * lon)
-            m = mask[i : i + 1].astype(F32)
-            rows_out[i] = ((masked[i].astype(F32) + branch[:, at]) * m).astype(BF16)
+            x = masked[i].astype(F32) + state["branch"][:, at]
+            rows_out[i] = (x * mask[i : i + 1]).astype(BF16)
             d_conv[i] = d[:, at]
-        copies.append(
-            pltpu.make_async_copy(
-                rows_out.at[count * r : count * (r + 1)],
-                output.at[count * r : count * (r + 1)],
-                sent.at[r],
-            )
-        )
+        at = slice(count * r, count * (r + 1))
+        copies.append(pltpu.make_async_copy(rows_out.at[at], output.at[at], sent.at[r]))
         copies[-1].start()
 
-    unrolled(lat // count, rows_block)
-
-    lane = iota((1, 128), 1)
-    y = []
-    for i in range(lat):
-        half, k = (i * GROUP) // 128 * 128, i % 8
-        line = []
-        for tile in range(0, channels, 128):
-            x = jnp.zeros((EDGE, 128), F32)
-            for g in range(tile // GROUP, min(tile + 128, channels) // GROUP):
-                piece = pltpu.roll(conv_edge[g, :, half : half + 128], (g - k) % 8 * GROUP, axis=1)
-                x = jnp.where((lane >> 4) == g % 8, piece, x)
-            line.append(x)
-        y.append(jnp.concatenate(line, axis=1))
-    y = jnp.concatenate(y, axis=0).T[:channels]
-    at = 2 * groups * EDGE
-    g = jnp.where((lane & (EDGE - 1)) < EDGE // 2, after[at:], before[at:]).astype(BF16)
-    d_edge[...], _ = block(y, g, False)
+    steps = [(r, h) for r in range(blocks + 1) for h in range(0, hidden, 256)]
+    states = {0: start(0)}
+    coming = head(states[0], 0)
+    for n, (r, h) in enumerate(steps):
+        here = coming
+        if h == 0 and r < blocks:
+            states[r + 1] = start(r + 1) if r + 1 < blocks else start_edges()
+        if n + 1 < len(steps):
+            coming = head(states[steps[n + 1][0]], steps[n + 1][1])
+        tail(states[r], h, *here)
+        if h + 256 == hidden:
+            end(r, states.pop(r))
 
     first = core[0] == 0
     rows = channels // shards
@@ -368,14 +425,15 @@
         copy.wait()
 
 
-def lay_cells(d_conv, d_edge, cells):
+def laid_cells(d_conv, d_edge, cells):
     lat, channels, lon = d_conv.shape
     rows = [d_conv[i] for i in range(lat)]
     near = iota((EDGE, 1), 0) < EDGE // 2
     lane = iota((1, 128), 1) >> 4
     blank = jnp.zeros((EDGE, 128), F32)
     edges = d_edge[...].astype(F32).T
-    for g in range(channels // GROUP):
+
+    def place(g):
         x = group_of(rows, g).astype(F32).T
         tile = (g * GROUP) // 128 * 128
         for half in range(2):
@@ -398,34 +456,43 @@
                 axis=0,
             )
 
-
-def taps_kernel(core, masked, d_conv, d_edge, sums, keep, send, cells, packed, small):
+    return place
+
+
+def taps_kernel(core, masked, d_conv, d_edge, sums, own, others, keep, send, cells, packed, small):
     lat, channels, lon = masked.shape
     groups = channels // GROUP
-    lay_cells(d_conv, d_edge, cells)
-    pack_shifts(cells, packed, lon)
+    place_cells = laid_cells(d_conv, d_edge, cells)
     rows = [masked[i] for i in range(lat)]
     bands = [band_mask(i) for i in range(lat)]
     sub, lane = iota((8, 1), 0), iota((1, 128), 1) >> 4
     small[...] = jnp.zeros_like(small)
 
     for g in range(groups):
-        g_all = dot(group_of(rows, g), packed[g])
+        place_cells(g)
+        pack_group(cells, packed, lon, g)
+        products = dot(group_of(rows, g), packed[g])
         taps = jnp.zeros((8, 128), F32)
         for b in range(7):
+            parts = [None] * 8
+            for i in range(lat):
+                at = slice(i * GROUP, (i + 1) * GROUP)
+                part = jnp.zeros((GROUP, 128), F32)
+                if i < 11:
+                    part = jnp.where(bands[i][:, :128], products[at, b * 256 : b * 256 + 128], part)
+                if i > 4:
+                    part = jnp.where(bands[i][:, 128:], products[at, b * 256 + 128 : b * 256 + 256], part)
+                part = part[:8] + part[8:]
+                parts[i % 8] = part if parts[i % 8] is None else parts[i % 8] + part
             total = None
-            for i in range(lat):
-                part = g_all[i * GROUP : (i + 1) * GROUP, b * 256 : (b + 1) * 256]
-                part = jnp.where(bands[i], part, 0.0)
-                part = part[:8] + part[8:]
-                part = pltpu.roll(part, ((3 - i) * GROUP) % 256, axis=1)[:, :128]
+            for i in range(8):
+                part = pltpu.roll(parts[i], (3 - i) % 8 * GROUP, axis=1)
                 total = part if total is None else total + part
             total = jnp.sum(total, axis=0, keepdims=True)
             taps = jnp.where(sub == 6 - b, total, taps)
         place = g * GROUP // 128
         for a in range(7):
-            shift = (g * GROUP - (6 - a) * GROUP) % 128
-            moved = pltpu.roll(taps, shift, axis=1)
+            moved = pltpu.roll(taps, (g + a - 6) % 8 * GROUP, axis=1)
             small[a, place] = jnp.where(lane == g % 8, moved, small[a, place])
 
     line = sums[0:1]
@@ -437,20 +504,24 @@
     )
     for k, piece in enumerate(pieces):
         small[k // 2, k % 2, 7:8] = piece
-    flat = small[...].reshape(112, 128)
+    flat = small[...].reshape(2 * SMALL, 128)
     first = core[0] == 0
-    keep[...] = jnp.where(first, flat[:56], flat[56:])
-    send[...] = jnp.where(first, flat[56:], flat[:56])
+    rows = own.shape[0]
+    keep[:rows] = own[...]
+    keep[rows:] = jnp.where(first, flat[:SMALL], flat[SMALL:]).astype(BF16)
+    send[:rows] = others[...]
+    send[rows:] = jnp.where(first, flat[SMALL:], flat[:SMALL]).astype(BF16)
 
 
 def spread_kernel(gm, mask, lines, d_conv, d_edge, grad_fields, rolled, tiles, cells, packed, spread):
     lat, channels, lon = gm.shape
     groups = channels // GROUP
     build_tiles(lines, rolled, tiles, True)
-    lay_cells(d_conv, d_edge, cells)
-    pack_shifts(cells, packed, lon)
+    place_cells = laid_cells(d_conv, d_edge, cells)
 
     def band(g):
+        place_cells(g)
+        pack_group(cells, packed, lon, g)
         spread[g] = dot(packed[g], tiles[g]).T
 
     unrolled(groups, band)
@@ -458,18 +529,17 @@
         x = jnp.concatenate(
             [spread[g, i * GROUP : (i + 1) * GROUP, :] for g in range(groups)], axis=0
         )
-        x = gm[i].astype(F32) + x * mask[i : i + 1].astype(F32)
+        x = gm[i].astype(F32) + x * mask[i : i + 1]
         grad_fields[i] = x.astype(BF16)
 
 
-def final_kernel(core, mine, other, small_mine, small_other, grad_in, grad_out, grad_kernel, grad_gain, grad_bias, scale):
+def final_kernel(core, mine, other, grad_in, grad_out, grad_kernel, grad_gain, grad_bias, scale):
     first = core[0] == 0
     mine, other = mine[...].astype(F32) * scale, other[...].astype(F32) * scale
     sum_in, sum_out = jnp.where(first, mine, other), jnp.where(first, other, mine)
-    mine, other = small_mine[...] * scale, small_other[...] * scale
-    small = jnp.concatenate(
-        [jnp.where(first, mine, other), jnp.where(first, other, mine)], axis=0
-    )
+    at = mine.shape[0] - SMALL
+    small = jnp.concatenate([sum_in[at:], sum_out[at:]], axis=0)
+    sum_in, sum_out = sum_in[:at], sum_out[:at]
     rows, hidden = grad_in.shape
     for k in range(hidden // 128):
         grad_in[:, k * 128 : (k + 1) * 128] = sum_in[k * rows : (k + 1) * rows]
@@ -511,17 +581,7 @@
     return kept, sent.reshape(-1, 128)
 
 
-def two_parts(x):
-    high = lax.reduce_precision(x, exponent_bits=8, mantissa_bits=7)
-    return jnp.concatenate([high, x - high], axis=0).astype(BF16)
-
-
-def one_part(x):
-    rows = x.shape[0] // 2
-    return x[:rows].astype(F32) + x[rows:].astype(F32)
-
-
-HBM, VMEM, SMEM = pltpu.HBM, pltpu.VMEM, pltpu.SMEM
+VMEM, SMEM, FAR = pltpu.VMEM, pltpu.SMEM, pltpu.HBM
 
 
 def call(body, name, outs, scratch, megabytes, spaces, out_spaces):
@@ -529,7 +589,7 @@
         return VMEM(shape, dtype) if space is VMEM else jax.ShapeDtypeStruct(shape, dtype)
 
     def spec(space):
-        return pl.BlockSpec(memory_space={SMEM: SMEM, pl.ANY: pl.ANY}.get(space, VMEM))
+        return pl.BlockSpec(memory_space={SMEM: SMEM, FAR: pl.ANY}.get(space, VMEM))
 
     kernel = pl.pallas_call(
         body,
@@ -544,7 +604,7 @@
     def run(*args):
         return kernel(
             *[
-                pltpu.with_memory_space_constraint(x, space) if space in (HBM, VMEM) else x
+                pltpu.with_memory_space_constraint(x, space) if space in (FAR, VMEM) else x
                 for x, space in zip(args, spaces, strict=True)
             ]
         )
@@ -573,8 +633,14 @@
     border = ((2 * groups, 2 * EDGE + BORDER, 128), F32)
     held = ((groups, 256, lon), F32)
 
-    first, last, masked, gm = call(
-        edge_kernel, "edges", [halo, halo, field, field], [], 8, [HBM] * 3, [None, None, VMEM, VMEM]
+    first, last, masked, gm, mask = call(
+        edge_kernel,
+        "edges",
+        [halo, halo, field, field, ((lat, lon), F32)],
+        [field, field, ((lat, lon), jnp.int32), pltpu.SemaphoreType.DMA((9,))],
+        8,
+        [FAR] * 3,
+        [VMEM] * 5,
     )(fields, cotangent, land_sea)
     up = [(i, (i + 1) % tiles) for i in range(tiles)]
     before = lax.ppermute(last, "lon", up)
@@ -594,13 +660,21 @@
             ((channels, 128), F32),
             ((8 * groups, 256), F32),
         ],
-        [rolled, cells],
-        16,
-        [VMEM] + [HBM] * 5,
+        [
+            rolled,
+            cells,
+            ((7, 7, channels), F32),
+            ((channels,), F32),
+            ((hidden,), F32),
+            pltpu.SemaphoreType.DMA((5,)),
+        ],
+        8,
+        [VMEM] + [FAR] * 5,
         [VMEM] * 9,
     )(masked, kernel, ln_gain, weight_in, bias_in, w_out)
     lines = ready[-1]
 
+    lines = ready[-1]
     output, d_conv, d_edge, keep, send, sums = call(
         functools.partial(forward_kernel, shards=shards),
         "forward",
@@ -624,51 +698,55 @@
             field,
             pltpu.SemaphoreType.DMA((lat // 4,)),
         ],
-        20,
-        [SMEM, HBM, HBM, VMEM, VMEM, HBM] + [VMEM] * 8,
-        [pl.ANY] + [VMEM] * 2 + [None] * 2 + [VMEM],
-    )(core, before, after, masked, gm, land_sea, *ready[:-1])
-
-    dp_bits, lon_bits = bits_of(shards), bits_of(tiles)
-    arrived = swapped(send, "lon", 1)
-    small, send = call(
+        14,
+        [SMEM] + [VMEM] * 13,
+        [FAR] + [VMEM] * 5,
+    )(core, before, after, masked, gm, mask, *ready[:-1])
+
+    keep, send = call(
         taps_kernel,
         "taps",
-        [((56, 128), F32)] * 2,
-        [cells, packed, ((7, 2, 8, 128), F32)],
-        20,
-        [SMEM] + [VMEM] * 4,
-        [None] * 2,
-    )(core, masked, d_conv, d_edge, sums)
-    small = small + swapped(send, "lon", 1)
-    mine = both(keep, arrived).reshape(shards, -1, 128)
-    for bit in dp_bits:
+        [((rows + SMALL, 128), BF16)] * 2,
+        [cells, packed, ((8, 2, 8, 128), F32)],
+        10,
+        [SMEM] + [VMEM] * 6,
+        [VMEM] * 2,
+    )(core, masked, d_conv, d_edge, sums, keep, send)
+    mine = both(keep, swapped(send, "lon", 1))
+    mine, small = mine[:rows].reshape(shards, -1, 128), mine[rows:]
+
+    def spread(d_conv):
+        return call(
+            spread_kernel,
+            "spread",
+            [field],
+            [rolled, tile, cells, packed, held],
+            24,
+            [VMEM] * 5,
+            [None],
+        )(gm, mask, lines, d_conv, d_edge)
+
+    beside = [(spread, d_conv)]
+    made = []
+    for bit in bits_of(shards):
         kept, sent = halved(mine, bit)
-        sent = jnp.concatenate([sent, two_parts(small)], axis=0)
-        if bit == 1:
-            sent, d_conv = lax.optimization_barrier((sent, d_conv))
-        arrived = swapped(sent, "dp", bit)
-        if bit == 1:
-            (grad_fields,) = call(
-                spread_kernel,
-                "spread",
-                [field],
-                [rolled, tile, cells, packed, held],
-                32,
-                [VMEM, HBM] + [VMEM] * 3,
-                [None],
-            )(gm, land_sea, lines, d_conv, d_edge)
-            arrived, grad_fields = lax.optimization_barrier((arrived, grad_fields))
-        count = kept.size // 128
-        mine = both(kept, arrived[:count].reshape(kept.shape))
-        small = small + one_part(arrived[count:])
-    mine = mine.reshape(-1, 128)
-    for bit in lon_bits[1:]:
-        arrived = swapped(jnp.concatenate([mine, two_parts(small)], axis=0), "lon", bit)
-        small = small + one_part(arrived[mine.shape[0] :])
-        mine = both(mine, arrived[: mine.shape[0]])
+        count = sent.shape[0]
+        sent = jnp.concatenate([sent, small], axis=0)
+        if beside:
+            work, needs = beside.pop(0)
+            sent, needs = lax.optimization_barrier((sent, needs))
+            arrived = swapped(sent, "dp", bit)
+            (result,) = work(needs)
+            arrived, result = lax.optimization_barrier((arrived, result))
+            made.append(result)
+        else:
+            arrived = swapped(sent, "dp", bit)
+        mine, small = both(kept, arrived[:count].reshape(kept.shape)), both(small, arrived[count:])
+    (grad_fields,) = made
+    mine = jnp.concatenate([mine.reshape(-1, 128), small], axis=0)
+    for bit in bits_of(tiles)[1:]:
+        mine = both(mine, swapped(mine, "lon", bit))
     other = swapped(mine, "lon", 1)
-    small_other = swapped(small, "lon", 1)
 
     scale = 1.0 / math.sqrt(samples * lat * lon * shards * tiles)
     grads = call(
@@ -683,9 +761,9 @@
         ],
         [],
         8,
-        [SMEM] + [None] * 4,
+        [SMEM] + [VMEM] * 2,
         [None] * 5,
-    )(core, mine, other, small, small_other)
+    )(core, mine, other)
     return (output.transpose(0, 2, 1)[None], grad_fields.transpose(0, 2, 1)[None], *grads)
 
 

time: 52.5 us -> 47.5 us (0.905)
  Pallas kernels: 27.3 us -> 22.7 us
  waiting for transfers between devices: 10.9 us -> 12.4 us
  starting transfers between devices: 12.3 us -> 11 us
  local copies, waits for them, and re-layouts: 0.72 us -> 0.1 us
    pallas_call x6, Pallas kernels: 27.3 us -> 22.7 us  [run(): kernel(*[pltpu.with_memory_space_constraint(x, space) if space in (FAR, V...]
    ppermute x8 -> x6, waiting for transfers between devices: 10.9 us -> 12.4 us  [swapped(): return lax.ppermute(x, axis, [(i, i ^ bit) for i in range(peers)])]
    ppermute x8 -> x6, starting transfers between devices: 9.76 us -> 8.54 us  [swapped(): return lax.ppermute(x, axis, [(i, i ^ bit) for i in range(peers)])]
    unnamed x4 -> x0, local copies, waits for them, and re-layouts: 0.65 us -> none
  transfers between devices with their start and end apart: 10 -> 8, of which waited for: 7 -> 6; matrix products, arithmetic and copies ran while one was open for 0% -> 0% of each run, Pallas kernels for 16% -> 14%
where the time goes in v4:
time: 47.5 us; the launch traced here: 47.3 us
  Pallas kernels  22.7 us (48%)
  waiting for transfers between devices  12.4 us (26%)
  starting transfers between devices  11 us (23%)
  between operations  0.8 us (2%)
    pallas_call x6, Pallas kernels, run(): kernel(*[pltpu.with_memory_space_constraint(x, space) if space in (FAR, V...  22.7 us
    ppermute x6, waiting for transfers between devices, swapped(): return lax.ppermute(x, axis, [(i, i ^ bit) for i in range(peers)])  12.4 us
    ppermute x6, starting transfers between devices, swapped(): return lax.ppermute(x, axis, [(i, i ^ bit) for i in range(peers)])  8.54 us
    ppermute x1, starting transfers between devices, per_device(): after = lax.ppermute(first, 'lon', [(j, i) for i, j in up])  1.99 us
  transfers between devices with their start and end apart: 8, of which 6 were waited for; matrix products, arithmetic and copies ran while one was open for 0% of the time, Pallas kernels for 14%

profile of v4, /device:TPU:0, one launch (start us, length us, event | category | flops | bytes accessed | tf_op | source)
XLA Modules:
  0.0 47.3 jit_solution(6348043104614314209)
XLA Ops:
  0.6 2.3 %edges.1 = (bf16[384,128]{1,0:T(8,128)(2,1)S(1)}, bf16[384,128]{1,0:T(8,128)(2,1)S(1)}, bf16[16,192,128]{2,1,0:T(8,128)(2,1)S(1)}, bf16[16,192,128]{2,1,0:T(8,128)(2,1)S(1)}, f32[16,128]{1,0:T(8,128)S(1)}) custom-call(bf16[16,192,128]{2,1,0:T(8,128)(2,1)} %bitcast.39, bf16[16,192,128]{2,1,0:T(8,128)(2,1)} %bitcast.40, s32[16,128]{1,0:T(8,128)} %mask.1), custom_call_target="tpu_custom_call" | custom-call | tf_op jit(solution)/shard_map/edges/pallas_call | solution.py:605
  2.9 0.5 %collective-permute-start = (bf16[384,128]{1,0:T(8,128)(2,1)S(1)}, bf16[384,128]{1,0:T(8,128)(2,1)S(1)}, u32[]{:S(2)}, u32[]{:S(2)}) collective-permute-start(bf16[384,128]{1,0:T(8,128)(2,1)S(1)} %get-tuple-element.38), channel_id=1, source_target_pairs={{0,1},{1,2},{2,3},{3,0},{4,5},{5,6},{6,7},{7,4},{8,9},{9,10},{10,1... | collective-permute-start | bytes 294920 | tf_op jit(solution)/shard_map/ppermute | solution.py:646
  3.4 2.0 %collective-permute-start.1 = (bf16[384,128]{1,0:T(8,128)(2,1)S(1)}, bf16[384,128]{1,0:T(8,128)(2,1)S(1)}, u32[]{:S(2)}, u32[]{:S(2)}) collective-permute-start(bf16[384,128]{1,0:T(8,128)(2,1)S(1)} %get-tuple-element.39), channel_id=1, source_target_pairs={{1,0},{2,1},{3,2},{0,3},{5,4},{6,5},{7,6},{4,7},{9,8},{10,9},{11,1... | collective-permute-start | bytes 294920 | tf_op jit(solution)/shard_map/ppermute | solution.py:647
  5.4 3.1 %prepare.1 = (bf16[12,1792,256]{2,1,0:T(8,128)(2,1)S(1)}, bf16[12,128,1792]{2,1,0:T(8,128)(2,1)S(1)}, f32[24,48,128]{2,1,0:T(8,128)S(1)}, bf16[768,256]{1,0:T(8,...) custom-call(bf16[16,192,128]{2,1,0:T(8,128)(2,1)S(1)} %get-tuple-ele, ...), custom_call_target="tpu_custom_call" | custom-call | tf_op jit(solution)/shard_map/prepare/pallas_call | solution.py:605
  8.6 0.0 collective-permute-done.halo_before
  8.6 0.0 collective-permute-done.1.halo_after
  8.6 9.2 %forward.1 = (bf16[16,192,128]{2,1,0:T(8,128)(2,1)}, bf16[16,192,128]{2,1,0:T(8,128)(2,1)S(1)}, bf16[192,128]{1,0:T(8,128)(2,1)S(1)}, bf16[1152,128]{1,0:T(8,128...) custom-call(s32[1]{0:T(128)} %bitcast.core, bf16[384,128]{1,0:T(8,128)(2,1)S(1)} %collective-permute-done.halo_before, ...), custom_call_target="tpu_custom_call" | custom-call | tf_op jit(solution)/shard_map/forward/pallas_call | solution.py:605
  17.8 3.8 %taps.1 = (bf16[1216,128]{1,0:T(8,128)(2,1)S(1)}, bf16[1216,128]{1,0:T(8,128)(2,1)S(1)}) custom-call(s32[1]{0:T(128)} %bitcast.core, bf16[16,192,128]{2,1,0:T(8,128)(2,1)S(1)} %get-tuple-element.40.masked, bf16[16,192,128]{2,1,0:T(8,128)(2,1)S(1)} %get-tuple-element.61.d_conv, bf16[192,128]{1,0:T(8,128)(2,1)S(1)} %get-tuple-element.53.d_edge, ...), custom_call_target="tpu_custom_call" | custom-call | tf_op jit(solution)/shard_map/taps/pallas_call | solution.py:605
  21.6 1.5 %collective-permute-start.2 = (bf16[1216,128]{1,0:T(8,128)(2,1)S(1)}, bf16[1216,128]{1,0:T(8,128)(2,1)S(1)}, u32[]{:S(2)}, u32[]{:S(2)}) collective-permute-start(bf16[1216,128]{1,0:T(8,128)(2,1)S(1)} %get-tuple-element.58), channel_id=1, source_target_pairs={{0,1},{1,0},{2,3},{3,2},{4,5},{5,4},{6,7},{7,6},{8,9},{9,8},{10,11... | collective-permute-start | bytes 933896 | tf_op jit(solution)/shard_map/ppermute | solution.py:562
  23.1 1.2 %collective-permute-done.2 = bf16[1216,128]{1,0:T(8,128)(2,1)S(1)} collective-permute-done((bf16[1216,128]{1,0:T(8,128)(2,1)S(1)}, bf16[1216,128]{1,0:T(8,128)(2,1)S(1)}, u32[]{:S(2)}, u32[]{:S(2)}) %collective-permute-start.2) | collective-permute-done | bytes 311328 | tf_op jit(solution)/shard_map/ppermute | solution.py:562
  24.4 0.1 add_convert_fusion
  24.5 1.6 %collective-permute-start.3 = (bf16[640,128]{1,0:T(8,128)(2,1)S(1)}, bf16[640,128]{1,0:T(8,128)(2,1)S(1)}, u32[]{:S(2)}, u32[]{:S(2)}) collective-permute-start(bf16[640,128]{1,0:T(8,128)(2,1)S(1)} %pad_maximum_fusion), channel_id=1, source_target_pairs={{0,4},{4,0},{8,12},{12,8},{16,20},{20,16},{24,28},{28,24},{1,5},{5... | collective-permute-start | bytes 491528 | tf_op jit(solution)/shard_map/ppermute | solution.py:562
  26.1 3.5 %spread.1 = bf16[16,192,128]{2,1,0:T(8,128)(2,1)} custom-call(bf16[16,192,128]{2,1,0:T(8,128)(2,1)S(1)} %get-tuple-element.41.gm, f32[16,128]{1,0:T(8,128)S(1)} %get-tuple-element.42.mask, f32[96,256]{1,0:T(8,128)S(1)} %get-tuple-element.60.lines, bf16[16,192,128]{2,1,0:T(8,128)(2,1)S(1)} %get-tuple-element.61.d_conv, ...), custom_call_target="tpu_custom_call" | custom-call | tf_op jit(solution)/shard_map/spread/pallas_call | solution.py:605
  29.6 1.4 %collective-permute-done.3 = bf16[640,128]{1,0:T(8,128)(2,1)S(1)} collective-permute-done((bf16[640,128]{1,0:T(8,128)(2,1)S(1)}, bf16[640,128]{1,0:T(8,128)(2,1)S(1)}, u32[]{:S(2)}, u32[]{:S(2)}) %collective-permute-start.3) | collective-permute-done | bytes 163872 | tf_op jit(solution)/shard_map/ppermute | solution.py:562
  31.2 1.6 %collective-permute-start.4 = (bf16[352,128]{1,0:T(8,128)(2,1)S(1)}, bf16[352,128]{1,0:T(8,128)(2,1)S(1)}, u32[]{:S(2)}, u32[]{:S(2)}) collective-permute-start(bf16[352,128]{1,0:T(8,128)(2,1)S(1)} %pad_maximum_fusion.1), channel_id=1, source_target_pairs={{0,8},{4,12},{8,0},{12,4},{16,24},{20,28},{24,16},{28,20},{1,9},{5... | collective-permute-start | bytes 270344 | tf_op jit(solution)/shard_map/ppermute | solution.py:562
  32.8 3.0 %collective-permute-done.4 = bf16[352,128]{1,0:T(8,128)(2,1)S(1)} collective-permute-done((bf16[352,128]{1,0:T(8,128)(2,1)S(1)}, bf16[352,128]{1,0:T(8,128)(2,1)S(1)}, u32[]{:S(2)}, u32[]{:S(2)}) %collective-permute-start.4) | collective-permute-done | bytes 90144 | tf_op jit(solution)/shard_map/ppermute | solution.py:562
  35.9 2.7 %collective-permute-start.5 = (bf16[208,128]{1,0:T(8,128)(2,1)S(1)}, bf16[208,128]{1,0:T(8,128)(2,1)S(1)}, u32[]{:S(2)}, u32[]{:S(2)}) collective-permute-start(bf16[208,128]{1,0:T(8,128)(2,1)S(1)} %pad_maximum_fusion.2), channel_id=1, source_target_pairs={{0,16},{4,20},{8,24},{12,28},{16,0},{20,4},{24,8},{28,12},{1,17},{... | collective-permute-start | bytes 159752 | tf_op jit(solution)/shard_map/ppermute | solution.py:562
  38.5 2.4 %collective-permute-done.5 = bf16[208,128]{1,0:T(8,128)(2,1)S(1)} collective-permute-done((bf16[208,128]{1,0:T(8,128)(2,1)S(1)}, bf16[208,128]{1,0:T(8,128)(2,1)S(1)}, u32[]{:S(2)}, u32[]{:S(2)}) %collective-permute-start.5) | collective-permute-done | bytes 53280 | tf_op jit(solution)/shard_map/ppermute | solution.py:562
  41.0 1.1 %collective-permute-start.6 = (bf16[208,128]{1,0:T(8,128)(2,1)S(1)}, bf16[208,128]{1,0:T(8,128)(2,1)S(1)}, u32[]{:S(2)}, u32[]{:S(2)}) collective-permute-start(bf16[208,128]{1,0:T(8,128)(2,1)S(1)} %pad_maximum_fusion.3), channel_id=1, source_target_pairs={{0,2},{1,3},{2,0},{3,1},{4,6},{5,7},{6,4},{7,5},{8,10},{9,11},{10,... | collective-permute-start | bytes 159752 | tf_op jit(solution)/shard_map/ppermute | solution.py:562
  42.1 3.1 %collective-permute-done.6 = bf16[208,128]{1,0:T(8,128)(2,1)S(1)} collective-permute-done((bf16[208,128]{1,0:T(8,128)(2,1)S(1)}, bf16[208,128]{1,0:T(8,128)(2,1)S(1)}, u32[]{:S(2)}, u32[]{:S(2)}) %collective-permute-start.6) | collective-permute-done | bytes 53280 | tf_op jit(solution)/shard_map/ppermute | solution.py:562
  45.3 0.1 collective-permute-start.7
  45.3 1.2 %collective-permute-done.7.other = bf16[208,128]{1,0:T(8,128)(2,1)S(1)} collective-permute-done((bf16[208,128]{1,0:T(8,128)(2,1)S(1)}, bf16[208,128]{1,0:T(8,128)(2,1)S(1)}, u32[]{:S(2)}, u32[]{:S(2)}) %collective-permute-start.7) | collective-permute-done | bytes 53280 | tf_op jit(solution)/shard_map/ppermute | solution.py:562
  46.6 0.7 %final.1 = (f32[24,768]{1,0:T(8,128)}, f32[96,192]{1,0:T(8,128)}, f32[7,7,192]{2,1,0:T(8,128)}, f32[192]{0:T(256)}, f32[768]{0:T(1024)}) custom-call(s32[1]{0:T(128)} %bitcast.core, bf16[208,128]{1,0:T(8,128)(2,1)S(1)} %add_convert_fusion.1.mine, bf16[208,128]{1,0:T(8,128)(2,1)S(1)} %collective-permute-done.7.other), custom_call_target="tpu_custom_call" | custom-call | tf_op jit(solution)/shard_map/final/pallas_call | solution.py:605
  (18 shorter events, 0.3 us)
Async XLA Ops:
  2.9 5.6 %collective-permute-start = (bf16[384,128]{1,0:T(8,128)(2,1)S(1)}, bf16[384,128]{1,0:T(8,128)(2,1)S(1)}, u32[]{:S(2)}, u32[]{:S(2)}) collective-permute-start(bf16[384,128]{1,0:T(8,128)(2,1)S(1)} %get-tuple-element.38), channel_id=1, source_target_pairs={{0,1},{1,2},{2,3},{3,0},{4,5},{5,6},{6,7},{7,4},{8,9},{9,10},{10,1... | collective-permute-start | bytes 294920 | tf_op jit(solution)/shard_map/ppermute | solution.py:646
  3.4 5.2 %collective-permute-start.1 = (bf16[384,128]{1,0:T(8,128)(2,1)S(1)}, bf16[384,128]{1,0:T(8,128)(2,1)S(1)}, u32[]{:S(2)}, u32[]{:S(2)}) collective-permute-start(bf16[384,128]{1,0:T(8,128)(2,1)S(1)} %get-tuple-element.39), channel_id=1, source_target_pairs={{1,0},{2,1},{3,2},{0,3},{5,4},{6,5},{7,6},{4,7},{9,8},{10,9},{11,1... | collective-permute-start | bytes 294920 | tf_op jit(solution)/shard_map/ppermute | solution.py:647
  21.6 2.8 %collective-permute-start.2 = (bf16[1216,128]{1,0:T(8,128)(2,1)S(1)}, bf16[1216,128]{1,0:T(8,128)(2,1)S(1)}, u32[]{:S(2)}, u32[]{:S(2)}) collective-permute-start(bf16[1216,128]{1,0:T(8,128)(2,1)S(1)} %get-tuple-element.58), channel_id=1, source_target_pairs={{0,1},{1,0},{2,3},{3,2},{4,5},{5,4},{6,7},{7,6},{8,9},{9,8},{10,11... | collective-permute-start | bytes 933896 | tf_op jit(solution)/shard_map/ppermute | solution.py:562
  24.5 6.5 %collective-permute-start.3 = (bf16[640,128]{1,0:T(8,128)(2,1)S(1)}, bf16[640,128]{1,0:T(8,128)(2,1)S(1)}, u32[]{:S(2)}, u32[]{:S(2)}) collective-permute-start(bf16[640,128]{1,0:T(8,128)(2,1)S(1)} %pad_maximum_fusion), channel_id=1, source_target_pairs={{0,4},{4,0},{8,12},{12,8},{16,20},{20,16},{24,28},{28,24},{1,5},{5... | collective-permute-start | bytes 491528 | tf_op jit(solution)/shard_map/ppermute | solution.py:562
  31.2 4.6 %collective-permute-start.4 = (bf16[352,128]{1,0:T(8,128)(2,1)S(1)}, bf16[352,128]{1,0:T(8,128)(2,1)S(1)}, u32[]{:S(2)}, u32[]{:S(2)}) collective-permute-start(bf16[352,128]{1,0:T(8,128)(2,1)S(1)} %pad_maximum_fusion.1), channel_id=1, source_target_pairs={{0,8},{4,12},{8,0},{12,4},{16,24},{20,28},{24,16},{28,20},{1,9},{5... | collective-permute-start | bytes 270344 | tf_op jit(solution)/shard_map/ppermute | solution.py:562
  35.9 5.1 %collective-permute-start.5 = (bf16[208,128]{1,0:T(8,128)(2,1)S(1)}, bf16[208,128]{1,0:T(8,128)(2,1)S(1)}, u32[]{:S(2)}, u32[]{:S(2)}) collective-permute-start(bf16[208,128]{1,0:T(8,128)(2,1)S(1)} %pad_maximum_fusion.2), channel_id=1, source_target_pairs={{0,16},{4,20},{8,24},{12,28},{16,0},{20,4},{24,8},{28,12},{1,17},{... | collective-permute-start | bytes 159752 | tf_op jit(solution)/shard_map/ppermute | solution.py:562
  41.0 4.2 %collective-permute-start.6 = (bf16[208,128]{1,0:T(8,128)(2,1)S(1)}, bf16[208,128]{1,0:T(8,128)(2,1)S(1)}, u32[]{:S(2)}, u32[]{:S(2)}) collective-permute-start(bf16[208,128]{1,0:T(8,128)(2,1)S(1)} %pad_maximum_fusion.3), channel_id=1, source_target_pairs={{0,2},{1,3},{2,0},{3,1},{4,6},{5,7},{6,4},{7,5},{8,10},{9,11},{10,... | collective-permute-start | bytes 159752 | tf_op jit(solution)/shard_map/ppermute | solution.py:562
  45.3 1.3 %collective-permute-start.7 = (bf16[208,128]{1,0:T(8,128)(2,1)S(1)}, bf16[208,128]{1,0:T(8,128)(2,1)S(1)}, u32[]{:S(2)}, u32[]{:S(2)}) collective-permute-start(bf16[208,128]{1,0:T(8,128)(2,1)S(1)} %add_convert_fusion.1.mine), channel_id=1, source_target_pairs={{0,1},{1,0},{2,3},{3,2},{4,5},{5,4},{6,7},{7,6},{8,9},{9,8},{10,11... | collective-permute-start | bytes 159752 | tf_op jit(solution)/shard_map/ppermute | solution.py:562

commit v5 on v4

--- a/solution.py
+++ b/solution.py
@@ -95,7 +95,7 @@
 
 
 BORDER = 24
-SMALL = 64
+SMALL = 96
 
 
 def pack_borders(before, after, borders, left, right, packed):
@@ -317,12 +317,14 @@
         at = slice(h, h + 256)
         cumulative, density = gelu_parts(z)
         d_pre = (d_act * (cumulative + z * density)).astype(BF16)
-        part = dot(w_in[:, at], d_pre)
-        state["d_normed"] = part if h == 0 else state["d_normed"] + part
+        state.setdefault("d_pre", []).append(d_pre)
+        if h + 256 == hidden:
+            state["d_normed"] = dot(w_in[...], jnp.concatenate(state["d_pre"], axis=0))
         if state["inner"]:
             act = (z * cumulative).astype(BF16)
-            part = dot(w_out[:, at], act)
-            state["branch"] = part if h == 0 else state["branch"] + part
+            state.setdefault("act", []).append(act)
+            if h + 256 == hidden:
+                state["branch"] = dot(w_out[...], jnp.concatenate(state["act"], axis=0))
             total_in[at, :] += dot(d_pre, state["upright"])
             total_out[at, :] += dot(act, state["g_upright"])
 
@@ -459,7 +461,7 @@
     return place
 
 
-def taps_kernel(core, masked, d_conv, d_edge, sums, own, others, keep, send, cells, packed, small):
+def taps_kernel(masked, d_conv, d_edge, sums, out, cells, packed, small):
     lat, channels, lon = masked.shape
     groups = channels // GROUP
     place_cells = laid_cells(d_conv, d_edge, cells)
@@ -490,10 +492,10 @@
                 total = part if total is None else total + part
             total = jnp.sum(total, axis=0, keepdims=True)
             taps = jnp.where(sub == 6 - b, total, taps)
-        place = g * GROUP // 128
         for a in range(7):
-            moved = pltpu.roll(taps, (g + a - 6) % 8 * GROUP, axis=1)
-            small[a, place] = jnp.where(lane == g % 8, moved, small[a, place])
+            place, slot = (a, g) if g < 8 else (7 + a // 2, g % 4 + 4 * (a % 2))
+            moved = pltpu.roll(taps, (slot + a - 6) % 8 * GROUP, axis=1)
+            small[place] = jnp.where(lane == slot, moved, small[place])
 
     line = sums[0:1]
     hidden = line.shape[1] - channels
@@ -503,14 +505,19 @@
         jnp.concatenate([line[:, hidden + 128 :], jnp.zeros((1, 256 - channels), F32)], axis=1)
     )
     for k, piece in enumerate(pieces):
-        small[k // 2, k % 2, 7:8] = piece
-    flat = small[...].reshape(2 * SMALL, 128)
-    first = core[0] == 0
-    rows = own.shape[0]
-    keep[:rows] = own[...]
-    keep[rows:] = jnp.where(first, flat[:SMALL], flat[SMALL:]).astype(BF16)
-    send[:rows] = others[...]
-    send[rows:] = jnp.where(first, flat[SMALL:], flat[:SMALL]).astype(BF16)
+        small[k, 7:8] = piece
+    out[...] = small[...].reshape(SMALL, 128).astype(BF16)
+
+
+def fold_kernel(have, keep, arrived, small, kept, sent, shards):
+    rows = kept.shape[0]
+    total = keep[...].astype(F32) + arrived[...].astype(F32)
+    total = total.reshape(-1, 2, total.shape[0] // shards, 128)
+    even, odd = total[:, 0].reshape(rows, 128), total[:, 1].reshape(rows, 128)
+    first = have[0] == 0
+    kept[...] = jnp.where(first, even, odd).astype(BF16)
+    sent[:rows] = jnp.where(first, odd, even).astype(BF16)
+    sent[rows:] = small[...]
 
 
 def spread_kernel(gm, mask, lines, d_conv, d_edge, grad_fields, rolled, tiles, cells, packed, spread):
@@ -538,7 +545,7 @@
     mine, other = mine[...].astype(F32) * scale, other[...].astype(F32) * scale
     sum_in, sum_out = jnp.where(first, mine, other), jnp.where(first, other, mine)
     at = mine.shape[0] - SMALL
-    small = jnp.concatenate([sum_in[at:], sum_out[at:]], axis=0)
+    small = mine[at:] + other[at:]
     sum_in, sum_out = sum_in[:at], sum_out[:at]
     rows, hidden = grad_in.shape
     for k in range(hidden // 128):
@@ -548,8 +555,10 @@
     rest = sum_out[rows:]
     grad_out[:, 128:] = jnp.concatenate([rest[:, :64], rest[:, 64:]], axis=0)
     for a in range(7):
-        grad_kernel[a, :, :128] = small[16 * a : 16 * a + 7]
-        grad_kernel[a, :, 128:] = small[16 * a + 8 : 16 * a + 15, : channels - 128]
+        at = 8 * (7 + a // 2)
+        half = slice(64 * (a % 2), 64 * (a % 2) + 64)
+        grad_kernel[a, :, :128] = small[8 * a : 8 * a + 7]
+        grad_kernel[a, :, 128:] = small[at : at + 7, half]
     lines = [small[8 * k + 7 : 8 * k + 8] for k in range(hidden // 128 + 2)]
     grad_bias[...] = jnp.concatenate(lines[:-2], axis=1).reshape(hidden)
     grad_gain[...] = jnp.concatenate([lines[-2], lines[-1][:, : channels - 128]], axis=1).reshape(
@@ -703,46 +712,47 @@
         [FAR] + [VMEM] * 5,
     )(core, before, after, masked, gm, mask, *ready[:-1])
 
-    keep, send = call(
+    arrived = swapped(send, "lon", 1)
+    (small,) = call(
         taps_kernel,
         "taps",
-        [((rows + SMALL, 128), BF16)] * 2,
-        [cells, packed, ((8, 2, 8, 128), F32)],
+        [((SMALL, 128), BF16)],
+        [cells, packed, ((12, 8, 128), F32)],
         10,
-        [SMEM] + [VMEM] * 6,
+        [VMEM] * 4,
+        [VMEM],
+    )(masked, d_conv, d_edge, sums)
+    have = (lax.axis_index("dp") & 1).reshape(1)
+    kept, sent = call(
+        functools.partial(fold_kernel, shards=shards),
+        "fold",
+        [((rows // 2, 128), BF16), ((rows // 2 + SMALL, 128), BF16)],
+        [],
+        6,
+        [SMEM] + [VMEM] * 3,
         [VMEM] * 2,
-    )(core, masked, d_conv, d_edge, sums, keep, send)
-    mine = both(keep, swapped(send, "lon", 1))
-    mine, small = mine[:rows].reshape(shards, -1, 128), mine[rows:]
-
-    def spread(d_conv):
-        return call(
-            spread_kernel,
-            "spread",
-            [field],
-            [rolled, tile, cells, packed, held],
-            24,
-            [VMEM] * 5,
-            [None],
-        )(gm, mask, lines, d_conv, d_edge)
-
-    beside = [(spread, d_conv)]
-    made = []
-    for bit in bits_of(shards):
+    )(have, keep, arrived, small)
+
+    sent, d_conv = lax.optimization_barrier((sent, d_conv))
+    arrived = swapped(sent, "dp", 1)
+    (grad_fields,) = call(
+        spread_kernel,
+        "spread",
+        [field],
+        [rolled, tile, cells, packed, held],
+        24,
+        [VMEM] * 5,
+        [None],
+    )(gm, mask, lines, d_conv, d_edge)
+    arrived, grad_fields = lax.optimization_barrier((arrived, grad_fields))
+    mine = both(kept, arrived[: rows // 2]).reshape(shards // 2, -1, 128)
+    small = both(small, arrived[rows // 2 :])
+    for bit in bits_of(shards)[1:]:
         kept, sent = halved(mine, bit)
         count = sent.shape[0]
-        sent = jnp.concatenate([sent, small], axis=0)
-        if beside:
-            work, needs = beside.pop(0)
-            sent, needs = lax.optimization_barrier((sent, needs))
-            arrived = swapped(sent, "dp", bit)
-            (result,) = work(needs)
-            arrived, result = lax.optimization_barrier((arrived, result))
-            made.append(result)
-        else:
-            arrived = swapped(sent, "dp", bit)
-        mine, small = both(kept, arrived[:count].reshape(kept.shape)), both(small, arrived[count:])
-    (grad_fields,) = made
+        arrived = swapped(jnp.concatenate([sent, small], axis=0), "dp", bit)
+        mine = both(kept, arrived[:count].reshape(kept.shape))
+        small = both(small, arrived[count:])
     mine = jnp.concatenate([mine.reshape(-1, 128), small], axis=0)
     for bit in bits_of(tiles)[1:]:
         mine = both(mine, swapped(mine, "lon", bit))

time: 47.5 us -> 46 us (0.968)
  waiting for transfers between devices: 12.4 us -> 11 us
    ppermute x6, waiting for transfers between devices: 12.4 us -> 11 us  [swapped(): return lax.ppermute(x, axis, [(i, i ^ bit) for i in range(peers)])]
    pallas_call x6 -> x7, Pallas kernels: 22.7 us -> 22.5 us  [run(): kernel(*[pltpu.with_memory_space_constraint(x, space) if space in (FAR, V...]
  transfers between devices with their start and end apart: 8 -> 8, of which waited for: 6 -> 5; matrix products, arithmetic and copies ran while one was open for 0% -> 0% of each run, Pallas kernels for 14% -> 23%
where the time goes in v5:
time: 46 us; the launch traced here: 45.8 us
  Pallas kernels  22.5 us (49%)
  starting transfers between devices  11.4 us (25%)
  waiting for transfers between devices  11 us (24%)
  between operations  0.77 us (2%)
    pallas_call x7, Pallas kernels, run(): kernel(*[pltpu.with_memory_space_constraint(x, space) if space in (FAR, V...  22.5 us
    ppermute x6, waiting for transfers between devices, swapped(): return lax.ppermute(x, axis, [(i, i ^ bit) for i in range(peers)])  11 us
    ppermute x6, starting transfers between devices, swapped(): return lax.ppermute(x, axis, [(i, i ^ bit) for i in range(peers)])  8.89 us
    ppermute x1, starting transfers between devices, per_device(): after = lax.ppermute(first, 'lon', [(j, i) for i, j in up])  1.99 us
  transfers between devices with their start and end apart: 8, of which 5 were waited for; matrix products, arithmetic and copies ran while one was open for 0% of the time, Pallas kernels for 23%

profile of v5, /device:TPU:0, one launch (start us, length us, event | category | flops | bytes accessed | tf_op | source)
XLA Modules:
  0.0 45.8 jit_solution(13789302102872954248)
XLA Ops:
  0.6 2.3 %edges.1 = (bf16[384,128]{1,0:T(8,128)(2,1)S(1)}, bf16[384,128]{1,0:T(8,128)(2,1)S(1)}, bf16[16,192,128]{2,1,0:T(8,128)(2,1)S(1)}, bf16[16,192,128]{2,1,0:T(8,128)(2,1)S(1)}, f32[16,128]{1,0:T(8,128)S(1)}) custom-call(bf16[16,192,128]{2,1,0:T(8,128)(2,1)} %bitcast.30, bf16[16,192,128]{2,1,0:T(8,128)(2,1)} %bitcast.31, s32[16,128]{1,0:T(8,128)} %mask.1), custom_call_target="tpu_custom_call" | custom-call | tf_op jit(solution)/shard_map/edges/pallas_call | solution.py:614
  2.9 0.5 %collective-permute-start = (bf16[384,128]{1,0:T(8,128)(2,1)S(1)}, bf16[384,128]{1,0:T(8,128)(2,1)S(1)}, u32[]{:S(2)}, u32[]{:S(2)}) collective-permute-start(bf16[384,128]{1,0:T(8,128)(2,1)S(1)} %get-tuple-element.38), channel_id=1, source_target_pairs={{0,1},{1,2},{2,3},{3,0},{4,5},{5,6},{6,7},{7,4},{8,9},{9,10},{10,1... | collective-permute-start | bytes 294920 | tf_op jit(solution)/shard_map/ppermute | solution.py:655
  3.4 2.0 %collective-permute-start.1 = (bf16[384,128]{1,0:T(8,128)(2,1)S(1)}, bf16[384,128]{1,0:T(8,128)(2,1)S(1)}, u32[]{:S(2)}, u32[]{:S(2)}) collective-permute-start(bf16[384,128]{1,0:T(8,128)(2,1)S(1)} %get-tuple-element.39), channel_id=1, source_target_pairs={{1,0},{2,1},{3,2},{0,3},{5,4},{6,5},{7,6},{4,7},{9,8},{10,9},{11,1... | collective-permute-start | bytes 294920 | tf_op jit(solution)/shard_map/ppermute | solution.py:656
  5.4 3.1 %prepare.1 = (bf16[12,1792,256]{2,1,0:T(8,128)(2,1)S(1)}, bf16[12,128,1792]{2,1,0:T(8,128)(2,1)S(1)}, f32[24,48,128]{2,1,0:T(8,128)S(1)}, bf16[768,256]{1,0:T(8,...) custom-call(bf16[16,192,128]{2,1,0:T(8,128)(2,1)S(1)} %get-tuple-ele, ...), custom_call_target="tpu_custom_call" | custom-call | tf_op jit(solution)/shard_map/prepare/pallas_call | solution.py:614
  8.6 0.0 collective-permute-done.halo_before
  8.6 0.0 collective-permute-done.1.halo_after
  8.6 8.9 %forward.1 = (bf16[16,192,128]{2,1,0:T(8,128)(2,1)}, bf16[16,192,128]{2,1,0:T(8,128)(2,1)S(1)}, bf16[192,128]{1,0:T(8,128)(2,1)S(1)}, bf16[1152,128]{1,0:T(8,128...) custom-call(s32[1]{0:T(128)} %bitcast.core, bf16[384,128]{1,0:T(8,128)(2,1)S(1)} %collective-permute-done.halo_before, ...), custom_call_target="tpu_custom_call" | custom-call | tf_op jit(solution)/shard_map/forward/pallas_call | solution.py:614
  17.5 1.5 %collective-permute-start.2 = (bf16[1152,128]{1,0:T(8,128)(2,1)S(1)}, bf16[1152,128]{1,0:T(8,128)(2,1)S(1)}, u32[]{:S(2)}, u32[]{:S(2)}) collective-permute-start(bf16[1152,128]{1,0:T(8,128)(2,1)S(1)} %get-tuple-element.53), channel_id=1, source_target_pairs={{0,1},{1,0},{2,3},{3,2},{4,5},{5,4},{6,7},{7,6},{8,9},{9,8},{10,11... | collective-permute-start | bytes 884744 | tf_op jit(solution)/shard_map/ppermute | solution.py:571
  19.1 3.8 %taps.1.small = bf16[96,128]{1,0:T(8,128)(2,1)S(1)} custom-call(bf16[16,192,128]{2,1,0:T(8,128)(2,1)S(1)} %get-tuple-element.40.masked, bf16[16,192,128]{2,1,0:T(8,128)(2,1)S(1)} %get-tuple-element.60.d_conv, bf16[192,128]{1,0:T(8,128)(2,1)S(1)} %get-tuple-element.55.d_edge, f32[8,960]{1,0:T(8,128)S(1)} %get-tuple-element.56.sums), custom_call_target="tpu_custom_call" | custom-call | tf_op jit(solution)/shard_map/taps/pallas_call | solution.py:614
  22.8 0.0 collective-permute-done.2.arrived
  22.8 0.1 fold.1
  23.0 1.6 %collective-permute-start.3 = (bf16[672,128]{1,0:T(8,128)(2,1)S(1)}, bf16[672,128]{1,0:T(8,128)(2,1)S(1)}, u32[]{:S(2)}, u32[]{:S(2)}) collective-permute-start(bf16[672,128]{1,0:T(8,128)(2,1)S(1)} %get-tuple-element.58), channel_id=1, source_target_pairs={{0,4},{4,0},{8,12},{12,8},{16,20},{20,16},{24,28},{28,24},{1,5},{5... | collective-permute-start | bytes 516104 | tf_op jit(solution)/shard_map/ppermute | solution.py:571
  24.5 3.5 %spread.1 = bf16[16,192,128]{2,1,0:T(8,128)(2,1)} custom-call(bf16[16,192,128]{2,1,0:T(8,128)(2,1)S(1)} %get-tuple-element.41.gm, f32[16,128]{1,0:T(8,128)S(1)} %get-tuple-element.42.mask, f32[96,256]{1,0:T(8,128)S(1)} %get-tuple-element.59.lines, bf16[16,192,128]{2,1,0:T(8,128)(2,1)S(1)} %get-tuple-element.60.d_conv, ...), custom_call_target="tpu_custom_call" | custom-call | tf_op jit(solution)/shard_map/spread/pallas_call | solution.py:614
  28.1 1.3 %collective-permute-done.3 = bf16[672,128]{1,0:T(8,128)(2,1)S(1)} collective-permute-done((bf16[672,128]{1,0:T(8,128)(2,1)S(1)}, bf16[672,128]{1,0:T(8,128)(2,1)S(1)}, u32[]{:S(2)}, u32[]{:S(2)}) %collective-permute-start.3) | collective-permute-done | bytes 172064 | tf_op jit(solution)/shard_map/ppermute | solution.py:571
  29.4 1.6 %collective-permute-start.4 = (bf16[384,128]{1,0:T(8,128)(2,1)S(1)}, bf16[384,128]{1,0:T(8,128)(2,1)S(1)}, u32[]{:S(2)}, u32[]{:S(2)}) collective-permute-start(bf16[384,128]{1,0:T(8,128)(2,1)S(1)} %pad_maximum_fusion), channel_id=1, source_target_pairs={{0,8},{4,12},{8,0},{12,4},{16,24},{20,28},{24,16},{28,20},{1,9},{5... | collective-permute-start | bytes 294920 | tf_op jit(solution)/shard_map/ppermute | solution.py:571
  31.1 3.0 %collective-permute-done.4 = bf16[384,128]{1,0:T(8,128)(2,1)S(1)} collective-permute-done((bf16[384,128]{1,0:T(8,128)(2,1)S(1)}, bf16[384,128]{1,0:T(8,128)(2,1)S(1)}, u32[]{:S(2)}, u32[]{:S(2)}) %collective-permute-start.4) | collective-permute-done | bytes 98336 | tf_op jit(solution)/shard_map/ppermute | solution.py:571
  34.2 2.7 %collective-permute-start.5 = (bf16[240,128]{1,0:T(8,128)(2,1)S(1)}, bf16[240,128]{1,0:T(8,128)(2,1)S(1)}, u32[]{:S(2)}, u32[]{:S(2)}) collective-permute-start(bf16[240,128]{1,0:T(8,128)(2,1)S(1)} %pad_maximum_fusion.1), channel_id=1, source_target_pairs={{0,16},{4,20},{8,24},{12,28},{16,0},{20,4},{24,8},{28,12},{1,17},{... | collective-permute-start | bytes 184328 | tf_op jit(solution)/shard_map/ppermute | solution.py:571
  36.8 2.5 %collective-permute-done.5 = bf16[240,128]{1,0:T(8,128)(2,1)S(1)} collective-permute-done((bf16[240,128]{1,0:T(8,128)(2,1)S(1)}, bf16[240,128]{1,0:T(8,128)(2,1)S(1)}, u32[]{:S(2)}, u32[]{:S(2)}) %collective-permute-start.5) | collective-permute-done | bytes 61472 | tf_op jit(solution)/shard_map/ppermute | solution.py:571
  39.4 1.4 %collective-permute-start.6 = (bf16[240,128]{1,0:T(8,128)(2,1)S(1)}, bf16[240,128]{1,0:T(8,128)(2,1)S(1)}, u32[]{:S(2)}, u32[]{:S(2)}) collective-permute-start(bf16[240,128]{1,0:T(8,128)(2,1)S(1)} %pad_maximum_fusion.2), channel_id=1, source_target_pairs={{0,2},{1,3},{2,0},{3,1},{4,6},{5,7},{6,4},{7,5},{8,10},{9,11},{10,... | collective-permute-start | bytes 184328 | tf_op jit(solution)/shard_map/ppermute | solution.py:571
  40.8 2.9 %collective-permute-done.6 = bf16[240,128]{1,0:T(8,128)(2,1)S(1)} collective-permute-done((bf16[240,128]{1,0:T(8,128)(2,1)S(1)}, bf16[240,128]{1,0:T(8,128)(2,1)S(1)}, u32[]{:S(2)}, u32[]{:S(2)}) %collective-permute-start.6) | collective-permute-done | bytes 61472 | tf_op jit(solution)/shard_map/ppermute | solution.py:571
  43.8 0.1 collective-permute-start.7
  43.8 1.2 %collective-permute-done.7.other = bf16[240,128]{1,0:T(8,128)(2,1)S(1)} collective-permute-done((bf16[240,128]{1,0:T(8,128)(2,1)S(1)}, bf16[240,128]{1,0:T(8,128)(2,1)S(1)}, u32[]{:S(2)}, u32[]{:S(2)}) %collective-permute-start.7) | collective-permute-done | bytes 61472 | tf_op jit(solution)/shard_map/ppermute | solution.py:571
  45.1 0.7 %final.1 = (f32[24,768]{1,0:T(8,128)}, f32[96,192]{1,0:T(8,128)}, f32[7,7,192]{2,1,0:T(8,128)}, f32[192]{0:T(256)}, f32[768]{0:T(1024)}) custom-call(s32[1]{0:T(128)} %bitcast.core, bf16[240,128]{1,0:T(8,128)(2,1)S(1)} %add_convert_fusion.1.mine, bf16[240,128]{1,0:T(8,128)(2,1)S(1)} %collective-permute-done.7.other), custom_call_target="tpu_custom_call" | custom-call | tf_op jit(solution)/shard_map/final/pallas_call | solution.py:614
  (13 shorter events, 0.2 us)
Async XLA Ops:
  2.9 5.7 %collective-permute-start = (bf16[384,128]{1,0:T(8,128)(2,1)S(1)}, bf16[384,128]{1,0:T(8,128)(2,1)S(1)}, u32[]{:S(2)}, u32[]{:S(2)}) collective-permute-start(bf16[384,128]{1,0:T(8,128)(2,1)S(1)} %get-tuple-element.38), channel_id=1, source_target_pairs={{0,1},{1,2},{2,3},{3,0},{4,5},{5,6},{6,7},{7,4},{8,9},{9,10},{10,1... | collective-permute-start | bytes 294920 | tf_op jit(solution)/shard_map/ppermute | solution.py:655
  3.4 5.2 %collective-permute-start.1 = (bf16[384,128]{1,0:T(8,128)(2,1)S(1)}, bf16[384,128]{1,0:T(8,128)(2,1)S(1)}, u32[]{:S(2)}, u32[]{:S(2)}) collective-permute-start(bf16[384,128]{1,0:T(8,128)(2,1)S(1)} %get-tuple-element.39), channel_id=1, source_target_pairs={{1,0},{2,1},{3,2},{0,3},{5,4},{6,5},{7,6},{4,7},{9,8},{10,9},{11,1... | collective-permute-start | bytes 294920 | tf_op jit(solution)/shard_map/ppermute | solution.py:656
  17.5 5.3 %collective-permute-start.2 = (bf16[1152,128]{1,0:T(8,128)(2,1)S(1)}, bf16[1152,128]{1,0:T(8,128)(2,1)S(1)}, u32[]{:S(2)}, u32[]{:S(2)}) collective-permute-start(bf16[1152,128]{1,0:T(8,128)(2,1)S(1)} %get-tuple-element.53), channel_id=1, source_target_pairs={{0,1},{1,0},{2,3},{3,2},{4,5},{5,4},{6,7},{7,6},{8,9},{9,8},{10,11... | collective-permute-start | bytes 884744 | tf_op jit(solution)/shard_map/ppermute | solution.py:571
  23.0 6.4 %collective-permute-start.3 = (bf16[672,128]{1,0:T(8,128)(2,1)S(1)}, bf16[672,128]{1,0:T(8,128)(2,1)S(1)}, u32[]{:S(2)}, u32[]{:S(2)}) collective-permute-start(bf16[672,128]{1,0:T(8,128)(2,1)S(1)} %get-tuple-element.58), channel_id=1, source_target_pairs={{0,4},{4,0},{8,12},{12,8},{16,20},{20,16},{24,28},{28,24},{1,5},{5... | collective-permute-start | bytes 516104 | tf_op jit(solution)/shard_map/ppermute | solution.py:571
  29.4 4.7 %collective-permute-start.4 = (bf16[384,128]{1,0:T(8,128)(2,1)S(1)}, bf16[384,128]{1,0:T(8,128)(2,1)S(1)}, u32[]{:S(2)}, u32[]{:S(2)}) collective-permute-start(bf16[384,128]{1,0:T(8,128)(2,1)S(1)} %pad_maximum_fusion), channel_id=1, source_target_pairs={{0,8},{4,12},{8,0},{12,4},{16,24},{20,28},{24,16},{28,20},{1,9},{5... | collective-permute-start | bytes 294920 | tf_op jit(solution)/shard_map/ppermute | solution.py:571
  34.2 5.2 %collective-permute-start.5 = (bf16[240,128]{1,0:T(8,128)(2,1)S(1)}, bf16[240,128]{1,0:T(8,128)(2,1)S(1)}, u32[]{:S(2)}, u32[]{:S(2)}) collective-permute-start(bf16[240,128]{1,0:T(8,128)(2,1)S(1)} %pad_maximum_fusion.1), channel_id=1, source_target_pairs={{0,16},{4,20},{8,24},{12,28},{16,0},{20,4},{24,8},{28,12},{1,17},{... | collective-permute-start | bytes 184328 | tf_op jit(solution)/shard_map/ppermute | solution.py:571
  39.4 4.3 %collective-permute-start.6 = (bf16[240,128]{1,0:T(8,128)(2,1)S(1)}, bf16[240,128]{1,0:T(8,128)(2,1)S(1)}, u32[]{:S(2)}, u32[]{:S(2)}) collective-permute-start(bf16[240,128]{1,0:T(8,128)(2,1)S(1)} %pad_maximum_fusion.2), channel_id=1, source_target_pairs={{0,2},{1,3},{2,0},{3,1},{4,6},{5,7},{6,4},{7,5},{8,10},{9,11},{10,... | collective-permute-start | bytes 184328 | tf_op jit(solution)/shard_map/ppermute | solution.py:571
  43.8 1.3 %collective-permute-start.7 = (bf16[240,128]{1,0:T(8,128)(2,1)S(1)}, bf16[240,128]{1,0:T(8,128)(2,1)S(1)}, u32[]{:S(2)}, u32[]{:S(2)}) collective-permute-start(bf16[240,128]{1,0:T(8,128)(2,1)S(1)} %add_convert_fusion.1.mine), channel_id=1, source_target_pairs={{0,1},{1,0},{2,3},{3,2},{4,5},{5,4},{6,7},{7,6},{8,9},{9,8},{10,11... | collective-permute-start | bytes 184328 | tf_op jit(solution)/shard_map/ppermute | solution.py:571

commit v6 on v5

--- a/solution.py
+++ b/solution.py
@@ -169,8 +169,14 @@
             x = [cell[k * EDGE : (k + 1) * EDGE, at] for cell in cells]
             count = groups * EDGE
             out[half * count : (half + 1) * count] = jnp.concatenate(x, axis=0).astype(BF16)
-        g = jnp.concatenate([x[k * EDGE : (k + 1) * EDGE] for x in outer], axis=0)
-        out[2 * groups * EDGE :] = g.T.astype(BF16)
+        g = jnp.concatenate([x[k * EDGE : (k + 1) * EDGE] for x in outer], axis=0).T
+        top, bottom = g[: channels // 2], g[channels // 2 :]
+        near = (iota((1, 128), 1) & (EDGE - 1)) < EDGE // 2
+        if k == 0:
+            g = jnp.where(near, top, pltpu.roll(bottom, EDGE // 2, axis=1))
+        else:
+            g = jnp.where(near, pltpu.roll(bottom, 128 - EDGE // 2, axis=1), top)
+        out[2 * groups * EDGE :] = g.astype(BF16)
 
 
 def prepare_kernel(
@@ -234,9 +240,7 @@
     bias_columns = jnp.where(
         lane == 0, high, jnp.where(lane == 1, middle, jnp.where(lane == 2, low, 0.0))
     )
-    turned_in[...] = jnp.concatenate(
-        [near_in[...].astype(F32).T, bias_columns], axis=1
-    ).astype(BF16)
+    turned_in[...] = jnp.concatenate([near_in[...].T, bias_columns.astype(BF16)], axis=1)
     turned_out[...] = near_out[...].T
 
 
@@ -371,7 +375,14 @@
             y.append(jnp.concatenate(line, axis=1))
         y = jnp.concatenate(y, axis=0).T[:channels]
         at = 2 * groups * EDGE
-        g = jnp.where((lane & (EDGE - 1)) < EDGE // 2, after[at:], before[at:]).astype(BF16)
+        near = (lane & (EDGE - 1)) < EDGE // 2
+        top = jnp.where(near, after[at:], before[at:])
+        bottom = jnp.where(
+            near,
+            pltpu.roll(after[at:], 128 - EDGE // 2, axis=1),
+            pltpu.roll(before[at:], EDGE // 2, axis=1),
+        )
+        g = jnp.concatenate([top, bottom], axis=0).astype(BF16)
         return normalise(y, g, False)
 
     def end(r, state):
@@ -394,7 +405,7 @@
     coming = head(states[0], 0)
     for n, (r, h) in enumerate(steps):
         here = coming
-        if h == 0 and r < blocks:
+        if h == 256 and r < blocks:
             states[r + 1] = start(r + 1) if r + 1 < blocks else start_edges()
         if n + 1 < len(steps):
             coming = head(states[steps[n + 1][0]], steps[n + 1][1])
@@ -633,7 +644,7 @@
     w_out = weight_out.T
 
     field = ((lat, channels, lon), BF16)
-    halo = ((2 * channels, 128), BF16)
+    halo = ((channels + channels // 2, 128), BF16)
     edge = ((channels, 128), BF16)
     rolled = ((16, 8 * groups, 256), F32)
     tile = ((groups, 7 * 256, 256), BF16)

time: 46 us -> 45.8 us (level)
  no operation moved by 1% of the time
where the time goes in v6:
time: 45.8 us; the launch traced here: 45.6 us
  Pallas kernels  22.5 us (49%)
  starting transfers between devices  11.4 us (25%)
  waiting for transfers between devices  10.7 us (23%)
  between operations  0.77 us (2%)
    pallas_call x7, Pallas kernels, run(): kernel(*[pltpu.with_memory_space_constraint(x, space) if space in (FAR, V...  22.5 us
    ppermute x6, waiting for transfers between devices, swapped(): return lax.ppermute(x, axis, [(i, i ^ bit) for i in range(peers)])  10.7 us
    ppermute x6, starting transfers between devices, swapped(): return lax.ppermute(x, axis, [(i, i ^ bit) for i in range(peers)])  8.87 us
    ppermute x1, starting transfers between devices, per_device(): after = lax.ppermute(first, 'lon', [(j, i) for i, j in up])  1.99 us
  transfers between devices with their start and end apart: 8, of which 5 were waited for; matrix products, arithmetic and copies ran while one was open for 0% of the time, Pallas kernels for 23%

profile of v6, /device:TPU:0, one launch (start us, length us, event | category | flops | bytes accessed | tf_op | source)
XLA Modules:
  0.0 45.6 jit_solution(8553031148441645805)
XLA Ops:
  0.6 2.3 %edges.1 = (bf16[288,128]{1,0:T(8,128)(2,1)S(1)}, bf16[288,128]{1,0:T(8,128)(2,1)S(1)}, bf16[16,192,128]{2,1,0:T(8,128)(2,1)S(1)}, bf16[16,192,128]{2,1,0:T(8,128)(2,1)S(1)}, f32[16,128]{1,0:T(8,128)S(1)}) custom-call(bf16[16,192,128]{2,1,0:T(8,128)(2,1)} %bitcast.30, bf16[16,192,128]{2,1,0:T(8,128)(2,1)} %bitcast.31, s32[16,128]{1,0:T(8,128)} %mask.1), custom_call_target="tpu_custom_call" | custom-call | tf_op jit(solution)/shard_map/edges/pallas_call | solution.py:625
  2.9 0.5 %collective-permute-start = (bf16[288,128]{1,0:T(8,128)(2,1)S(1)}, bf16[288,128]{1,0:T(8,128)(2,1)S(1)}, u32[]{:S(2)}, u32[]{:S(2)}) collective-permute-start(bf16[288,128]{1,0:T(8,128)(2,1)S(1)} %get-tuple-element.38), channel_id=1, source_target_pairs={{0,1},{1,2},{2,3},{3,0},{4,5},{5,6},{6,7},{7,4},{8,9},{9,10},{10,1... | collective-permute-start | bytes 221192 | tf_op jit(solution)/shard_map/ppermute | solution.py:666
  3.4 2.0 %collective-permute-start.1 = (bf16[288,128]{1,0:T(8,128)(2,1)S(1)}, bf16[288,128]{1,0:T(8,128)(2,1)S(1)}, u32[]{:S(2)}, u32[]{:S(2)}) collective-permute-start(bf16[288,128]{1,0:T(8,128)(2,1)S(1)} %get-tuple-element.39), channel_id=1, source_target_pairs={{1,0},{2,1},{3,2},{0,3},{5,4},{6,5},{7,6},{4,7},{9,8},{10,9},{11,1... | collective-permute-start | bytes 221192 | tf_op jit(solution)/shard_map/ppermute | solution.py:667
  5.4 3.1 %prepare.1 = (bf16[12,1792,256]{2,1,0:T(8,128)(2,1)S(1)}, bf16[12,128,1792]{2,1,0:T(8,128)(2,1)S(1)}, f32[24,48,128]{2,1,0:T(8,128)S(1)}, bf16[768,256]{1,0:T(8,...) custom-call(bf16[16,192,128]{2,1,0:T(8,128)(2,1)S(1)} %get-tuple-ele, ...), custom_call_target="tpu_custom_call" | custom-call | tf_op jit(solution)/shard_map/prepare/pallas_call | solution.py:625
  8.6 0.0 collective-permute-done.halo_before
  8.6 0.0 collective-permute-done.1.halo_after
  8.6 9.0 %forward.1 = (bf16[16,192,128]{2,1,0:T(8,128)(2,1)}, bf16[16,192,128]{2,1,0:T(8,128)(2,1)S(1)}, bf16[192,128]{1,0:T(8,128)(2,1)S(1)}, bf16[1152,128]{1,0:T(8,128...) custom-call(s32[1]{0:T(128)} %bitcast.core, bf16[288,128]{1,0:T(8,128)(2,1)S(1)} %collective-permute-done.halo_before, ...), custom_call_target="tpu_custom_call" | custom-call | tf_op jit(solution)/shard_map/forward/pallas_call | solution.py:625
  17.6 1.3 %collective-permute-start.2 = (bf16[1152,128]{1,0:T(8,128)(2,1)S(1)}, bf16[1152,128]{1,0:T(8,128)(2,1)S(1)}, u32[]{:S(2)}, u32[]{:S(2)}) collective-permute-start(bf16[1152,128]{1,0:T(8,128)(2,1)S(1)} %get-tuple-element.53), channel_id=1, source_target_pairs={{0,1},{1,0},{2,3},{3,2},{4,5},{5,4},{6,7},{7,6},{8,9},{9,8},{10,11... | collective-permute-start | bytes 884744 | tf_op jit(solution)/shard_map/ppermute | solution.py:582
  18.8 3.8 %taps.1.small = bf16[96,128]{1,0:T(8,128)(2,1)S(1)} custom-call(bf16[16,192,128]{2,1,0:T(8,128)(2,1)S(1)} %get-tuple-element.40.masked, bf16[16,192,128]{2,1,0:T(8,128)(2,1)S(1)} %get-tuple-element.60.d_conv, bf16[192,128]{1,0:T(8,128)(2,1)S(1)} %get-tuple-element.55.d_edge, f32[8,960]{1,0:T(8,128)S(1)} %get-tuple-element.56.sums), custom_call_target="tpu_custom_call" | custom-call | tf_op jit(solution)/shard_map/taps/pallas_call | solution.py:625
  22.6 0.0 collective-permute-done.2.arrived
  22.6 0.1 fold.1
  22.7 1.6 %collective-permute-start.3 = (bf16[672,128]{1,0:T(8,128)(2,1)S(1)}, bf16[672,128]{1,0:T(8,128)(2,1)S(1)}, u32[]{:S(2)}, u32[]{:S(2)}) collective-permute-start(bf16[672,128]{1,0:T(8,128)(2,1)S(1)} %get-tuple-element.58), channel_id=1, source_target_pairs={{0,4},{4,0},{8,12},{12,8},{16,20},{20,16},{24,28},{28,24},{1,5},{5... | collective-permute-start | bytes 516104 | tf_op jit(solution)/shard_map/ppermute | solution.py:582
  24.3 3.5 %spread.1 = bf16[16,192,128]{2,1,0:T(8,128)(2,1)} custom-call(bf16[16,192,128]{2,1,0:T(8,128)(2,1)S(1)} %get-tuple-element.41.gm, f32[16,128]{1,0:T(8,128)S(1)} %get-tuple-element.42.mask, f32[96,256]{1,0:T(8,128)S(1)} %get-tuple-element.59.lines, bf16[16,192,128]{2,1,0:T(8,128)(2,1)S(1)} %get-tuple-element.60.d_conv, ...), custom_call_target="tpu_custom_call" | custom-call | tf_op jit(solution)/shard_map/spread/pallas_call | solution.py:625
  27.8 1.3 %collective-permute-done.3 = bf16[672,128]{1,0:T(8,128)(2,1)S(1)} collective-permute-done((bf16[672,128]{1,0:T(8,128)(2,1)S(1)}, bf16[672,128]{1,0:T(8,128)(2,1)S(1)}, u32[]{:S(2)}, u32[]{:S(2)}) %collective-permute-start.3) | collective-permute-done | bytes 172064 | tf_op jit(solution)/shard_map/ppermute | solution.py:582
  29.2 1.7 %collective-permute-start.4 = (bf16[384,128]{1,0:T(8,128)(2,1)S(1)}, bf16[384,128]{1,0:T(8,128)(2,1)S(1)}, u32[]{:S(2)}, u32[]{:S(2)}) collective-permute-start(bf16[384,128]{1,0:T(8,128)(2,1)S(1)} %pad_maximum_fusion), channel_id=1, source_target_pairs={{0,8},{4,12},{8,0},{12,4},{16,24},{20,28},{24,16},{28,20},{1,9},{5... | collective-permute-start | bytes 294920 | tf_op jit(solution)/shard_map/ppermute | solution.py:582
  30.9 3.0 %collective-permute-done.4 = bf16[384,128]{1,0:T(8,128)(2,1)S(1)} collective-permute-done((bf16[384,128]{1,0:T(8,128)(2,1)S(1)}, bf16[384,128]{1,0:T(8,128)(2,1)S(1)}, u32[]{:S(2)}, u32[]{:S(2)}) %collective-permute-start.4) | collective-permute-done | bytes 98336 | tf_op jit(solution)/shard_map/ppermute | solution.py:582
  34.0 2.7 %collective-permute-start.5 = (bf16[240,128]{1,0:T(8,128)(2,1)S(1)}, bf16[240,128]{1,0:T(8,128)(2,1)S(1)}, u32[]{:S(2)}, u32[]{:S(2)}) collective-permute-start(bf16[240,128]{1,0:T(8,128)(2,1)S(1)} %pad_maximum_fusion.1), channel_id=1, source_target_pairs={{0,16},{4,20},{8,24},{12,28},{16,0},{20,4},{24,8},{28,12},{1,17},{... | collective-permute-start | bytes 184328 | tf_op jit(solution)/shard_map/ppermute | solution.py:582
  36.7 2.5 %collective-permute-done.5 = bf16[240,128]{1,0:T(8,128)(2,1)S(1)} collective-permute-done((bf16[240,128]{1,0:T(8,128)(2,1)S(1)}, bf16[240,128]{1,0:T(8,128)(2,1)S(1)}, u32[]{:S(2)}, u32[]{:S(2)}) %collective-permute-start.5) | collective-permute-done | bytes 61472 | tf_op jit(solution)/shard_map/ppermute | solution.py:582
  39.2 1.6 %collective-permute-start.6 = (bf16[240,128]{1,0:T(8,128)(2,1)S(1)}, bf16[240,128]{1,0:T(8,128)(2,1)S(1)}, u32[]{:S(2)}, u32[]{:S(2)}) collective-permute-start(bf16[240,128]{1,0:T(8,128)(2,1)S(1)} %pad_maximum_fusion.2), channel_id=1, source_target_pairs={{0,2},{1,3},{2,0},{3,1},{4,6},{5,7},{6,4},{7,5},{8,10},{9,11},{10,... | collective-permute-start | bytes 184328 | tf_op jit(solution)/shard_map/ppermute | solution.py:582
  40.8 2.7 %collective-permute-done.6 = bf16[240,128]{1,0:T(8,128)(2,1)S(1)} collective-permute-done((bf16[240,128]{1,0:T(8,128)(2,1)S(1)}, bf16[240,128]{1,0:T(8,128)(2,1)S(1)}, u32[]{:S(2)}, u32[]{:S(2)}) %collective-permute-start.6) | collective-permute-done | bytes 61472 | tf_op jit(solution)/shard_map/ppermute | solution.py:582
  43.5 0.1 collective-permute-start.7
  43.6 1.2 %collective-permute-done.7.other = bf16[240,128]{1,0:T(8,128)(2,1)S(1)} collective-permute-done((bf16[240,128]{1,0:T(8,128)(2,1)S(1)}, bf16[240,128]{1,0:T(8,128)(2,1)S(1)}, u32[]{:S(2)}, u32[]{:S(2)}) %collective-permute-start.7) | collective-permute-done | bytes 61472 | tf_op jit(solution)/shard_map/ppermute | solution.py:582
  44.8 0.7 %final.1 = (f32[24,768]{1,0:T(8,128)}, f32[96,192]{1,0:T(8,128)}, f32[7,7,192]{2,1,0:T(8,128)}, f32[192]{0:T(256)}, f32[768]{0:T(1024)}) custom-call(s32[1]{0:T(128)} %bitcast.core, bf16[240,128]{1,0:T(8,128)(2,1)S(1)} %add_convert_fusion.1.mine, bf16[240,128]{1,0:T(8,128)(2,1)S(1)} %collective-permute-done.7.other), custom_call_target="tpu_custom_call" | custom-call | tf_op jit(solution)/shard_map/final/pallas_call | solution.py:625
  (13 shorter events, 0.2 us)
Async XLA Ops:
  2.9 5.6 %collective-permute-start = (bf16[288,128]{1,0:T(8,128)(2,1)S(1)}, bf16[288,128]{1,0:T(8,128)(2,1)S(1)}, u32[]{:S(2)}, u32[]{:S(2)}) collective-permute-start(bf16[288,128]{1,0:T(8,128)(2,1)S(1)} %get-tuple-element.38), channel_id=1, source_target_pairs={{0,1},{1,2},{2,3},{3,0},{4,5},{5,6},{6,7},{7,4},{8,9},{9,10},{10,1... | collective-permute-start | bytes 221192 | tf_op jit(solution)/shard_map/ppermute | solution.py:666
  3.4 5.2 %collective-permute-start.1 = (bf16[288,128]{1,0:T(8,128)(2,1)S(1)}, bf16[288,128]{1,0:T(8,128)(2,1)S(1)}, u32[]{:S(2)}, u32[]{:S(2)}) collective-permute-start(bf16[288,128]{1,0:T(8,128)(2,1)S(1)} %get-tuple-element.39), channel_id=1, source_target_pairs={{1,0},{2,1},{3,2},{0,3},{5,4},{6,5},{7,6},{4,7},{9,8},{10,9},{11,1... | collective-permute-start | bytes 221192 | tf_op jit(solution)/shard_map/ppermute | solution.py:667
  17.6 5.1 %collective-permute-start.2 = (bf16[1152,128]{1,0:T(8,128)(2,1)S(1)}, bf16[1152,128]{1,0:T(8,128)(2,1)S(1)}, u32[]{:S(2)}, u32[]{:S(2)}) collective-permute-start(bf16[1152,128]{1,0:T(8,128)(2,1)S(1)} %get-tuple-element.53), channel_id=1, source_target_pairs={{0,1},{1,0},{2,3},{3,2},{4,5},{5,4},{6,7},{7,6},{8,9},{9,8},{10,11... | collective-permute-start | bytes 884744 | tf_op jit(solution)/shard_map/ppermute | solution.py:582
  22.7 6.4 %collective-permute-start.3 = (bf16[672,128]{1,0:T(8,128)(2,1)S(1)}, bf16[672,128]{1,0:T(8,128)(2,1)S(1)}, u32[]{:S(2)}, u32[]{:S(2)}) collective-permute-start(bf16[672,128]{1,0:T(8,128)(2,1)S(1)} %get-tuple-element.58), channel_id=1, source_target_pairs={{0,4},{4,0},{8,12},{12,8},{16,20},{20,16},{24,28},{28,24},{1,5},{5... | collective-permute-start | bytes 516104 | tf_op jit(solution)/shard_map/ppermute | solution.py:582
  29.2 4.7 %collective-permute-start.4 = (bf16[384,128]{1,0:T(8,128)(2,1)S(1)}, bf16[384,128]{1,0:T(8,128)(2,1)S(1)}, u32[]{:S(2)}, u32[]{:S(2)}) collective-permute-start(bf16[384,128]{1,0:T(8,128)(2,1)S(1)} %pad_maximum_fusion), channel_id=1, source_target_pairs={{0,8},{4,12},{8,0},{12,4},{16,24},{20,28},{24,16},{28,20},{1,9},{5... | collective-permute-start | bytes 294920 | tf_op jit(solution)/shard_map/ppermute | solution.py:582
  34.0 5.2 %collective-permute-start.5 = (bf16[240,128]{1,0:T(8,128)(2,1)S(1)}, bf16[240,128]{1,0:T(8,128)(2,1)S(1)}, u32[]{:S(2)}, u32[]{:S(2)}) collective-permute-start(bf16[240,128]{1,0:T(8,128)(2,1)S(1)} %pad_maximum_fusion.1), channel_id=1, source_target_pairs={{0,16},{4,20},{8,24},{12,28},{16,0},{20,4},{24,8},{28,12},{1,17},{... | collective-permute-start | bytes 184328 | tf_op jit(solution)/shard_map/ppermute | solution.py:582
  39.2 4.3 %collective-permute-start.6 = (bf16[240,128]{1,0:T(8,128)(2,1)S(1)}, bf16[240,128]{1,0:T(8,128)(2,1)S(1)}, u32[]{:S(2)}, u32[]{:S(2)}) collective-permute-start(bf16[240,128]{1,0:T(8,128)(2,1)S(1)} %pad_maximum_fusion.2), channel_id=1, source_target_pairs={{0,2},{1,3},{2,0},{3,1},{4,6},{5,7},{6,4},{7,5},{8,10},{9,11},{10,... | collective-permute-start | bytes 184328 | tf_op jit(solution)/shard_map/ppermute | solution.py:582
  43.5 1.3 %collective-permute-start.7 = (bf16[240,128]{1,0:T(8,128)(2,1)S(1)}, bf16[240,128]{1,0:T(8,128)(2,1)S(1)}, u32[]{:S(2)}, u32[]{:S(2)}) collective-permute-start(bf16[240,128]{1,0:T(8,128)(2,1)S(1)} %add_convert_fusion.1.mine), channel_id=1, source_target_pairs={{0,1},{1,0},{2,3},{3,2},{4,5},{5,4},{6,7},{7,6},{8,9},{9,8},{10,11... | collective-permute-start | bytes 184328 | tf_op jit(solution)/shard_map/ppermute | solution.py:582

commit v7 on v6

--- a/solution.py
+++ b/solution.py
@@ -137,9 +137,9 @@
 ):
     lat, channels, lon = fields.shape
     groups = channels // GROUP
-    count = lat // 4
+    count = lat // 2
     copies = [pltpu.make_async_copy(mask, held_mask, arrived.at[0])]
-    for r in range(4):
+    for r in range(2):
         at = slice(count * r, count * (r + 1))
         for k, (far, held) in enumerate(((fields, held_x), (cotangent, held_g))):
             copies.append(
@@ -153,7 +153,7 @@
     copies[0].wait()
     near_mask[...] = held_mask[...].astype(F32)
     rows, outer = [], []
-    for r in range(4):
+    for r in range(2):
         copies[1 + 2 * r].wait()
         copies[2 + 2 * r].wait()
         for i in range(count * r, count * (r + 1)):

time: 45.8 us -> 45.6 us (level)
  no operation moved by 1% of the time
where the time goes in v7:
time: 45.6 us; the launch traced here: 45.4 us
  Pallas kernels  22.4 us (49%)
  starting transfers between devices  11.4 us (25%)
  waiting for transfers between devices  10.7 us (23%)
  between operations  0.77 us (2%)
    pallas_call x7, Pallas kernels, run(): kernel(*[pltpu.with_memory_space_constraint(x, space) if space in (FAR, V...  22.4 us
    ppermute x6, waiting for transfers between devices, swapped(): return lax.ppermute(x, axis, [(i, i ^ bit) for i in range(peers)])  10.7 us
    ppermute x6, starting transfers between devices, swapped(): return lax.ppermute(x, axis, [(i, i ^ bit) for i in range(peers)])  8.89 us
    ppermute x1, starting transfers between devices, per_device(): after = lax.ppermute(first, 'lon', [(j, i) for i, j in up])  1.99 us
  transfers between devices with their start and end apart: 8, of which 5 were waited for; matrix products, arithmetic and copies ran while one was open for 0% of the time, Pallas kernels for 23%

profile of v7, /device:TPU:0, one launch (start us, length us, event | category | flops | bytes accessed | tf_op | source)
XLA Modules:
  0.0 45.4 jit_solution(10508866292511584739)
XLA Ops:
  0.6 2.1 %edges.1 = (bf16[288,128]{1,0:T(8,128)(2,1)S(1)}, bf16[288,128]{1,0:T(8,128)(2,1)S(1)}, bf16[16,192,128]{2,1,0:T(8,128)(2,1)S(1)}, bf16[16,192,128]{2,1,0:T(8,128)(2,1)S(1)}, f32[16,128]{1,0:T(8,128)S(1)}) custom-call(bf16[16,192,128]{2,1,0:T(8,128)(2,1)} %bitcast.30, bf16[16,192,128]{2,1,0:T(8,128)(2,1)} %bitcast.31, s32[16,128]{1,0:T(8,128)} %mask.1), custom_call_target="tpu_custom_call" | custom-call | tf_op jit(solution)/shard_map/edges/pallas_call | solution.py:625
  2.7 0.5 %collective-permute-start = (bf16[288,128]{1,0:T(8,128)(2,1)S(1)}, bf16[288,128]{1,0:T(8,128)(2,1)S(1)}, u32[]{:S(2)}, u32[]{:S(2)}) collective-permute-start(bf16[288,128]{1,0:T(8,128)(2,1)S(1)} %get-tuple-element.38), channel_id=1, source_target_pairs={{0,1},{1,2},{2,3},{3,0},{4,5},{5,6},{6,7},{7,4},{8,9},{9,10},{10,1... | collective-permute-start | bytes 221192 | tf_op jit(solution)/shard_map/ppermute | solution.py:666
  3.2 2.0 %collective-permute-start.1 = (bf16[288,128]{1,0:T(8,128)(2,1)S(1)}, bf16[288,128]{1,0:T(8,128)(2,1)S(1)}, u32[]{:S(2)}, u32[]{:S(2)}) collective-permute-start(bf16[288,128]{1,0:T(8,128)(2,1)S(1)} %get-tuple-element.39), channel_id=1, source_target_pairs={{1,0},{2,1},{3,2},{0,3},{5,4},{6,5},{7,6},{4,7},{9,8},{10,9},{11,1... | collective-permute-start | bytes 221192 | tf_op jit(solution)/shard_map/ppermute | solution.py:667
  5.2 3.1 %prepare.1 = (bf16[12,1792,256]{2,1,0:T(8,128)(2,1)S(1)}, bf16[12,128,1792]{2,1,0:T(8,128)(2,1)S(1)}, f32[24,48,128]{2,1,0:T(8,128)S(1)}, bf16[768,256]{1,0:T(8,...) custom-call(bf16[16,192,128]{2,1,0:T(8,128)(2,1)S(1)} %get-tuple-ele, ...), custom_call_target="tpu_custom_call" | custom-call | tf_op jit(solution)/shard_map/prepare/pallas_call | solution.py:625
  8.4 0.0 collective-permute-done.halo_before
  8.4 0.0 collective-permute-done.1.halo_after
  8.4 9.0 %forward.1 = (bf16[16,192,128]{2,1,0:T(8,128)(2,1)}, bf16[16,192,128]{2,1,0:T(8,128)(2,1)S(1)}, bf16[192,128]{1,0:T(8,128)(2,1)S(1)}, bf16[1152,128]{1,0:T(8,128...) custom-call(s32[1]{0:T(128)} %bitcast.core, bf16[288,128]{1,0:T(8,128)(2,1)S(1)} %collective-permute-done.halo_before, ...), custom_call_target="tpu_custom_call" | custom-call | tf_op jit(solution)/shard_map/forward/pallas_call | solution.py:625
  17.4 1.3 %collective-permute-start.2 = (bf16[1152,128]{1,0:T(8,128)(2,1)S(1)}, bf16[1152,128]{1,0:T(8,128)(2,1)S(1)}, u32[]{:S(2)}, u32[]{:S(2)}) collective-permute-start(bf16[1152,128]{1,0:T(8,128)(2,1)S(1)} %get-tuple-element.53), channel_id=1, source_target_pairs={{0,1},{1,0},{2,3},{3,2},{4,5},{5,4},{6,7},{7,6},{8,9},{9,8},{10,11... | collective-permute-start | bytes 884744 | tf_op jit(solution)/shard_map/ppermute | solution.py:582
  18.6 3.8 %taps.1.small = bf16[96,128]{1,0:T(8,128)(2,1)S(1)} custom-call(bf16[16,192,128]{2,1,0:T(8,128)(2,1)S(1)} %get-tuple-element.40.masked, bf16[16,192,128]{2,1,0:T(8,128)(2,1)S(1)} %get-tuple-element.60.d_conv, bf16[192,128]{1,0:T(8,128)(2,1)S(1)} %get-tuple-element.55.d_edge, f32[8,960]{1,0:T(8,128)S(1)} %get-tuple-element.56.sums), custom_call_target="tpu_custom_call" | custom-call | tf_op jit(solution)/shard_map/taps/pallas_call | solution.py:625
  22.4 0.0 collective-permute-done.2.arrived
  22.4 0.1 fold.1
  22.5 1.6 %collective-permute-start.3 = (bf16[672,128]{1,0:T(8,128)(2,1)S(1)}, bf16[672,128]{1,0:T(8,128)(2,1)S(1)}, u32[]{:S(2)}, u32[]{:S(2)}) collective-permute-start(bf16[672,128]{1,0:T(8,128)(2,1)S(1)} %get-tuple-element.58), channel_id=1, source_target_pairs={{0,4},{4,0},{8,12},{12,8},{16,20},{20,16},{24,28},{28,24},{1,5},{5... | collective-permute-start | bytes 516104 | tf_op jit(solution)/shard_map/ppermute | solution.py:582
  24.1 3.5 %spread.1 = bf16[16,192,128]{2,1,0:T(8,128)(2,1)} custom-call(bf16[16,192,128]{2,1,0:T(8,128)(2,1)S(1)} %get-tuple-element.41.gm, f32[16,128]{1,0:T(8,128)S(1)} %get-tuple-element.42.mask, f32[96,256]{1,0:T(8,128)S(1)} %get-tuple-element.59.lines, bf16[16,192,128]{2,1,0:T(8,128)(2,1)S(1)} %get-tuple-element.60.d_conv, ...), custom_call_target="tpu_custom_call" | custom-call | tf_op jit(solution)/shard_map/spread/pallas_call | solution.py:625
  27.7 1.2 %collective-permute-done.3 = bf16[672,128]{1,0:T(8,128)(2,1)S(1)} collective-permute-done((bf16[672,128]{1,0:T(8,128)(2,1)S(1)}, bf16[672,128]{1,0:T(8,128)(2,1)S(1)}, u32[]{:S(2)}, u32[]{:S(2)}) %collective-permute-start.3) | collective-permute-done | bytes 172064 | tf_op jit(solution)/shard_map/ppermute | solution.py:582
  29.0 1.7 %collective-permute-start.4 = (bf16[384,128]{1,0:T(8,128)(2,1)S(1)}, bf16[384,128]{1,0:T(8,128)(2,1)S(1)}, u32[]{:S(2)}, u32[]{:S(2)}) collective-permute-start(bf16[384,128]{1,0:T(8,128)(2,1)S(1)} %pad_maximum_fusion), channel_id=1, source_target_pairs={{0,8},{4,12},{8,0},{12,4},{16,24},{20,28},{24,16},{28,20},{1,9},{5... | collective-permute-start | bytes 294920 | tf_op jit(solution)/shard_map/ppermute | solution.py:582
  30.7 3.0 %collective-permute-done.4 = bf16[384,128]{1,0:T(8,128)(2,1)S(1)} collective-permute-done((bf16[384,128]{1,0:T(8,128)(2,1)S(1)}, bf16[384,128]{1,0:T(8,128)(2,1)S(1)}, u32[]{:S(2)}, u32[]{:S(2)}) %collective-permute-start.4) | collective-permute-done | bytes 98336 | tf_op jit(solution)/shard_map/ppermute | solution.py:582
  33.8 2.7 %collective-permute-start.5 = (bf16[240,128]{1,0:T(8,128)(2,1)S(1)}, bf16[240,128]{1,0:T(8,128)(2,1)S(1)}, u32[]{:S(2)}, u32[]{:S(2)}) collective-permute-start(bf16[240,128]{1,0:T(8,128)(2,1)S(1)} %pad_maximum_fusion.1), channel_id=1, source_target_pairs={{0,16},{4,20},{8,24},{12,28},{16,0},{20,4},{24,8},{28,12},{1,17},{... | collective-permute-start | bytes 184328 | tf_op jit(solution)/shard_map/ppermute | solution.py:582
  36.5 2.5 %collective-permute-done.5 = bf16[240,128]{1,0:T(8,128)(2,1)S(1)} collective-permute-done((bf16[240,128]{1,0:T(8,128)(2,1)S(1)}, bf16[240,128]{1,0:T(8,128)(2,1)S(1)}, u32[]{:S(2)}, u32[]{:S(2)}) %collective-permute-start.5) | collective-permute-done | bytes 61472 | tf_op jit(solution)/shard_map/ppermute | solution.py:582
  39.0 1.6 %collective-permute-start.6 = (bf16[240,128]{1,0:T(8,128)(2,1)S(1)}, bf16[240,128]{1,0:T(8,128)(2,1)S(1)}, u32[]{:S(2)}, u32[]{:S(2)}) collective-permute-start(bf16[240,128]{1,0:T(8,128)(2,1)S(1)} %pad_maximum_fusion.2), channel_id=1, source_target_pairs={{0,2},{1,3},{2,0},{3,1},{4,6},{5,7},{6,4},{7,5},{8,10},{9,11},{10,... | collective-permute-start | bytes 184328 | tf_op jit(solution)/shard_map/ppermute | solution.py:582
  40.6 2.7 %collective-permute-done.6 = bf16[240,128]{1,0:T(8,128)(2,1)S(1)} collective-permute-done((bf16[240,128]{1,0:T(8,128)(2,1)S(1)}, bf16[240,128]{1,0:T(8,128)(2,1)S(1)}, u32[]{:S(2)}, u32[]{:S(2)}) %collective-permute-start.6) | collective-permute-done | bytes 61472 | tf_op jit(solution)/shard_map/ppermute | solution.py:582
  43.3 0.1 collective-permute-start.7
  43.4 1.2 %collective-permute-done.7.other = bf16[240,128]{1,0:T(8,128)(2,1)S(1)} collective-permute-done((bf16[240,128]{1,0:T(8,128)(2,1)S(1)}, bf16[240,128]{1,0:T(8,128)(2,1)S(1)}, u32[]{:S(2)}, u32[]{:S(2)}) %collective-permute-start.7) | collective-permute-done | bytes 61472 | tf_op jit(solution)/shard_map/ppermute | solution.py:582
  44.7 0.7 %final.1 = (f32[24,768]{1,0:T(8,128)}, f32[96,192]{1,0:T(8,128)}, f32[7,7,192]{2,1,0:T(8,128)}, f32[192]{0:T(256)}, f32[768]{0:T(1024)}) custom-call(s32[1]{0:T(128)} %bitcast.core, bf16[240,128]{1,0:T(8,128)(2,1)S(1)} %add_convert_fusion.1.mine, bf16[240,128]{1,0:T(8,128)(2,1)S(1)} %collective-permute-done.7.other), custom_call_target="tpu_custom_call" | custom-call | tf_op jit(solution)/shard_map/final/pallas_call | solution.py:625
  (13 shorter events, 0.2 us)
Async XLA Ops:
  2.7 5.6 %collective-permute-start = (bf16[288,128]{1,0:T(8,128)(2,1)S(1)}, bf16[288,128]{1,0:T(8,128)(2,1)S(1)}, u32[]{:S(2)}, u32[]{:S(2)}) collective-permute-start(bf16[288,128]{1,0:T(8,128)(2,1)S(1)} %get-tuple-element.38), channel_id=1, source_target_pairs={{0,1},{1,2},{2,3},{3,0},{4,5},{5,6},{6,7},{7,4},{8,9},{9,10},{10,1... | collective-permute-start | bytes 221192 | tf_op jit(solution)/shard_map/ppermute | solution.py:666
  3.2 5.2 %collective-permute-start.1 = (bf16[288,128]{1,0:T(8,128)(2,1)S(1)}, bf16[288,128]{1,0:T(8,128)(2,1)S(1)}, u32[]{:S(2)}, u32[]{:S(2)}) collective-permute-start(bf16[288,128]{1,0:T(8,128)(2,1)S(1)} %get-tuple-element.39), channel_id=1, source_target_pairs={{1,0},{2,1},{3,2},{0,3},{5,4},{6,5},{7,6},{4,7},{9,8},{10,9},{11,1... | collective-permute-start | bytes 221192 | tf_op jit(solution)/shard_map/ppermute | solution.py:667
  17.4 5.1 %collective-permute-start.2 = (bf16[1152,128]{1,0:T(8,128)(2,1)S(1)}, bf16[1152,128]{1,0:T(8,128)(2,1)S(1)}, u32[]{:S(2)}, u32[]{:S(2)}) collective-permute-start(bf16[1152,128]{1,0:T(8,128)(2,1)S(1)} %get-tuple-element.53), channel_id=1, source_target_pairs={{0,1},{1,0},{2,3},{3,2},{4,5},{5,4},{6,7},{7,6},{8,9},{9,8},{10,11... | collective-permute-start | bytes 884744 | tf_op jit(solution)/shard_map/ppermute | solution.py:582
  22.5 6.4 %collective-permute-start.3 = (bf16[672,128]{1,0:T(8,128)(2,1)S(1)}, bf16[672,128]{1,0:T(8,128)(2,1)S(1)}, u32[]{:S(2)}, u32[]{:S(2)}) collective-permute-start(bf16[672,128]{1,0:T(8,128)(2,1)S(1)} %get-tuple-element.58), channel_id=1, source_target_pairs={{0,4},{4,0},{8,12},{12,8},{16,20},{20,16},{24,28},{28,24},{1,5},{5... | collective-permute-start | bytes 516104 | tf_op jit(solution)/shard_map/ppermute | solution.py:582
  29.0 4.7 %collective-permute-start.4 = (bf16[384,128]{1,0:T(8,128)(2,1)S(1)}, bf16[384,128]{1,0:T(8,128)(2,1)S(1)}, u32[]{:S(2)}, u32[]{:S(2)}) collective-permute-start(bf16[384,128]{1,0:T(8,128)(2,1)S(1)} %pad_maximum_fusion), channel_id=1, source_target_pairs={{0,8},{4,12},{8,0},{12,4},{16,24},{20,28},{24,16},{28,20},{1,9},{5... | collective-permute-start | bytes 294920 | tf_op jit(solution)/shard_map/ppermute | solution.py:582
  33.8 5.2 %collective-permute-start.5 = (bf16[240,128]{1,0:T(8,128)(2,1)S(1)}, bf16[240,128]{1,0:T(8,128)(2,1)S(1)}, u32[]{:S(2)}, u32[]{:S(2)}) collective-permute-start(bf16[240,128]{1,0:T(8,128)(2,1)S(1)} %pad_maximum_fusion.1), channel_id=1, source_target_pairs={{0,16},{4,20},{8,24},{12,28},{16,0},{20,4},{24,8},{28,12},{1,17},{... | collective-permute-start | bytes 184328 | tf_op jit(solution)/shard_map/ppermute | solution.py:582
  39.0 4.3 %collective-permute-start.6 = (bf16[240,128]{1,0:T(8,128)(2,1)S(1)}, bf16[240,128]{1,0:T(8,128)(2,1)S(1)}, u32[]{:S(2)}, u32[]{:S(2)}) collective-permute-start(bf16[240,128]{1,0:T(8,128)(2,1)S(1)} %pad_maximum_fusion.2), channel_id=1, source_target_pairs={{0,2},{1,3},{2,0},{3,1},{4,6},{5,7},{6,4},{7,5},{8,10},{9,11},{10,... | collective-permute-start | bytes 184328 | tf_op jit(solution)/shard_map/ppermute | solution.py:582
  43.3 1.3 %collective-permute-start.7 = (bf16[240,128]{1,0:T(8,128)(2,1)S(1)}, bf16[240,128]{1,0:T(8,128)(2,1)S(1)}, u32[]{:S(2)}, u32[]{:S(2)}) collective-permute-start(bf16[240,128]{1,0:T(8,128)(2,1)S(1)} %add_convert_fusion.1.mine), channel_id=1, source_target_pairs={{0,1},{1,0},{2,3},{3,2},{4,5},{5,4},{6,7},{7,6},{8,9},{9,8},{10,11... | collective-permute-start | bytes 184328 | tf_op jit(solution)/shard_map/ppermute | solution.py:582
